TPU v7x, 512 devices: a whole 4x8x8 slice. The times are simulated.
512 devices in a mesh: tm: 32 (over y_hi, z, core), rows: 16 (over x, y_lo).
Axes of the slice: x: 4, y: 8 (y_hi: 2, y_lo: 4; y = y_hi * 4 + y_lo), z: 8, core: 2. Of those that a mesh axis runs over, the one named last changes fastest.
Arguments:
- col_feat: bfloat16 [32, 256, 256], P('tm', 'rows'), may hold values from -6 to 6
- w_depth: bfloat16 [256, 128], replicated, may hold values from -0.375 to 0.375
- w_ctx: bfloat16 [256, 80], replicated, may hold values from -0.375 to 0.375
- col_table: int32 [128, 128], P('rows'), may hold values from 0 to 255
- w_bev: bfloat16 [3, 3, 80, 80], replicated, may hold values from -0.21875 to 0.21875
- offsets: int32 [32, 16, 2], P('tm'), may hold values from -4 to 4, as said below
- w_join: bfloat16 [3, 3, 1360, 160], replicated, may hold values from -0.0546875 to 0.0546875
- w_out: bfloat16 [3, 3, 160, 160], replicated, may hold values from -0.15625 to 0.15625
Outputs:
- joined: bfloat16 [32, 128, 160, 128], P('tm', 'rows')
Inputs may be any that keep to these rules, and one draw needn't show every extreme that they name: Where f - k >= 0, offsets[f, k - 1, :] is the ego path's displacement from frame f to frame f - k: the sum of k per-frame steps of -1, 0 or 1 in each coordinate, clipped to the range.
All inputs are finite; a program needn't handle non-finite values.
Results may differ from a plain program's by a relative error of at most 0.0065.
Values may be sent and summed in bfloat16 or wider, within the bound.
No kernel may reach another device: no remote copies, remote signals or barrier semaphores. Data moves between devices by JAX's collectives and lax.ppermute only.
A program may use at most 128 MiB of HBM per device.

v0:
```python
import jax
import jax.numpy as jnp
from jax import lax
from jax.sharding import PartitionSpec as P


def extended(block, sides, width):
    for axis, dim in sides:
        count = lax.axis_size(axis)
        forward = [(i, i + 1) for i in range(count - 1)]
        backward = [(target, source) for source, target in forward]
        low = lax.ppermute(
            lax.slice_in_dim(block, block.shape[dim] - width, None, axis=dim), axis, forward
        )
        high = lax.ppermute(lax.slice_in_dim(block, 0, width, axis=dim), axis, backward)
        block = jnp.concatenate([low, block, high], axis=dim)
    return block


def conv_local(field, weight, rows):
    cols = field.shape[2]
    wide = jnp.pad(field, ((0, 0), (0, 0), (1, 1)))
    total = jnp.zeros((rows, weight.shape[3], cols), jnp.float32)
    for a in range(3):
        for b in range(3):
            total = total + jnp.einsum(
                "rcw,co->row",
                wide[a : a + rows, :, b : b + cols],
                weight[a, b],
                preferred_element_type=jnp.float32,
            )
    return total


def collect(slab, count):
    every = lax.all_gather(slab[None], "tm", axis=0, tiled=True)
    leading = jnp.zeros((count - 1,) + slab.shape, slab.dtype)
    padded = jnp.concatenate([leading, every], axis=0)
    return lax.dynamic_slice_in_dim(padded, lax.axis_index("tm"), count, 0)[::-1]


def shards(col_feat, w_depth, w_ctx, col_table, w_bev, offsets, w_join, w_out):
    rows = col_table.shape[0]
    cols = col_table.shape[1]
    count = offsets.shape[1] + 1
    chans = w_ctx.shape[1]
    depth = jax.nn.sigmoid(
        jnp.einsum("fnk,kd->fnd", col_feat, w_depth, preferred_element_type=jnp.float32)
    )
    ctx = jnp.einsum("fnk,kc->fnc", col_feat, w_ctx, preferred_element_type=jnp.float32)
    local_ray = (depth[:, :, :, None] * ctx[:, :, None, :]).astype(jnp.bfloat16)
    ray = lax.all_to_all(local_ray, "rows", split_axis=2, concat_axis=1, tiled=True)
    columns = ray.shape[1]
    onehot = (col_table[:, :, None] == jnp.arange(columns, dtype=jnp.int32)[None, None, :]).astype(
        jnp.bfloat16
    )
    lifted = jnp.einsum("rwn,nrc->rcw", onehot, ray[0], preferred_element_type=jnp.float32).astype(
        jnp.bfloat16
    )
    rimmed = extended(lifted, (("rows", 0),), 1)
    bev = jax.nn.silu(conv_local(rimmed, w_bev, rows)).astype(jnp.bfloat16)
    window = extended(collect(bev, count), (("rows", 1),), 5)
    zero_moves = jnp.zeros((1, 2), jnp.int32)
    moves_all = jnp.concatenate([zero_moves, offsets[0]], axis=0)
    shifted = jnp.pad(window, ((0, 0), (0, 0), (0, 0), (4, 4)))
    anchor = jnp.zeros((), jnp.int32)

    def warp(slab_one, move):
        return lax.dynamic_slice(
            slab_one, (4 + move[0], anchor, 4 + move[1]), (rows + 2, chans, cols)
        )

    warped = jax.vmap(warp)(shifted, moves_all)
    wide = jnp.pad(warped, ((0, 0), (0, 0), (0, 0), (1, 1)))
    w_win = w_join.reshape(3, 3, count, chans, w_join.shape[3])
    total = jnp.zeros((rows, w_join.shape[3], cols), jnp.float32)
    for a in range(3):
        for b in range(3):
            total = total + jnp.einsum(
                "krcw,kco->row",
                wide[:, a : a + rows, :, b : b + cols],
                w_win[a, b],
                preferred_element_type=jnp.float32,
            )
    hidden = jax.nn.silu(total).astype(jnp.bfloat16)
    hidden_rimmed = extended(hidden, (("rows", 0),), 1)
    joined = conv_local(hidden_rimmed, w_out, rows).astype(jnp.bfloat16)
    return joined[None]


def solution(mesh):
    in_specs = (
        P("tm", "rows", None),
        P(),
        P(),
        P("rows", None),
        P(),
        P("tm", None, None),
        P(),
        P(),
    )
    out_specs = P("tm", "rows", None, None)
    return jax.shard_map(shards, mesh=mesh, in_specs=in_specs, out_specs=out_specs, check_vma=False)
```

profile of v0, /device:TPU:1, one launch (start us, length us, event | category | flops | bytes accessed | tf_op | source)
XLA Modules:
  0.0 364.6 jit_solution(15749338432552457876)
XLA Ops:
  9.6 23.5 %all_to_all.15 = bf16[1,16,128,80]{3,1,0,2:T(8,128)(2,1)S(1)} all-to-all(bf16[1,16,128,80]{3,1,0,2:T(8,128)(2,1)S(1)} %multiply_convert_fusion), channel_id=1, replica_groups=mesh['tm'=32,'rows'=16] {'rows'}, dimensions={2} | all-to-all | bytes 655360 | tf_op jit(solution)/shard_map/all_to_all | solution.py:52
  36.5 3.2 collective-permute-done.1
  42.8 117.1 %all-gather.3.cloned.1.call-done = bf16[256,80,128]{2,1,0:T(8,128)(2,1)} async-done(((bf16[8,80,128]{2,1,0:T(8,128)(2,1)}), bf16[256,80,128]{2,1,0:T(8,128)(2,1)}) %all-gather.3.cloned.1.call-update) | async-done | bytes 5242896 | tf_op jit(solution)/shard_map/all_gather | solution.py:36
  163.0 8.2 %collective-permute-start.2 = (bf16[17,5,80,128]{3,2,1,0:T(8,128)(2,1)}, bf16[17,5,80,128]{3,2,1,0:T(8,128)(2,1)}, u32[]{:S(2)}, u32[]{:S(2)}) collective-permute-start(bf16[17,5,80,128]{3,2,1,0:T(8,128)(2,1)} %slice.221), channel_id=1, source_target_pairs={{0,1},{1,2},{2,3},{3,4},{4,5},{5,6},{6,7},{7,8},{8,9},{9,10},{10,1... | collective-permute-start | bytes 5222408 | tf_op jit(solution)/shard_map/ppermute | solution.py:12
  174.0 8.4 %copy.79 = bf16[3,3,1360,160]{3,2,1,0:T(8,128)(2,1)} copy(bf16[3,3,1360,160]{2,3,1,0:T(8,128)(2,1)} %param.14) | data formatting | bytes 7833600 | tf_op args[6]
  182.5 3.2 pad_dynamic-slice_fusion.2
  185.7 2.3 rev.3
  188.0 19.5 %collective-permute-done.2 = bf16[17,5,80,128]{3,2,1,0:T(8,128)(2,1)} collective-permute-done((bf16[17,5,80,128]{3,2,1,0:T(8,128)(2,1)}, bf16[17,5,80,128]{3,2,1,0:T(8,128)(2,1)}, u32[]{:S(2)}, u32[]{:S(2)}) %collective-permute-start.2) | collective-permute-done | bytes 1740832 | tf_op jit(solution)/shard_map/ppermute | solution.py:12
  207.5 37.5 %collective-permute-done.3 = bf16[17,5,80,128]{3,2,1,0:T(8,128)(2,1)} collective-permute-done((bf16[17,5,80,128]{3,2,1,0:T(8,128)(2,1)}, bf16[17,5,80,128]{3,2,1,0:T(8,128)(2,1)}, u32[]{:S(2)}, u32[]{:S(2)}) %collective-permute-start.3) | collective-permute-done | bytes 1740832 | tf_op jit(solution)/shard_map/ppermute | solution.py:15
  245.0 15.7 %fusion.5 = bf16[17,18,80,136]{3,2,1,0:T(8,128)(2,1)} fusion(bf16[17,5,80,128]{3,2,1,0:T(8,128)(2,1)} %collective-permute-done.3, bf16[17,8,80,128]{3,2,1,0:T(8,128)(2,1)S(1)} %rev.3, bf16[17,5,80,128]{3,2,1,0:T(8,128)(2,1)} %collective-permute-done.2), kind=kLoop, calls=%fused_computation.9 | loop fusion | flops 39951360 | bytes 12925440 | tf_op jit(solution)/shard_map/concatenate | solution.py:16
  260.7 73.0 %while.1 = (s32[]{:T(128)}, bf16[17,18,80,136]{3,2,1,0:T(8,128)(2,1)}, s32[17,4]{0,1:T(4,128)S(1)}, bf16[17,10,80,128]{3,2,0,1:T(8,128)(2,1)}, s32[]{:T(128)}) while((s32[]{:T(128)}, bf16[17,18,80,136]{3,2,1,0:T(8,128)(2,1)}, s32[17,4]{0,1:T(4,128)S(1)}, bf16[17,10,80,128]{3,2,0,1:T(8,128)(2,1)}, s32[]{:T(128)}) %tuple.24), condition=%wide.while_cond, body=%wide.while_body.sunk | while | flops 2 | bytes 411769 | solution.py:69
  261.3 3.7 %bitcast_dynamic-update-slice_fusion.2 = bf16[17,10,80,128]{3,2,0,1:T(8,128)(2,1)} fusion(bf16[17,10,80,128]{3,2,0,1:T(8,128)(2,1)} %get-tuple-element.71, s32[]{:T(128)} %get-tuple-element.68, bf16[17,18,80,136]{3,2,1,0:T(8,128)(2,1)} %get-tuple-element.74, s32[]{:T(128)} %bitcast.251, s32[]{:T(128)} %bitcast.252, s32[]{:T(128)} %bitcast.253), kind=kLoop, calls=%fused_computation.clone.1 | loop fusion | bytes 411648 | tf_op jit(solution)/shard_map/vmap()/gather
  265.6 3.7 %bitcast_dynamic-update-slice_fusion.2 = bf16[17,10,80,128]{3,2,0,1:T(8,128)(2,1)} fusion(bf16[17,10,80,128]{3,2,0,1:T(8,128)(2,1)} %get-tuple-element.71, s32[]{:T(128)} %get-tuple-element.68, bf16[17,18,80,136]{3,2,1,0:T(8,128)(2,1)} %get-tuple-element.74, s32[]{:T(128)} %bitcast.251, s32[]{:T(128)} %bitcast.252, s32[]{:T(128)} %bitcast.253), kind=kLoop, calls=%fused_computation.clone.1 | loop fusion | bytes 411648 | tf_op jit(solution)/shard_map/vmap()/gather
  269.9 3.7 %bitcast_dynamic-update-slice_fusion.2 = bf16[17,10,80,128]{3,2,0,1:T(8,128)(2,1)} fusion(bf16[17,10,80,128]{3,2,0,1:T(8,128)(2,1)} %get-tuple-element.71, s32[]{:T(128)} %get-tuple-element.68, bf16[17,18,80,136]{3,2,1,0:T(8,128)(2,1)} %get-tuple-element.74, s32[]{:T(128)} %bitcast.251, s32[]{:T(128)} %bitcast.252, s32[]{:T(128)} %bitcast.253), kind=kLoop, calls=%fused_computation.clone.1 | loop fusion | bytes 411648 | tf_op jit(solution)/shard_map/vmap()/gather
  274.2 3.7 %bitcast_dynamic-update-slice_fusion.2 = bf16[17,10,80,128]{3,2,0,1:T(8,128)(2,1)} fusion(bf16[17,10,80,128]{3,2,0,1:T(8,128)(2,1)} %get-tuple-element.71, s32[]{:T(128)} %get-tuple-element.68, bf16[17,18,80,136]{3,2,1,0:T(8,128)(2,1)} %get-tuple-element.74, s32[]{:T(128)} %bitcast.251, s32[]{:T(128)} %bitcast.252, s32[]{:T(128)} %bitcast.253), kind=kLoop, calls=%fused_computation.clone.1 | loop fusion | bytes 411648 | tf_op jit(solution)/shard_map/vmap()/gather
  278.5 3.7 %bitcast_dynamic-update-slice_fusion.2 = bf16[17,10,80,128]{3,2,0,1:T(8,128)(2,1)} fusion(bf16[17,10,80,128]{3,2,0,1:T(8,128)(2,1)} %get-tuple-element.71, s32[]{:T(128)} %get-tuple-element.68, bf16[17,18,80,136]{3,2,1,0:T(8,128)(2,1)} %get-tuple-element.74, s32[]{:T(128)} %bitcast.251, s32[]{:T(128)} %bitcast.252, s32[]{:T(128)} %bitcast.253), kind=kLoop, calls=%fused_computation.clone.1 | loop fusion | bytes 411648 | tf_op jit(solution)/shard_map/vmap()/gather
  282.8 3.7 %bitcast_dynamic-update-slice_fusion.2 = bf16[17,10,80,128]{3,2,0,1:T(8,128)(2,1)} fusion(bf16[17,10,80,128]{3,2,0,1:T(8,128)(2,1)} %get-tuple-element.71, s32[]{:T(128)} %get-tuple-element.68, bf16[17,18,80,136]{3,2,1,0:T(8,128)(2,1)} %get-tuple-element.74, s32[]{:T(128)} %bitcast.251, s32[]{:T(128)} %bitcast.252, s32[]{:T(128)} %bitcast.253), kind=kLoop, calls=%fused_computation.clone.1 | loop fusion | bytes 411648 | tf_op jit(solution)/shard_map/vmap()/gather
  287.1 3.7 %bitcast_dynamic-update-slice_fusion.2 = bf16[17,10,80,128]{3,2,0,1:T(8,128)(2,1)} fusion(bf16[17,10,80,128]{3,2,0,1:T(8,128)(2,1)} %get-tuple-element.71, s32[]{:T(128)} %get-tuple-element.68, bf16[17,18,80,136]{3,2,1,0:T(8,128)(2,1)} %get-tuple-element.74, s32[]{:T(128)} %bitcast.251, s32[]{:T(128)} %bitcast.252, s32[]{:T(128)} %bitcast.253), kind=kLoop, calls=%fused_computation.clone.1 | loop fusion | bytes 411648 | tf_op jit(solution)/shard_map/vmap()/gather
  291.4 3.7 %bitcast_dynamic-update-slice_fusion.2 = bf16[17,10,80,128]{3,2,0,1:T(8,128)(2,1)} fusion(bf16[17,10,80,128]{3,2,0,1:T(8,128)(2,1)} %get-tuple-element.71, s32[]{:T(128)} %get-tuple-element.68, bf16[17,18,80,136]{3,2,1,0:T(8,128)(2,1)} %get-tuple-element.74, s32[]{:T(128)} %bitcast.251, s32[]{:T(128)} %bitcast.252, s32[]{:T(128)} %bitcast.253), kind=kLoop, calls=%fused_computation.clone.1 | loop fusion | bytes 411648 | tf_op jit(solution)/shard_map/vmap()/gather
  295.6 3.7 %bitcast_dynamic-update-slice_fusion.2 = bf16[17,10,80,128]{3,2,0,1:T(8,128)(2,1)} fusion(bf16[17,10,80,128]{3,2,0,1:T(8,128)(2,1)} %get-tuple-element.71, s32[]{:T(128)} %get-tuple-element.68, bf16[17,18,80,136]{3,2,1,0:T(8,128)(2,1)} %get-tuple-element.74, s32[]{:T(128)} %bitcast.251, s32[]{:T(128)} %bitcast.252, s32[]{:T(128)} %bitcast.253), kind=kLoop, calls=%fused_computation.clone.1 | loop fusion | bytes 411648 | tf_op jit(solution)/shard_map/vmap()/gather
  299.9 3.7 %bitcast_dynamic-update-slice_fusion.2 = bf16[17,10,80,128]{3,2,0,1:T(8,128)(2,1)} fusion(bf16[17,10,80,128]{3,2,0,1:T(8,128)(2,1)} %get-tuple-element.71, s32[]{:T(128)} %get-tuple-element.68, bf16[17,18,80,136]{3,2,1,0:T(8,128)(2,1)} %get-tuple-element.74, s32[]{:T(128)} %bitcast.251, s32[]{:T(128)} %bitcast.252, s32[]{:T(128)} %bitcast.253), kind=kLoop, calls=%fused_computation.clone.1 | loop fusion | bytes 411648 | tf_op jit(solution)/shard_map/vmap()/gather
  304.3 3.7 %bitcast_dynamic-update-slice_fusion.2 = bf16[17,10,80,128]{3,2,0,1:T(8,128)(2,1)} fusion(bf16[17,10,80,128]{3,2,0,1:T(8,128)(2,1)} %get-tuple-element.71, s32[]{:T(128)} %get-tuple-element.68, bf16[17,18,80,136]{3,2,1,0:T(8,128)(2,1)} %get-tuple-element.74, s32[]{:T(128)} %bitcast.251, s32[]{:T(128)} %bitcast.252, s32[]{:T(128)} %bitcast.253), kind=kLoop, calls=%fused_computation.clone.1 | loop fusion | bytes 411648 | tf_op jit(solution)/shard_map/vmap()/gather
  308.5 3.7 %bitcast_dynamic-update-slice_fusion.2 = bf16[17,10,80,128]{3,2,0,1:T(8,128)(2,1)} fusion(bf16[17,10,80,128]{3,2,0,1:T(8,128)(2,1)} %get-tuple-element.71, s32[]{:T(128)} %get-tuple-element.68, bf16[17,18,80,136]{3,2,1,0:T(8,128)(2,1)} %get-tuple-element.74, s32[]{:T(128)} %bitcast.251, s32[]{:T(128)} %bitcast.252, s32[]{:T(128)} %bitcast.253), kind=kLoop, calls=%fused_computation.clone.1 | loop fusion | bytes 411648 | tf_op jit(solution)/shard_map/vmap()/gather
  312.8 3.7 %bitcast_dynamic-update-slice_fusion.2 = bf16[17,10,80,128]{3,2,0,1:T(8,128)(2,1)} fusion(bf16[17,10,80,128]{3,2,0,1:T(8,128)(2,1)} %get-tuple-element.71, s32[]{:T(128)} %get-tuple-element.68, bf16[17,18,80,136]{3,2,1,0:T(8,128)(2,1)} %get-tuple-element.74, s32[]{:T(128)} %bitcast.251, s32[]{:T(128)} %bitcast.252, s32[]{:T(128)} %bitcast.253), kind=kLoop, calls=%fused_computation.clone.1 | loop fusion | bytes 411648 | tf_op jit(solution)/shard_map/vmap()/gather
  317.1 3.7 %bitcast_dynamic-update-slice_fusion.2 = bf16[17,10,80,128]{3,2,0,1:T(8,128)(2,1)} fusion(bf16[17,10,80,128]{3,2,0,1:T(8,128)(2,1)} %get-tuple-element.71, s32[]{:T(128)} %get-tuple-element.68, bf16[17,18,80,136]{3,2,1,0:T(8,128)(2,1)} %get-tuple-element.74, s32[]{:T(128)} %bitcast.251, s32[]{:T(128)} %bitcast.252, s32[]{:T(128)} %bitcast.253), kind=kLoop, calls=%fused_computation.clone.1 | loop fusion | bytes 411648 | tf_op jit(solution)/shard_map/vmap()/gather
  321.4 3.7 %bitcast_dynamic-update-slice_fusion.2 = bf16[17,10,80,128]{3,2,0,1:T(8,128)(2,1)} fusion(bf16[17,10,80,128]{3,2,0,1:T(8,128)(2,1)} %get-tuple-element.71, s32[]{:T(128)} %get-tuple-element.68, bf16[17,18,80,136]{3,2,1,0:T(8,128)(2,1)} %get-tuple-element.74, s32[]{:T(128)} %bitcast.251, s32[]{:T(128)} %bitcast.252, s32[]{:T(128)} %bitcast.253), kind=kLoop, calls=%fused_computation.clone.1 | loop fusion | bytes 411648 | tf_op jit(solution)/shard_map/vmap()/gather
  325.7 3.7 %bitcast_dynamic-update-slice_fusion.2 = bf16[17,10,80,128]{3,2,0,1:T(8,128)(2,1)} fusion(bf16[17,10,80,128]{3,2,0,1:T(8,128)(2,1)} %get-tuple-element.71, s32[]{:T(128)} %get-tuple-element.68, bf16[17,18,80,136]{3,2,1,0:T(8,128)(2,1)} %get-tuple-element.74, s32[]{:T(128)} %bitcast.251, s32[]{:T(128)} %bitcast.252, s32[]{:T(128)} %bitcast.253), kind=kLoop, calls=%fused_computation.clone.1 | loop fusion | bytes 411648 | tf_op jit(solution)/shard_map/vmap()/gather
  330.0 3.7 %bitcast_dynamic-update-slice_fusion.2 = bf16[17,10,80,128]{3,2,0,1:T(8,128)(2,1)} fusion(bf16[17,10,80,128]{3,2,0,1:T(8,128)(2,1)} %get-tuple-element.71, s32[]{:T(128)} %get-tuple-element.68, bf16[17,18,80,136]{3,2,1,0:T(8,128)(2,1)} %get-tuple-element.74, s32[]{:T(128)} %bitcast.251, s32[]{:T(128)} %bitcast.252, s32[]{:T(128)} %bitcast.253), kind=kLoop, calls=%fused_computation.clone.1 | loop fusion | bytes 411648 | tf_op jit(solution)/shard_map/vmap()/gather
  333.7 2.8 fusion.19
  336.7 2.6 fusion.32
  347.0 2.1 collective-permute-start.4
  350.4 3.4 collective-permute-done.5
  (103 shorter events, 38.7 us)
Async XLA Ops:
  6.5 0.8 copy-start
  6.5 26.8 %copy-start.5 = (s32[8,128]{1,0:T(8,128)S(1)}, s32[8,128]{1,0:T(8,128)}, u32[]{:S(2)}) copy-start(s32[8,128]{1,0:T(8,128)} %param.11) | copy-start | bytes 12292
  6.5 33.4 %copy-start.2 = (bf16[3,3,80,80]{3,2,1,0:T(8,128)(2,1)S(1)}, bf16[3,3,80,80]{3,2,1,0:T(8,128)(2,1)}, u32[]{:S(2)}) copy-start(bf16[3,3,80,80]{3,2,1,0:T(8,128)(2,1)} %param.12) | copy-start | bytes 345604
  6.5 153.4 %all-gather.3.cloned.1.call-start = ((), (), s32[]{:S(2)}) async-start(), calls=%async_computation.1 | async-start | bytes 5406720 | tf_op jit(solution)/shard_map/all_gather | solution.py:36
  33.9 2.6 collective-permute-start
  35.2 4.5 %collective-permute-start.1 = (bf16[1,80,128]{2,1,0:T(8,128)(2,1)S(1)}, bf16[1,80,128]{2,1,0:T(8,128)(2,1)S(1)}, u32[]{:S(2)}, u32[]{:S(2)}) collective-permute-start(bf16[1,80,128]{2,1,0:T(8,128)(2,1)S(1)} %get-tuple-element.29), channel_id=1, source_target_pairs={{1,0},{2,1},{3,2},{4,3},{5,4},{6,5},{7,6},{8,7},{9,8},{10,9},{11,1... | collective-permute-start | bytes 61448 | tf_op jit(solution)/shard_map/ppermute | solution.py:15
  163.0 44.5 %collective-permute-start.2 = (bf16[17,5,80,128]{3,2,1,0:T(8,128)(2,1)}, bf16[17,5,80,128]{3,2,1,0:T(8,128)(2,1)}, u32[]{:S(2)}, u32[]{:S(2)}) collective-permute-start(bf16[17,5,80,128]{3,2,1,0:T(8,128)(2,1)} %slice.221), channel_id=1, source_target_pairs={{0,1},{1,2},{2,3},{3,4},{4,5},{5,6},{6,7},{7,8},{8,9},{9,10},{10,1... | collective-permute-start | bytes 5222408 | tf_op jit(solution)/shard_map/ppermute | solution.py:12
  172.5 72.5 %collective-permute-start.3 = (bf16[17,5,80,128]{3,2,1,0:T(8,128)(2,1)}, bf16[17,5,80,128]{3,2,1,0:T(8,128)(2,1)}, u32[]{:S(2)}, u32[]{:S(2)}) collective-permute-start(bf16[17,5,80,128]{3,2,1,0:T(8,128)(2,1)} %slice.223), channel_id=1, source_target_pairs={{1,0},{2,1},{3,2},{4,3},{5,4},{6,5},{7,6},{8,7},{9,8},{10,9},{11,1... | collective-permute-start | bytes 5222408 | tf_op jit(solution)/shard_map/ppermute | solution.py:15
  174.0 8.5 %copy-start.3 = (s32[1,16,2]{1,2,0:T(2,128)S(1)}, s32[1,16,2]{1,2,0:T(2,128)}, u32[]{:S(2)}) copy-start(s32[1,16,2]{1,2,0:T(2,128)} %param.13) | copy-start | bytes 388
  333.7 3.0 copy-start.4
  333.7 5.6 %slice-start = ((s8[6266880]{0:T(1024)(128)(4,1)}), s8[4194304]{0:T(1024)(128)(4,1)S(1)}, s32[]{:S(2)}) async-start(s8[6266880]{0:T(1024)(128)(4,1)} %bitcast.258), calls=%async_computation.2 | async-start | bytes 8388608
  336.7 2.6 slice-start.1
  346.1 8.1 %copy-start.1 = (bf16[3,3,160,160]{3,2,1,0:T(8,128)(2,1)S(1)}, bf16[3,3,160,160]{3,2,1,0:T(8,128)(2,1)}, u32[]{:S(2)}) copy-start(bf16[3,3,160,160]{3,2,1,0:T(8,128)(2,1)} %param.15) | copy-start | bytes 1382404
  347.0 3.4 collective-permute-start.4
  349.1 4.7 %collective-permute-start.5 = (bf16[1,160,128]{2,1,0:T(8,128)(2,1)S(1)}, bf16[1,160,128]{2,1,0:T(8,128)(2,1)S(1)}, u32[]{:S(2)}, u32[]{:S(2)}) collective-permute-start(bf16[1,160,128]{2,1,0:T(8,128)(2,1)S(1)} %get-tuple-element.27), channel_id=1, source_target_pairs={{1,0},{2,1},{3,2},{4,3},{5,4},{6,5},{7,6},{8,7},{9,8},{10,9},{11,1... | collective-permute-start | bytes 122888 | tf_op jit(solution)/shard_map/ppermute | solution.py:15
Sparse Core Ops, SparseCore 0:
  43.0 116.9 all-gather.2
where the time goes:
time: 371 us; the launch traced here: 365 us
  waiting for transfers between devices  181 us (49%)
  local copies, waits for them, and re-layouts  92.6 us (25%)
  blocking collectives  23.5 us (6%)
  matrix products  21.5 us (6%)
  other arithmetic  16.7 us (5%)
  starting transfers between devices  15.7 us (4%)
  between operations  13.7 us (4%)
    all_gather x1, waiting for transfers between devices, collect(): every = lax.all_gather(slab[None], 'tm', axis=0, tiled=True)  117 us
    gather x51, local copies, waits for them, and re-layouts  73 us
    ppermute x3, waiting for transfers between devices, extended(): lax.ppermute(lax.slice_in_dim(block, 0, width, axis=dim), axis, backward)  44.2 us
    all_to_all x1, blocking collectives, shards(): lax.all_to_all(local_ray, 'rows', split_axis=2, concat_axis=1, tiled=True)  23.5 us
    ppermute x3, waiting for transfers between devices, extended(): lax.ppermute(lax.slice_in_dim(block, block.shape[dim] - width, None, axis...  19.5 us
    concatenate x3, other arithmetic, extended(): block = jnp.concatenate([low, block, high], axis=dim)  16.3 us
    dot_general x9, matrix products, shards(): jnp.einsum('krcw,kco->row', wide[:, a:a + rows, :, b:b + cols], w_win[a,...  13 us
    ppermute x3, starting transfers between devices, extended(): lax.ppermute(lax.slice_in_dim(block, block.shape[dim] - width, None, axis...  11.6 us
  transfers between devices with their start and end apart: 7, of which 5 were waited for; matrix products, arithmetic and copies ran while one was open for 4% of the time, Pallas kernels for 0%

commit v1 on v0

v1 whole, which is shorter than its diff:
```python
import functools

import jax
import jax.numpy as jnp
from jax import lax
from jax.experimental import pallas as pl
from jax.experimental.pallas import tpu as pltpu
from jax.sharding import PartitionSpec as P

BF = jnp.bfloat16
F32 = jnp.float32
EXTRA = 7
REACH = 4


def silu(v):
    return v / (1.0 + jnp.exp(-v))


def spread(acc, lane, chans):
    cols = acc.shape[1]
    low = jnp.where(lane == 0, 0.0, pltpu.roll(acc[:chans], 1, 1))
    high = jnp.where(lane == cols - 1, 0.0, pltpu.roll(acc[2 * chans :], cols - 1, 1))
    return acc[chans : 2 * chans] + low + high


def pack_kernel(shape, scal, feats, w_depth, w_ctx, table, out, stack):
    blocks, frames, columns, chans, rows, total = shape
    frame = scal[1]
    for slot in range(frames):
        source = frame - (frames - 1) + slot
        piece = feats[jnp.maximum(source, 0)]
        stack[slot * columns : (slot + 1) * columns, :] = jnp.where(
            source >= 0, piece, jnp.zeros_like(piece)
        )
    stacked = stack[...]
    depth = jax.nn.sigmoid(jnp.dot(stacked, w_depth[...], preferred_element_type=F32))
    ctx = jnp.dot(stacked, w_ctx[...], preferred_element_type=F32)
    lane = lax.broadcasted_iota(jnp.int32, ctx.shape, 1)
    tab = jnp.concatenate([table[...].astype(F32), jnp.zeros_like(table[...]).astype(F32)], axis=0)
    for block in range(blocks):
        first = rows * block - EXTRA
        turned = pltpu.roll(depth, (chans - first) % depth.shape[1], 1)
        low = max(chans, chans - first)
        high = min(chans + rows + 2 * EXTRA, total - first + chans)
        keep = (lane >= low) & (lane < high)
        message = jnp.where(lane < chans, ctx, jnp.where(keep, turned, 0.0))
        out[block, : frames * columns, :] = message.astype(BF)
        out[block, frames * columns :, :] = tab.astype(BF)


def main_kernel(shape, scal, got, w_bev, w_join, w_out, out, ctx, dep, tab, lifted, moved, hidden):
    blocks, frames, columns, chans, rows, total, cols, wide = shape
    here = scal[0]
    count = blocks * columns
    span = rows + 2 * EXTRA

    for k in range(frames):
        slot = frames - 1 - k
        piece = got[:, slot * columns : (slot + 1) * columns, :].reshape(count, cols)
        turned = piece.astype(F32).T
        ctx[k * chans : (k + 1) * chans, :] = turned[:chans].astype(BF)
        dep[:, k, :] = turned[chans : chans + span]
    for side in range(3):
        block = jnp.clip(here + (side - 1), 0, blocks - 1)
        both = got[block, frames * columns :, :].astype(F32)
        tab[side * rows : (side + 1) * rows, :] = both[:rows]

    number = lax.broadcasted_iota(jnp.int32, (count, cols), 0)

    def lift(pair, carry):
        hots = []
        gains = []
        for half in range(2):
            row = 2 * pair + half
            seen = tab[pl.ds(row + rows - EXTRA, 1), :].astype(jnp.int32)
            hot = jnp.where(number == seen, 1.0, 0.0).astype(BF)
            hots.append(hot)
            gains.append(jnp.dot(dep[row].astype(BF), hot, preferred_element_type=F32))
        hot = jnp.concatenate(hots, axis=1)
        group = 4
        for start in range(0, frames, group):
            stop = min(start + group, frames)
            picked = jnp.dot(
                ctx[start * chans : stop * chans, :], hot, preferred_element_type=F32
            )
            for k in range(start, stop):
                part = picked[(k - start) * chans : (k - start + 1) * chans]
                for half in range(2):
                    value = part[:, half * cols : (half + 1) * cols] * gains[half][k : k + 1, :]
                    lifted[2 * pair + half, k * chans : (k + 1) * chans, :] = value.astype(BF)
        return carry

    lax.fori_loop(0, span // 2, lift, 0)

    lane = lax.broadcasted_iota(jnp.int32, (chans, cols), 1)
    need = rows + 4

    def bev(k, carry):
        dy = scal[2 + 2 * k]
        dx = scal[3 + 2 * k]
        base = dy + REACH
        at = pl.multiple_of(k * chans, 16)
        inside = (lane + dx >= 0) & (lane + dx < cols)
        turn = jnp.where(dx > 0, cols - dx, -dx)
        for pair in range(need // 2):
            sides = [
                lifted[pl.ds(base + 2 * pair + half, 3), pl.ds(at, chans), :].reshape(3 * chans, cols)
                for half in range(2)
            ]
            acc = jnp.dot(w_bev[...], jnp.concatenate(sides, axis=1), preferred_element_type=F32)
            for half in range(2):
                row = here * rows - 2 + dy + 2 * pair + half
                value = silu(spread(acc[:, half * cols : (half + 1) * cols], lane, chans))
                value = pltpu.roll(value, turn, 1)
                keep = inside & (row >= 0) & (row < total)
                moved[2 * pair + half, pl.ds(at, chans), :] = jnp.where(keep, value, 0.0).astype(BF)
        return carry

    lax.fori_loop(0, frames, bev, 0)

    lane_wide = lax.broadcasted_iota(jnp.int32, (wide, cols), 1)

    def join(pair, carry):
        sides = [
            moved[pl.ds(2 * pair + half, 3), :, :].reshape(3 * frames * chans, cols) for half in range(2)
        ]
        acc = jnp.dot(w_join[...], jnp.concatenate(sides, axis=1), preferred_element_type=F32)
        for half in range(2):
            row = here * rows - 1 + 2 * pair + half
            value = silu(spread(acc[:, half * cols : (half + 1) * cols], lane_wide, wide))
            keep = (row >= 0) & (row < total)
            hidden[2 * pair + half] = jnp.where(keep, value, 0.0).astype(BF)
        return carry

    lax.fori_loop(0, (rows + 2) // 2, join, 0)

    def close(pair, carry):
        sides = [hidden[pl.ds(2 * pair + half, 3), :, :].reshape(3 * wide, cols) for half in range(2)]
        acc = jnp.dot(w_out[...], jnp.concatenate(sides, axis=1), preferred_element_type=F32)
        for half in range(2):
            value = spread(acc[:, half * cols : (half + 1) * cols], lane_wide, wide)
            out[2 * pair + half] = value.astype(BF)
        return carry

    lax.fori_loop(0, rows // 2, close, 0)


def taps(weight):
    turned = jnp.transpose(weight, (1, 3, 0, 2))
    return turned.reshape(weight.shape[1] * weight.shape[3], weight.shape[0] * weight.shape[2])


def shards(col_feat, w_depth, w_ctx, col_table, w_bev, offsets, w_join, w_out):
    rows, cols = col_table.shape
    frames = offsets.shape[1] + 1
    chans = w_ctx.shape[1]
    wide = w_out.shape[3]
    columns, depth_k = col_feat.shape[1:]
    blocks = lax.axis_size("rows")
    window = lax.axis_size("tm")
    total = w_depth.shape[1]
    span = rows + 2 * EXTRA

    feats = jnp.broadcast_to(col_feat, (window, columns, depth_k))
    feats = lax.all_to_all(feats, "tm", split_axis=0, concat_axis=0, tiled=True)

    moves = jnp.concatenate([jnp.zeros((1, 2), jnp.int32), offsets[0]], axis=0)
    scal = jnp.concatenate(
        [
            lax.axis_index("rows").astype(jnp.int32).reshape(1),
            lax.axis_index("tm").astype(jnp.int32).reshape(1),
            moves.reshape(-1),
        ]
    )
    vmem = pl.BlockSpec(memory_space=pltpu.VMEM)
    smem = pl.BlockSpec(memory_space=pltpu.SMEM)
    deep = frames * columns + 2 * rows
    messages = pl.pallas_call(
        functools.partial(pack_kernel, (blocks, frames, columns, chans, rows, total)),
        out_shape=jax.ShapeDtypeStruct((blocks, deep, cols), BF),
        in_specs=[smem, vmem, vmem, vmem, vmem],
        out_specs=vmem,
        scratch_shapes=[pltpu.VMEM((frames * columns, depth_k), BF)],
        compiler_params=pltpu.CompilerParams(vmem_limit_bytes=32 * 1024 * 1024),
        name="pack",
    )(scal, feats, w_depth, jnp.pad(w_ctx, ((0, 0), (0, cols - chans))), col_table)
    got = lax.all_to_all(messages, "rows", split_axis=0, concat_axis=0, tiled=True)

    count = blocks * columns
    joined = pl.pallas_call(
        functools.partial(
            main_kernel, (blocks, frames, columns, chans, rows, total, cols, wide)
        ),
        out_shape=jax.ShapeDtypeStruct((rows, wide, cols), BF),
        in_specs=[smem, vmem, vmem, vmem, vmem],
        out_specs=vmem,
        scratch_shapes=[
            pltpu.VMEM((frames * chans, count), BF),
            pltpu.VMEM((span, 32, count), F32),
            pltpu.VMEM((3 * rows, cols), F32),
            pltpu.VMEM((span, frames * chans, cols), BF),
            pltpu.VMEM((rows + 4, frames * chans, cols), BF),
            pltpu.VMEM((rows + 2, wide, cols), BF),
        ],
        compiler_params=pltpu.CompilerParams(vmem_limit_bytes=56 * 1024 * 1024),
        name="main",
    )(scal, got, taps(w_bev), taps(w_join), taps(w_out))
    return joined[None]


def solution(mesh):
    in_specs = (
        P("tm", "rows", None),
        P(),
        P(),
        P("rows", None),
        P(),
        P("tm", None, None),
        P(),
        P(),
    )
    out_specs = P("tm", "rows", None, None)
    return jax.shard_map(shards, mesh=mesh, in_specs=in_specs, out_specs=out_specs, check_vma=False)
```

time: 371 us -> 101 us (0.27); the launches traced: 365 us -> 99.8 us
  waiting for transfers between devices: 181 us -> 20.7 us
  local copies, waits for them, and re-layouts: 92.6 us -> 26.4 us
  Pallas kernels: 0 us -> 28.4 us
  blocking collectives: 23.5 us -> 0 us
  matrix products: 21.5 us -> 0 us
  other arithmetic: 16.7 us -> 0.08 us
  between operations: 13.7 us -> 0.07 us
  starting transfers between devices: 15.7 us -> 24.2 us
    all_gather x1 -> x0, waiting for transfers between devices: 117 us -> none  [collect(): every = lax.all_gather(slab[None], 'tm', axis=0, tiled=True)]
    gather x51 -> x0, local copies, waits for them, and re-layouts: 73 us -> none
    ppermute x6 -> x0, waiting for transfers between devices: 63.7 us -> none  [the longest x3 44.2 us: extended(): lax.ppermute(lax.slice_in_dim(block, 0, width, axis=dim), axis, backward)]
    pallas_call x0 -> x2, Pallas kernels: none -> 28.4 us  [the longest x1 26.3 us: shards(): pl.pallas_call(functools.partial(main_kernel, (blocks, frames, columns, c...]
    all_to_all x0 -> x2, starting transfers between devices: none -> 24.2 us  [the longest x1 17.2 us: shards(): feats = lax.all_to_all(feats, 'tm', split_axis=0, concat_axis=0, tiled=True)]
    all_to_all x1 -> x0, blocking collectives: 23.5 us -> none  [shards(): lax.all_to_all(local_ray, 'rows', split_axis=2, concat_axis=1, tiled=True)]
    dot_general x30 -> x0, matrix products: 21.5 us -> none  [the longest x9 13 us: shards(): jnp.einsum('krcw,kco->row', wide[:, a:a + rows, :, b:b + cols], w_win[a,...]
    all_to_all x0 -> x2, waiting for transfers between devices: none -> 20.7 us  [the longest x1 11.6 us: shards(): feats = lax.all_to_all(feats, 'tm', split_axis=0, concat_axis=0, tiled=True)]
  transfers between devices with their start and end apart: 7 -> 2, of which waited for: 5 -> 2; matrix products, arithmetic and copies ran while one was open for 4% -> 23% of each run, Pallas kernels for 0% -> 0%
where the time goes in v1:
time: 101 us; the launch traced here: 99.8 us
  Pallas kernels  28.4 us (28%)
  local copies, waits for them, and re-layouts  26.4 us (26%)
  starting transfers between devices  24.2 us (24%)
  waiting for transfers between devices  20.7 us (20%)
    pallas_call x1, Pallas kernels, shards(): pl.pallas_call(functools.partial(main_kernel, (blocks, frames, columns, c...  26.3 us
    all_to_all x1, starting transfers between devices, shards(): feats = lax.all_to_all(feats, 'tm', split_axis=0, concat_axis=0, tiled=True)  17.2 us
    reshape x3, local copies, waits for them, and re-layouts, taps(): turned.reshape(weight.shape[1] * weight.shape[3], weight.shape[0] * weigh...  12.3 us
    all_to_all x1, waiting for transfers between devices, shards(): feats = lax.all_to_all(feats, 'tm', split_axis=0, concat_axis=0, tiled=True)  11.6 us
    all_to_all x1, waiting for transfers between devices, shards(): lax.all_to_all(messages, 'rows', split_axis=0, concat_axis=0, tiled=True)  9.11 us
    transpose x3, local copies, waits for them, and re-layouts, taps(): turned = jnp.transpose(weight, (1, 3, 0, 2))  8.38 us
    all_to_all x1, starting transfers between devices, shards(): lax.all_to_all(messages, 'rows', split_axis=0, concat_axis=0, tiled=True)  6.95 us
    unnamed x14, local copies, waits for them, and re-layouts  4.21 us
  transfers between devices with their start and end apart: 2, of which 2 were waited for; matrix products, arithmetic and copies ran while one was open for 23% of the time, Pallas kernels for 0%

profile of v1, /device:TPU:1, one launch (start us, length us, event | category | flops | bytes accessed | tf_op | source)
XLA Modules:
  0.0 99.8 jit_solution(13687768066183383956)
XLA Ops:
  0.0 1.4 %broadcast_in_dim.11 = bf16[32,16,256]{2,1,0:T(8,128)(2,1)} broadcast(bf16[16,256]{1,0:T(8,128)(2,1)} %bitcast.11), dimensions={1,2} | broadcast | bytes 270336 | tf_op jit(solution)/shard_map/broadcast_in_dim | solution.py:165
  1.4 17.2 %all-to-all-start = ((bf16[32,16,256]{2,1,0:T(8,128)(2,1)}), bf16[32,16,256]{2,1,0:T(8,128)(2,1)S(1)}, u32[]{:S(2)}, u32[]{:S(2)}) async-start(bf16[32,16,256]{2,1,0:T(8,128)(2,1)} %broadcast_in_dim.11), calls=%async_computation | async-start | bytes 524288 | tf_op jit(solution)/shard_map/all_to_all | solution.py:166
  18.7 0.8 copy.19
  19.4 0.1 reshape.20
  19.5 0.9 copy.15
  20.4 0.1 pad_add_fusion.scal
  20.5 0.0 copy-start.1
  20.5 11.6 %all-to-all-done.feats = bf16[32,16,256]{2,1,0:T(8,128)(2,1)S(1)} async-done(((bf16[32,16,256]{2,1,0:T(8,128)(2,1)}), bf16[32,16,256]{2,1,0:T(8,128)(2,1)S(1)}, u32[]{:S(2)}, u32[]{:S(2)}) %all-to-all-start) | async-done | bytes 262176 | tf_op jit(solution)/shard_map/all_to_all | solution.py:166
  32.1 0.0 copy-start
  32.1 0.8 copy-done
  32.9 0.0 copy-start.2
  32.9 0.7 copy-done.2
  33.6 2.1 %pack.1 = bf16[16,288,128]{2,1,0:T(8,128)(2,1)} custom-call(s32[36]{0:T(128)S(1)} %pad_add_fusion.scal, bf16[32,16,256]{2,1,0:T(8,128)(2,1)S(1)} %all-to-all-done.feats, bf16[256,128]{1,0:T(8,128)(2,1)S(1)} %copy-done, bf16[256,128]{1,0:T(8,128)(2,1)S(1)} %pad.5.w_ctx, s32[8,128]{1,0:T(8,128)S(1)} %copy-done.2), custom_call_target="tpu_custom_call" | custom-call | tf_op jit(solution)/shard_map/pack/pallas_call | solution.py:179
  35.7 6.9 %all-to-all-start.1 = ((bf16[16,288,128]{2,1,0:T(8,128)(2,1)}), bf16[16,288,128]{2,1,0:T(8,128)(2,1)S(1)}, u32[]{:S(2)}, u32[]{:S(2)}) async-start(bf16[16,288,128]{2,1,0:T(8,128)(2,1)} %pack.1), calls=%async_computation.1 | async-start | bytes 2359296 | tf_op jit(solution)/shard_map/all_to_all | solution.py:188
  42.7 7.3 %copy.17 = bf16[3,160,3,1360]{3,2,1,0:T(4,128)(2,1)} copy(bf16[3,160,3,1360]{3,1,0,2:T(8,128)(2,1)} %bitcast.8) | data formatting | bytes 7833600 | tf_op jit(solution)/shard_map/transpose | solution.py:150
  49.9 0.0 copy-done.1
  49.9 0.0 copy-start.4
  49.9 0.0 copy-start.5
  49.9 10.2 %reshape.22.w_join = bf16[480,4080]{1,0:T(8,128)(2,1)} reshape(bf16[3,160,3,1360]{3,2,1,0:T(4,128)(2,1)} %copy.17) | data formatting | bytes 7833600 | tf_op jit(solution)/shard_map/reshape | solution.py:151
  60.2 0.0 copy-done.4
  60.2 0.9 copy.18
  61.1 1.3 %reshape.23.w_out = bf16[480,480]{1,0:T(8,128)(2,1)} reshape(bf16[3,160,3,160]{3,2,1,0:T(4,128)(2,1)S(1)} %copy.18) | data formatting | bytes 921600 | tf_op jit(solution)/shard_map/reshape | solution.py:151
  62.3 0.0 copy-done.5
  62.3 0.2 copy.16
  62.5 0.8 reshape.21.w_bev
  63.3 9.1 %all-to-all-done.1.got = bf16[16,288,128]{2,1,0:T(8,128)(2,1)S(1)} async-done(((bf16[16,288,128]{2,1,0:T(8,128)(2,1)}), bf16[16,288,128]{2,1,0:T(8,128)(2,1)S(1)}, u32[]{:S(2)}, u32[]{:S(2)}) %all-to-all-start.1) | async-done | bytes 1179680 | tf_op jit(solution)/shard_map/all_to_all | solution.py:188
  72.4 0.0 copy-start.3
  72.4 1.0 %copy-done.3 = bf16[16,288,128]{2,1,0:T(8,128)(2,1)} copy-done((bf16[16,288,128]{2,1,0:T(8,128)(2,1)}, bf16[16,288,128]{2,1,0:T(8,128)(2,1)S(1)}, u32[]{:S(2)}) %copy-start.3) | copy-done | bytes 1179672
  73.5 26.3 %main.1 = bf16[8,160,128]{2,1,0:T(8,128)(2,1)} custom-call(s32[36]{0:T(128)} %copy-done.1, bf16[16,288,128]{2,1,0:T(8,128)(2,1)} %copy-done.3, bf16[240,240]{1,0:T(8,128)(2,1)} %reshape.21.w_bev, bf16[480,4080]{1,0:T(8,128)(2,1)} %reshape.22.w_join, bf16[480,480]{1,0:T(8,128)(2,1)} %reshape.23.w_out), custom_call_target="tpu_custom_call" | custom-call | tf_op jit(solution)/shard_map/main/pallas_call | solution.py:191
  (2 shorter events, 0.0 us)
Async XLA Ops:
  1.4 30.7 %all-to-all-start = ((bf16[32,16,256]{2,1,0:T(8,128)(2,1)}), bf16[32,16,256]{2,1,0:T(8,128)(2,1)S(1)}, u32[]{:S(2)}, u32[]{:S(2)}) async-start(bf16[32,16,256]{2,1,0:T(8,128)(2,1)} %broadcast_in_dim.11), calls=%async_computation | async-start | bytes 524288 | tf_op jit(solution)/shard_map/all_to_all | solution.py:166
  20.5 29.4 %copy-start.1 = (s32[36]{0:T(128)}, s32[36]{0:T(128)S(1)}, u32[]{:S(2)}) copy-start(s32[36]{0:T(128)S(1)} %pad_add_fusion.scal) | copy-start | bytes 436
  32.1 0.8 copy-start
  32.9 0.7 copy-start.2
  35.7 36.8 %all-to-all-start.1 = ((bf16[16,288,128]{2,1,0:T(8,128)(2,1)}), bf16[16,288,128]{2,1,0:T(8,128)(2,1)S(1)}, u32[]{:S(2)}, u32[]{:S(2)}) async-start(bf16[16,288,128]{2,1,0:T(8,128)(2,1)} %pack.1), calls=%async_computation.1 | async-start | bytes 2359296 | tf_op jit(solution)/shard_map/all_to_all | solution.py:188
  49.9 10.2 %copy-start.4 = (bf16[3,3,160,160]{3,2,1,0:T(8,128)(2,1)S(1)}, bf16[3,3,160,160]{3,2,1,0:T(8,128)(2,1)}, u32[]{:S(2)}) copy-start(bf16[3,3,160,160]{3,2,1,0:T(8,128)(2,1)} %param.15) | copy-start | bytes 1382404
  49.9 12.4 %copy-start.5 = (bf16[3,3,80,80]{3,2,1,0:T(8,128)(2,1)S(1)}, bf16[3,3,80,80]{3,2,1,0:T(8,128)(2,1)}, u32[]{:S(2)}) copy-start(bf16[3,3,80,80]{3,2,1,0:T(8,128)(2,1)} %param.12) | copy-start | bytes 345604
  72.4 1.0 %copy-start.3 = (bf16[16,288,128]{2,1,0:T(8,128)(2,1)}, bf16[16,288,128]{2,1,0:T(8,128)(2,1)S(1)}, u32[]{:S(2)}) copy-start(bf16[16,288,128]{2,1,0:T(8,128)(2,1)S(1)} %all-to-all-done.1.got) | copy-start | bytes 3538948

commit v2 on v1

v2 whole, which is shorter than its diff:
```python
import functools

import jax
import jax.numpy as jnp
from jax import lax
from jax.experimental import pallas as pl
from jax.experimental.pallas import tpu as pltpu
from jax.sharding import PartitionSpec as P

BF = jnp.bfloat16
F32 = jnp.float32
EXTRA = 7
REACH = 4
GROUP = 3


def silu(v):
    return v / (1.0 + jnp.exp(-v))


def spread(acc, lane, chans):
    cols = acc.shape[1]
    low = jnp.where(lane == 0, 0.0, pltpu.roll(acc[:chans], 1, 1))
    high = jnp.where(lane == cols - 1, 0.0, pltpu.roll(acc[2 * chans :], cols - 1, 1))
    return acc[chans : 2 * chans] + low + high


def pack_kernel(shape, scal, feats, w_depth, w_ctx, table, out, stack):
    blocks, share, columns, chans, rows, total = shape
    span = rows + 2 * EXTRA
    for slot in range(share):
        source = scal[1] + slot
        piece = feats[jnp.maximum(source, 0)]
        stack[slot * columns : (slot + 1) * columns, :] = jnp.where(
            source >= 0, piece, jnp.zeros_like(piece)
        )
    stacked = stack[...]
    depth = jax.nn.sigmoid(jnp.dot(stacked, w_depth[...], preferred_element_type=F32))
    main = depth.astype(BF).astype(F32)
    rest = depth - main
    ctx = jnp.dot(stacked, w_ctx[...], preferred_element_type=F32)
    lane = lax.broadcasted_iota(jnp.int32, ctx.shape, 1)
    tab = jnp.concatenate([table[...].astype(F32), jnp.zeros_like(table[...]).astype(F32)], axis=0)
    cols = depth.shape[1]
    for block in range(blocks):
        first = rows * block - EXTRA
        message = jnp.where(lane < chans, ctx, 0.0)
        for part, values in enumerate((main, rest)):
            start = chans + part * span
            turned = pltpu.roll(values, (start - first) % cols, 1)
            low = max(start, start - first)
            high = min(start + span, total - first + start)
            message = jnp.where((lane >= low) & (lane < high), turned, message)
        out[block, : share * columns, :] = message.astype(BF)
        out[block, share * columns :, :] = tab.astype(BF)


def lift_and_convolve(shape, scal, got, tabled, w_bev, store, ctx, dep, tab, lifted, skip, last, frames):
    blocks, share, columns, chans, rows, total, cols, wide = shape
    here = scal[0]
    count = blocks * columns
    span = rows + 2 * EXTRA

    for i in range(frames):
        at = (skip + i) * columns
        if not isinstance(at, int):
            at = pl.multiple_of(at, 16)
        piece = got[:, pl.ds(at, columns), :].reshape(count, cols)
        turned = piece.astype(F32).T
        ctx[i * chans : (i + 1) * chans, :] = turned[:chans].astype(BF)
        dep[:, i, :] = turned[chans : chans + span]
        dep[:, 16 + i, :] = turned[chans + span : chans + 2 * span]
    for side in range(3):
        block = jnp.clip(here + (side - 1), 0, blocks - 1)
        both = tabled[block, share * columns :, :].astype(F32)
        tab[side * rows : (side + 1) * rows, :] = both[:rows]

    number = lax.broadcasted_iota(jnp.int32, (count, cols), 0)

    def lift(pair, carry):
        hots = []
        gains = []
        for half in range(2):
            row = 2 * pair + half
            seen = tab[pl.ds(row + rows - EXTRA, 1), :].astype(jnp.int32)
            hot = jnp.where(number == seen, 1.0, 0.0).astype(BF)
            hots.append(hot)
            both = jnp.dot(dep[row].astype(BF), hot, preferred_element_type=F32)
            gains.append(both[:16] + both[16:])
        hot = jnp.concatenate(hots, axis=1)
        for start in range(0, frames, GROUP):
            stop = min(start + GROUP, frames)
            picked = jnp.dot(
                ctx[start * chans : stop * chans, :], hot, preferred_element_type=F32
            )
            for i in range(start, stop):
                part = picked[(i - start) * chans : (i - start + 1) * chans]
                for half in range(2):
                    value = part[:, half * cols : (half + 1) * cols] * gains[half][i : i + 1, :]
                    lifted[2 * pair + half, i * chans : (i + 1) * chans, :] = value.astype(BF)
        return carry

    lax.fori_loop(0, span // 2, lift, 0)

    lane = lax.broadcasted_iota(jnp.int32, (chans, cols), 1)
    need = rows + 4

    def bev(i, carry):
        k = last - i
        dy = scal[4 + 2 * k]
        dx = scal[5 + 2 * k]
        base = dy + REACH
        at = pl.multiple_of(i * chans, 16)
        inside = (lane + dx >= 0) & (lane + dx < cols)
        turn = jnp.where(dx > 0, cols - dx, -dx)
        for pair in range(need // 2):
            sides = [
                lifted[pl.ds(base + 2 * pair + half, 3), pl.ds(at, chans), :].reshape(3 * chans, cols)
                for half in range(2)
            ]
            acc = jnp.dot(w_bev[...], jnp.concatenate(sides, axis=1), preferred_element_type=F32)
            for half in range(2):
                row = here * rows - 2 + dy + 2 * pair + half
                value = silu(spread(acc[:, half * cols : (half + 1) * cols], lane, chans))
                value = pltpu.roll(value, turn, 1)
                keep = inside & (row >= 0) & (row < total)
                store(2 * pair + half, i, jnp.where(keep, value, 0.0).astype(BF))
        return carry

    lax.fori_loop(0, frames, bev, 0)


def own_kernel(shape, scal, got, w_bev, out, ctx, dep, tab, lifted):
    blocks, share, columns, chans, rows, total, cols, wide = shape

    def store(j, i, value):
        at = pl.multiple_of((share - 1 - i) * chans, 16)
        out[j, pl.ds(at, chans), :] = value

    lift_and_convolve(
        shape, scal, got, got, w_bev, store, ctx, dep, tab, lifted, 0, scal[2], share
    )


def join_kernel(
    shape, scal, got, other, own, w_bev, w_join, w_out, out, ctx, dep, tab, lifted, moved, hidden
):
    blocks, share, columns, chans, rows, total, cols, wide = shape
    here = scal[0]
    rest = share - 1
    last = scal[3]

    def store(j, i, value):
        at = pl.multiple_of((last - i) * chans, 16)
        moved[j, pl.ds(at, chans), :] = value

    lift_and_convolve(
        shape, scal, other, got, w_bev, store, ctx, dep, tab, lifted, jnp.where(last > rest, 1, 0), last, rest
    )
    at = pl.multiple_of((scal[2] - rest) * chans, 16)
    for j in range(rows + 4):
        moved[j, pl.ds(at, share * chans), :] = own[j]

    lane_wide = lax.broadcasted_iota(jnp.int32, (wide, cols), 1)

    def join(pair, carry):
        acc = None
        for a in range(3):
            both = jnp.concatenate([moved[2 * pair + a], moved[2 * pair + 1 + a]], axis=1)
            part = jnp.dot(w_join[a], both, preferred_element_type=F32)
            acc = part if acc is None else acc + part
        for half in range(2):
            row = here * rows - 1 + 2 * pair + half
            value = silu(spread(acc[:, half * cols : (half + 1) * cols], lane_wide, wide))
            keep = (row >= 0) & (row < total)
            hidden[2 * pair + half] = jnp.where(keep, value, 0.0).astype(BF)
        return carry

    lax.fori_loop(0, (rows + 2) // 2, join, 0)

    def close(pair, carry):
        sides = [hidden[pl.ds(2 * pair + half, 3), :, :].reshape(3 * wide, cols) for half in range(2)]
        acc = jnp.dot(w_out[...], jnp.concatenate(sides, axis=1), preferred_element_type=F32)
        for half in range(2):
            value = spread(acc[:, half * cols : (half + 1) * cols], lane_wide, wide)
            out[2 * pair + half] = value.astype(BF)
        return carry

    lax.fori_loop(0, rows // 2, close, 0)


def taps(weight):
    turned = jnp.transpose(weight, (1, 3, 0, 2))
    return turned.reshape(weight.shape[1] * weight.shape[3], weight.shape[0] * weight.shape[2])


VMEM = pl.BlockSpec(memory_space=pltpu.VMEM)
SMEM = pl.BlockSpec(memory_space=pltpu.SMEM)


def scratch(frames, chans, count, rows, cols):
    span = rows + 2 * EXTRA
    return [
        pltpu.VMEM((frames * chans, count), BF),
        pltpu.VMEM((span, 32, count), F32),
        pltpu.VMEM((3 * rows, cols), F32),
        pltpu.VMEM((span, frames * chans, cols), BF),
    ]


def call_pack(shape, scal, feats, w_depth, w_ctx, table):
    blocks, share, columns, chans, rows, total, cols, wide = shape
    return pl.pallas_call(
        functools.partial(pack_kernel, shape[:6]),
        out_shape=jax.ShapeDtypeStruct((blocks, share * columns + 2 * rows, cols), BF),
        in_specs=[SMEM, VMEM, VMEM, VMEM, VMEM],
        out_specs=VMEM,
        scratch_shapes=[pltpu.VMEM((share * columns, feats.shape[2]), BF)],
        compiler_params=pltpu.CompilerParams(vmem_limit_bytes=32 * 1024 * 1024),
        name="pack",
    )(scal, feats, w_depth, w_ctx, table)


def call_own(shape, scal, got, w_bev):
    blocks, share, columns, chans, rows, total, cols, wide = shape
    return pl.pallas_call(
        functools.partial(own_kernel, shape),
        out_shape=jax.ShapeDtypeStruct((rows + 4, share * chans, cols), BF),
        in_specs=[SMEM, VMEM, VMEM],
        out_specs=VMEM,
        scratch_shapes=scratch(share, chans, blocks * columns, rows, cols),
        compiler_params=pltpu.CompilerParams(vmem_limit_bytes=32 * 1024 * 1024),
        name="own",
    )(scal, got, w_bev)


def call_join(shape, scal, got, other, own, w_bev, w_join, w_out):
    blocks, share, columns, chans, rows, total, cols, wide = shape
    return pl.pallas_call(
        functools.partial(join_kernel, shape),
        out_shape=jax.ShapeDtypeStruct((rows, wide, cols), BF),
        in_specs=[SMEM] + [VMEM] * 6,
        out_specs=VMEM,
        scratch_shapes=scratch(share - 1, chans, blocks * columns, rows, cols)
        + [
            pltpu.VMEM((rows + 4, (2 * share - 1) * chans, cols), BF),
            pltpu.VMEM((rows + 2, wide, cols), BF),
        ],
        compiler_params=pltpu.CompilerParams(vmem_limit_bytes=48 * 1024 * 1024),
        name="join",
    )(scal, got, other, own, w_bev, w_join, w_out)


def shards(col_feat, w_depth, w_ctx, col_table, w_bev, offsets, w_join, w_out):
    rows, cols = col_table.shape
    frames = offsets.shape[1] + 1
    chans = w_ctx.shape[1]
    wide = w_out.shape[3]
    columns, depth_k = col_feat.shape[1:]
    blocks = lax.axis_size("rows")
    window = lax.axis_size("tm")
    total = w_depth.shape[1]
    share = (frames + 1) // 2
    shape = (blocks, share, columns, chans, rows, total, cols, wide)

    feats = jnp.broadcast_to(col_feat, (window, columns, depth_k))
    feats = lax.all_to_all(feats, "tm", split_axis=0, concat_axis=0, tiled=True)
    w_ctx = jnp.pad(w_ctx, ((0, 0), (0, cols - chans)))
    feats, w_ctx, w_bev, w_out = lax.optimization_barrier((feats, w_ctx, taps(w_bev), taps(w_out)))

    frame = lax.axis_index("tm").astype(jnp.int32)
    core = frame % 2
    head = jnp.stack(
        [
            lax.axis_index("rows").astype(jnp.int32),
            frame - core - (frames - 1) + share * core,
            frames - 1 - (share - 1) * core,
            share - 2 + share * core,
        ]
    )
    moves = jnp.concatenate([jnp.zeros((1, 2), jnp.int32), offsets[0]], axis=0)
    scal = jnp.concatenate([head, moves.reshape(-1)])

    messages = call_pack(shape, scal, feats, w_depth, w_ctx, col_table)
    got = lax.all_to_all(messages, "rows", split_axis=0, concat_axis=0, tiled=True)
    other = lax.ppermute(got, "tm", [(i, i ^ 1) for i in range(window)])

    w_join = jnp.transpose(w_join, (0, 1, 3, 2)).reshape(3, 3 * wide, frames * chans)
    own = call_own(shape, scal, got, w_bev)
    joined = call_join(shape, scal, got, other, own, w_bev, w_join, w_out)
    return joined[None]


def solution(mesh):
    in_specs = (
        P("tm", "rows", None),
        P(),
        P(),
        P("rows", None),
        P(),
        P("tm", None, None),
        P(),
        P(),
    )
    out_specs = P("tm", "rows", None, None)
    return jax.shard_map(shards, mesh=mesh, in_specs=in_specs, out_specs=out_specs, check_vma=False)
```

time: 101 us -> 92.1 us (0.912)
  blocking collectives: 0 us -> 25.3 us
  local copies, waits for them, and re-layouts: 26.4 us -> 7.02 us
  waiting for transfers between devices: 20.7 us -> 7.8 us
  starting transfers between devices: 24.2 us -> 20.9 us
  Pallas kernels: 28.4 us -> 30.6 us
    all_to_all x0 -> x1, blocking collectives: none -> 25.3 us  [shards(): lax.all_to_all(messages, 'rows', split_axis=0, concat_axis=0, tiled=True)]
    reshape x3 -> x2, local copies, waits for them, and re-layouts: 12.3 us -> 0.71 us  [taps(): turned.reshape(weight.shape[1] * weight.shape[3], weight.shape[0] * weigh...]
    all_to_all x1 -> x0, waiting for transfers between devices: 9.11 us -> none  [shards(): lax.all_to_all(messages, 'rows', split_axis=0, concat_axis=0, tiled=True)]
    all_to_all x1 -> x0, starting transfers between devices: 6.95 us -> none  [shards(): lax.all_to_all(messages, 'rows', split_axis=0, concat_axis=0, tiled=True)]
    transpose x3 -> x2, local copies, waits for them, and re-layouts: 8.38 us -> 3.01 us  [taps(): turned = jnp.transpose(weight, (1, 3, 0, 2))]
    all_to_all x1, waiting for transfers between devices: 11.6 us -> 7.8 us  [shards(): feats = lax.all_to_all(feats, 'tm', split_axis=0, concat_axis=0, tiled=True)]
    ppermute x0 -> x1, starting transfers between devices: none -> 3.65 us  [shards(): other = lax.ppermute(got, 'tm', [(i, i ^ 1) for i in range(window)])]
    unnamed x14 -> x6, local copies, waits for them, and re-layouts: 4.21 us -> 1.66 us
  transfers between devices with their start and end apart: 2 -> 2, of which waited for: 2 -> 1; matrix products, arithmetic and copies ran while one was open for 23% -> 6% of each run, Pallas kernels for 0% -> 11%
where the time goes in v2:
time: 92.1 us; the launch traced here: 91.7 us
  Pallas kernels  30.6 us (33%)
  blocking collectives  25.3 us (27%)
  starting transfers between devices  20.9 us (23%)
  waiting for transfers between devices  7.8 us (8%)
  local copies, waits for them, and re-layouts  7.02 us (8%)
    all_to_all x1, blocking collectives, shards(): lax.all_to_all(messages, 'rows', split_axis=0, concat_axis=0, tiled=True)  25.3 us
    pallas_call x1, Pallas kernels, call_join(): pl.pallas_call(functools.partial(join_kernel, shape), out_shape=jax.Shape...  19.9 us
    all_to_all x1, starting transfers between devices, shards(): feats = lax.all_to_all(feats, 'tm', split_axis=0, concat_axis=0, tiled=True)  17.2 us
    pallas_call x1, Pallas kernels, call_own(): pl.pallas_call(functools.partial(own_kernel, shape), out_shape=jax.ShapeD...  9.68 us
    all_to_all x1, waiting for transfers between devices, shards(): feats = lax.all_to_all(feats, 'tm', split_axis=0, concat_axis=0, tiled=True)  7.8 us
    ppermute x1, starting transfers between devices, shards(): other = lax.ppermute(got, 'tm', [(i, i ^ 1) for i in range(window)])  3.65 us
    transpose x2, local copies, waits for them, and re-layouts, taps(): turned = jnp.transpose(weight, (1, 3, 0, 2))  3.01 us
  transfers between devices with their start and end apart: 2, of which 1 were waited for; matrix products, arithmetic and copies ran while one was open for 6% of the time, Pallas kernels for 11%

profile of v2, /device:TPU:1, one launch (start us, length us, event | category | flops | bytes accessed | tf_op | source)
XLA Modules:
  0.0 91.7 jit_solution(8252251469957341617)
XLA Ops:
  0.0 0.0 copy-start.1
  0.0 0.0 copy-start
  0.0 1.4 %broadcast_in_dim.11 = bf16[32,16,256]{2,1,0:T(8,128)(2,1)} broadcast(bf16[16,256]{1,0:T(8,128)(2,1)} %bitcast.15), dimensions={1,2} | broadcast | bytes 270336 | tf_op jit(solution)/shard_map/broadcast_in_dim | solution.py:266
  1.5 17.2 %all-to-all-start = ((bf16[32,16,256]{2,1,0:T(8,128)(2,1)}), bf16[32,16,256]{2,1,0:T(8,128)(2,1)S(1)}, u32[]{:S(2)}, u32[]{:S(2)}) async-start(bf16[32,16,256]{2,1,0:T(8,128)(2,1)} %broadcast_in_dim.11), calls=%async_computation | async-start | bytes 524288 | tf_op jit(solution)/shard_map/all_to_all | solution.py:267
  18.7 0.8 copy.17
  19.5 0.1 reshape.12
  19.6 0.9 copy.14
  20.5 1.1 %copy.15 = bf16[3,80,3,80]{3,2,1,0:T(4,128)(2,1)S(1)} copy(bf16[3,80,3,80]{1,3,0,2:T(8,128)(2,1)} %bitcast.14) | data formatting | bytes 230400 | tf_op jit(solution)/shard_map/transpose | solution.py:193
  21.6 0.2 reshape.13.w_bev
  21.7 1.9 %copy.16 = bf16[3,160,3,160]{3,2,1,0:T(4,128)(2,1)S(1)} copy(bf16[3,160,3,160]{1,3,0,2:T(8,128)(2,1)} %bitcast.13) | data formatting | bytes 921600 | tf_op jit(solution)/shard_map/transpose | solution.py:193
  23.7 0.6 reshape.14.w_out
  24.3 0.1 concatenate.7.scal
  24.3 7.8 %all-to-all-done.feats = bf16[32,16,256]{2,1,0:T(8,128)(2,1)S(1)} async-done(((bf16[32,16,256]{2,1,0:T(8,128)(2,1)}), bf16[32,16,256]{2,1,0:T(8,128)(2,1)S(1)}, u32[]{:S(2)}, u32[]{:S(2)}) %all-to-all-start) | async-done | bytes 262176 | tf_op jit(solution)/shard_map/all_to_all | solution.py:267
  32.1 0.0 copy-done.1
  32.1 0.0 copy-done
  32.1 1.1 %pack.1 = bf16[16,160,128]{2,1,0:T(8,128)(2,1)S(1)} custom-call(s32[38]{0:T(128)S(1)} %concatenate.7.scal, bf16[32,16,256]{2,1,0:T(8,128)(2,1)S(1)} %all-to-all-done.feats, bf16[256,128]{1,0:T(8,128)(2,1)S(1)} %copy-done, bf16[256,128]{1,0:T(8,128)(2,1)S(1)} %pad.5.w_ctx, s32[8,128]{1,0:T(8,128)S(1)} %copy-done.1), custom_call_target="tpu_custom_call" | custom-call | tf_op jit(solution)/shard_map/pack/pallas_call | solution.py:213
  33.2 25.3 %all_to_all.10.got = bf16[16,160,128]{2,1,0:T(8,128)(2,1)S(1)} all-to-all(bf16[16,160,128]{2,1,0:T(8,128)(2,1)S(1)} %pack.1), channel_id=1, replica_groups=mesh['tm'=32,'rows'=16] {'rows'}, dimensions={0} | all-to-all | bytes 1310720 | tf_op jit(solution)/shard_map/all_to_all | solution.py:285
  58.5 3.7 %collective-permute-start = (bf16[16,160,128]{2,1,0:T(8,128)(2,1)S(1)}, bf16[16,160,128]{2,1,0:T(8,128)(2,1)S(1)}, u32[]{:S(2)}, u32[]{:S(2)}) collective-permute-start(bf16[16,160,128]{2,1,0:T(8,128)(2,1)S(1)} %all_to_all.10.got), channel_id=1, source_target_pairs={{0,16},{16,0},{32,48},{48,32},{64,80},{80,64},{96,112},{112,96},{1... | collective-permute-start | bytes 1966088 | tf_op jit(solution)/shard_map/ppermute | solution.py:286
  62.1 9.7 %own.1 = bf16[12,720,128]{2,1,0:T(8,128)(2,1)S(1)} custom-call(s32[38]{0:T(128)S(1)} %concatenate.7.scal, bf16[16,160,128]{2,1,0:T(8,128)(2,1)S(1)} %all_to_all.10.got, bf16[240,240]{1,0:T(8,128)(2,1)S(1)} %reshape.13.w_bev), custom_call_target="tpu_custom_call" | custom-call | tf_op jit(solution)/shard_map/own/pallas_call | solution.py:226
  71.8 0.0 collective-permute-done.other
  71.8 19.9 %join.1 = bf16[8,160,128]{2,1,0:T(8,128)(2,1)} custom-call(s32[38]{0:T(128)S(1)} %concatenate.7.scal, bf16[16,160,128]{2,1,0:T(8,128)(2,1)S(1)} %all_to_all.10.got, bf16[16,160,128]{2,1,0:T(8,128)(2,1)S(1)} %collective-permute-done.other, bf16[12,720,128]{2,1,0:T(8,128)(2,1)S(1)} %own.1, bf16[240,240]{1,0:T(8,128)(2,1)S(1)} %reshape.13.w_bev, ...), custom_call_target="tpu_custom_call" | custom-call | tf_op jit(solution)/shard_map/join/pallas_call | solution.py:239
  (2 shorter events, 0.0 us)
Async XLA Ops:
  0.0 32.1 %copy-start.1 = (s32[8,128]{1,0:T(8,128)S(1)}, s32[8,128]{1,0:T(8,128)}, u32[]{:S(2)}) copy-start(s32[8,128]{1,0:T(8,128)} %table.1) | copy-start | bytes 12292
  0.0 32.1 %copy-start = (bf16[256,128]{1,0:T(8,128)(2,1)S(1)}, bf16[256,128]{1,0:T(8,128)(2,1)}, u32[]{:S(2)}) copy-start(bf16[256,128]{1,0:T(8,128)(2,1)} %w_depth.1) | copy-start | bytes 196612
  1.5 30.7 %all-to-all-start = ((bf16[32,16,256]{2,1,0:T(8,128)(2,1)}), bf16[32,16,256]{2,1,0:T(8,128)(2,1)S(1)}, u32[]{:S(2)}, u32[]{:S(2)}) async-start(bf16[32,16,256]{2,1,0:T(8,128)(2,1)} %broadcast_in_dim.11), calls=%async_computation | async-start | bytes 524288 | tf_op jit(solution)/shard_map/all_to_all | solution.py:267
  58.5 13.3 %collective-permute-start = (bf16[16,160,128]{2,1,0:T(8,128)(2,1)S(1)}, bf16[16,160,128]{2,1,0:T(8,128)(2,1)S(1)}, u32[]{:S(2)}, u32[]{:S(2)}) collective-permute-start(bf16[16,160,128]{2,1,0:T(8,128)(2,1)S(1)} %all_to_all.10.got), channel_id=1, source_target_pairs={{0,16},{16,0},{32,48},{48,32},{64,80},{80,64},{96,112},{112,96},{1... | collective-permute-start | bytes 1966088 | tf_op jit(solution)/shard_map/ppermute | solution.py:286

commit v3 on v2

v3 whole, which is shorter than its diff:
```python
import functools

import jax
import jax.numpy as jnp
from jax import lax
from jax.experimental import pallas as pl
from jax.experimental.pallas import tpu as pltpu
from jax.sharding import PartitionSpec as P

BF = jnp.bfloat16
F32 = jnp.float32
EXTRA = 7
REACH = 4
GROUP = 3
LIFT = 22
BEV = 2
JOIN = 10
CLOSE = 8


def silu(v):
    return v / (1.0 + jnp.exp(-v))


def spread(acc, lane, chans):
    cols = acc.shape[1]
    low = jnp.where(lane == 0, 0.0, pltpu.roll(acc[:chans], 1, 1))
    high = jnp.where(lane == cols - 1, 0.0, pltpu.roll(acc[2 * chans :], cols - 1, 1))
    return acc[chans : 2 * chans] + low + high


def pack_kernel(shape, scal, feats, w_depth, w_ctx, out, stack):
    blocks, share, columns, chans, rows, total = shape
    span = rows + 2 * EXTRA
    for slot in range(share):
        source = scal[1] + slot
        piece = feats[jnp.maximum(source, 0)]
        stack[slot * columns : (slot + 1) * columns, :] = jnp.where(
            source >= 0, piece, jnp.zeros_like(piece)
        )
    stacked = stack[...]
    depth = jax.nn.sigmoid(jnp.dot(stacked, w_depth[...], preferred_element_type=F32))
    main = depth.astype(BF).astype(F32)
    rest = depth - main
    ctx = jnp.dot(stacked, w_ctx[...], preferred_element_type=F32)
    lane = lax.broadcasted_iota(jnp.int32, ctx.shape, 1)
    cols = depth.shape[1]
    for block in range(blocks):
        first = rows * block - EXTRA
        message = jnp.where(lane < chans, ctx, 0.0)
        for part, values in enumerate((main, rest)):
            start = chans + part * span
            turned = pltpu.roll(values, (start - first) % cols, 1)
            low = max(start, start - first)
            high = min(start + span, total - first + start)
            message = jnp.where((lane >= low) & (lane < high), turned, message)
        out[block] = message.astype(BF)


def lift_and_convolve(shape, scal, got, tables, w_bev, store, ctx, dep, tab, lifted, skip, last, frames):
    blocks, share, columns, chans, rows, total, cols, wide = shape
    here = scal[0]
    count = blocks * columns
    span = rows + 2 * EXTRA

    for i in range(frames):
        at = (skip + i) * columns
        if not isinstance(at, int):
            at = pl.multiple_of(at, 16)
        piece = got[:, pl.ds(at, columns), :].reshape(count, cols)
        turned = piece.astype(F32).T
        ctx[i * chans : (i + 1) * chans, :] = turned[:chans].astype(BF)
        dep[:, i, :] = turned[chans : chans + span]
        dep[:, 16 + i, :] = turned[chans + span : chans + 2 * span]
    for side in range(3):
        tab[side * rows : (side + 1) * rows, :] = tables[side][...]

    number = lax.broadcasted_iota(jnp.int32, (count, cols), 0)

    def lift(pair, carry):
        hots = []
        gains = []
        for half in range(LIFT):
            row = LIFT * pair + half
            seen = tab[pl.ds(row + rows - EXTRA, 1), :]
            hot = jnp.where(number == seen, 1.0, 0.0).astype(BF)
            hots.append(hot)
            both = jnp.dot(dep[row].astype(BF), hot, preferred_element_type=F32)
            gains.append(both[:16] + both[16:])
        hot = jnp.concatenate(hots, axis=1)
        for start in range(0, frames, GROUP):
            stop = min(start + GROUP, frames)
            picked = jnp.dot(
                ctx[start * chans : stop * chans, :], hot, preferred_element_type=F32
            )
            for i in range(start, stop):
                part = picked[(i - start) * chans : (i - start + 1) * chans]
                for half in range(LIFT):
                    value = part[:, half * cols : (half + 1) * cols] * gains[half][i : i + 1, :]
                    lifted[LIFT * pair + half, i * chans : (i + 1) * chans, :] = value.astype(BF)
        return carry

    lax.fori_loop(0, span // LIFT, lift, 0)

    lane = lax.broadcasted_iota(jnp.int32, (chans, cols), 1)
    need = rows + 4

    def bev(i, carry):
        k = last - 2 * i
        dy = scal[3 + 2 * k]
        dx = scal[4 + 2 * k]
        base = dy + REACH
        at = pl.multiple_of(i * chans, 16)
        inside = (lane + dx >= 0) & (lane + dx < cols)
        turn = jnp.where(dx > 0, cols - dx, -dx)
        for pair in range(need // BEV):
            sides = [
                lifted[pl.ds(base + BEV * pair + half, 3), pl.ds(at, chans), :].reshape(3 * chans, cols)
                for half in range(BEV)
            ]
            acc = jnp.dot(w_bev[...], jnp.concatenate(sides, axis=1), preferred_element_type=F32)
            for half in range(BEV):
                row = here * rows - 2 + dy + BEV * pair + half
                value = silu(spread(acc[:, half * cols : (half + 1) * cols], lane, chans))
                value = pltpu.roll(value, turn, 1)
                keep = inside & (row >= 0) & (row < total)
                store(BEV * pair + half, i, jnp.where(keep, value, 0.0).astype(BF))
        return carry

    lax.fori_loop(0, frames, bev, 0)


def own_kernel(shape, scal, got, low, mid, high, w_bev, out, ctx, dep, tab, lifted):
    share, chans = shape[1], shape[3]

    def store(j, i, value):
        out[j, pl.ds(pl.multiple_of(i * chans, 16), chans), :] = value

    lift_and_convolve(
        shape, scal, got, (low, mid, high), w_bev, store, ctx, dep, tab, lifted, 0, 2 * share - 2, share
    )


def join_kernel(
    shape, scal, other, low, mid, high, own, w_bev, w_join, w_out, out, ctx, dep, tab, lifted, moved, hidden
):
    blocks, share, columns, chans, rows, total, cols, wide = shape
    here = scal[0]
    last = 2 * share - 3

    def store(j, i, value):
        moved[j, pl.ds(pl.multiple_of((last - 2 * i) * chans, 16), chans), :] = value

    lift_and_convolve(
        shape, scal, other, (low, mid, high), w_bev, store, ctx, dep, tab, lifted, scal[2], last, share - 1
    )
    for i in range(share):
        at = (2 * share - 2 - 2 * i) * chans
        for j in range(rows + 4):
            moved[j, at : at + chans, :] = own[j, i * chans : (i + 1) * chans, :]

    lane_wide = lax.broadcasted_iota(jnp.int32, (wide, cols), 1)

    def join(pair, carry):
        acc = None
        for a in range(3):
            both = jnp.concatenate([moved[JOIN * pair + h + a] for h in range(JOIN)], axis=1)
            part = jnp.dot(w_join[a], both, preferred_element_type=F32)
            acc = part if acc is None else acc + part
        for half in range(JOIN):
            row = here * rows - 1 + JOIN * pair + half
            value = silu(spread(acc[:, half * cols : (half + 1) * cols], lane_wide, wide))
            keep = (row >= 0) & (row < total)
            hidden[JOIN * pair + half] = jnp.where(keep, value, 0.0).astype(BF)
        return carry

    lax.fori_loop(0, (rows + 2) // JOIN, join, 0)

    def close(pair, carry):
        sides = [hidden[pl.ds(CLOSE * pair + half, 3), :, :].reshape(3 * wide, cols) for half in range(CLOSE)]
        acc = jnp.dot(w_out[...], jnp.concatenate(sides, axis=1), preferred_element_type=F32)
        for half in range(CLOSE):
            value = spread(acc[:, half * cols : (half + 1) * cols], lane_wide, wide)
            out[CLOSE * pair + half] = value.astype(BF)
        return carry

    lax.fori_loop(0, rows // CLOSE, close, 0)


def taps(weight):
    turned = jnp.transpose(weight, (1, 3, 0, 2))
    return turned.reshape(weight.shape[1] * weight.shape[3], weight.shape[0] * weight.shape[2])


VMEM = pl.BlockSpec(memory_space=pltpu.VMEM)
SMEM = pl.BlockSpec(memory_space=pltpu.SMEM)


def scratch(frames, chans, count, rows, cols):
    span = rows + 2 * EXTRA
    return [
        pltpu.VMEM((frames * chans, count), BF),
        pltpu.VMEM((span, 32, count), F32),
        pltpu.VMEM((3 * rows, cols), jnp.int32),
        pltpu.VMEM((span, frames * chans, cols), BF),
    ]


def call_pack(shape, scal, feats, w_depth, w_ctx):
    blocks, share, columns, chans, rows, total, cols, wide = shape
    return pl.pallas_call(
        functools.partial(pack_kernel, shape[:6]),
        out_shape=jax.ShapeDtypeStruct((blocks, share * columns, cols), BF),
        in_specs=[SMEM, VMEM, VMEM, VMEM],
        out_specs=VMEM,
        scratch_shapes=[pltpu.VMEM((share * columns, feats.shape[2]), BF)],
        compiler_params=pltpu.CompilerParams(vmem_limit_bytes=32 * 1024 * 1024),
        name="pack",
    )(scal, feats, w_depth, w_ctx)


def call_own(shape, scal, got, tables, w_bev):
    blocks, share, columns, chans, rows, total, cols, wide = shape
    return pl.pallas_call(
        functools.partial(own_kernel, shape),
        out_shape=jax.ShapeDtypeStruct((rows + 4, share * chans, cols), BF),
        in_specs=[SMEM] + [VMEM] * 5,
        out_specs=VMEM,
        scratch_shapes=scratch(share, chans, blocks * columns, rows, cols),
        compiler_params=pltpu.CompilerParams(vmem_limit_bytes=24 * 1024 * 1024),
        name="own",
    )(scal, got, *tables, w_bev)


def call_join(shape, scal, other, tables, own, w_bev, w_join, w_out):
    blocks, share, columns, chans, rows, total, cols, wide = shape
    return pl.pallas_call(
        functools.partial(join_kernel, shape),
        out_shape=jax.ShapeDtypeStruct((rows, wide, cols), BF),
        in_specs=[SMEM] + [VMEM] * 8,
        out_specs=VMEM,
        scratch_shapes=scratch(share - 1, chans, blocks * columns, rows, cols)
        + [
            pltpu.VMEM((rows + 4, (2 * share - 1) * chans, cols), BF),
            pltpu.VMEM((rows + 2, wide, cols), BF),
        ],
        compiler_params=pltpu.CompilerParams(vmem_limit_bytes=36 * 1024 * 1024),
        name="join",
    )(scal, other, *tables, own, w_bev, w_join, w_out)


def shards(col_feat, w_depth, w_ctx, col_table, w_bev, offsets, w_join, w_out):
    rows, cols = col_table.shape
    frames = offsets.shape[1] + 1
    chans = w_ctx.shape[1]
    wide = w_out.shape[3]
    columns, depth_k = col_feat.shape[1:]
    blocks = lax.axis_size("rows")
    window = lax.axis_size("tm")
    total = w_depth.shape[1]
    share = (frames + 1) // 2
    shape = (blocks, share, columns, chans, rows, total, cols, wide)

    feats = jnp.broadcast_to(col_feat, (window // 2, columns, depth_k))
    groups = [list(range(core, window, 2)) for core in range(2)]
    feats = lax.all_to_all(
        feats, "tm", split_axis=0, concat_axis=0, axis_index_groups=groups, tiled=True
    )
    up = [(i, i + 1) for i in range(blocks - 1)]
    tables = (
        lax.ppermute(col_table, "rows", up),
        col_table,
        lax.ppermute(col_table, "rows", [(t, s) for s, t in up]),
    )
    w_ctx = jnp.pad(w_ctx, ((0, 0), (0, cols - chans)))
    feats, tables, w_ctx, w_bev, w_out = lax.optimization_barrier(
        (feats, tables, w_ctx, taps(w_bev), taps(w_out))
    )

    frame = lax.axis_index("tm").astype(jnp.int32)
    head = jnp.stack(
        [lax.axis_index("rows").astype(jnp.int32), (frame >> 1) - (share - 1), frame & 1]
    )
    moves = jnp.concatenate([jnp.zeros((1, 2), jnp.int32), offsets[0]], axis=0)
    scal = jnp.concatenate([head, moves.reshape(-1)])

    messages = call_pack(shape, scal, feats, w_depth, w_ctx)
    got = lax.all_to_all(messages, "rows", split_axis=0, concat_axis=0, tiled=True)
    other = lax.ppermute(got, "tm", [(i, i ^ 1) for i in range(window)])

    w_join = jnp.transpose(w_join, (0, 1, 3, 2)).reshape(3, 3 * wide, frames * chans)
    own = call_own(shape, scal, got, tables, w_bev)
    joined = call_join(shape, scal, other, tables, own, w_bev, w_join, w_out)
    return joined[None]


def solution(mesh):
    in_specs = (
        P("tm", "rows", None),
        P(),
        P(),
        P("rows", None),
        P(),
        P("tm", None, None),
        P(),
        P(),
    )
    out_specs = P("tm", "rows", None, None)
    return jax.shard_map(shards, mesh=mesh, in_specs=in_specs, out_specs=out_specs, check_vma=False)
```

time: 92.1 us -> 81 us (0.88)
  Pallas kernels: 30.6 us -> 24.2 us
  waiting for transfers between devices: 7.8 us -> 2.18 us
  starting transfers between devices: 20.9 us -> 23.7 us
  blocking collectives: 25.3 us -> 23.4 us
    all_to_all x1, waiting for transfers between devices: 7.8 us -> 2.17 us  [shards(): lax.all_to_all(feats, 'tm', split_axis=0, concat_axis=0, axis_index_group...]
    pallas_call x1, Pallas kernels: 19.9 us -> 15.2 us  [call_join(): pl.pallas_call(functools.partial(join_kernel, shape), out_shape=jax.Shape...]
    ppermute x0 -> x2, starting transfers between devices: none -> 3.6 us  [the longest x1 2.3 us: shards(): lax.ppermute(col_table, 'rows', up)]
    all_to_all x1, blocking collectives: 25.3 us -> 23.4 us  [shards(): lax.all_to_all(messages, 'rows', split_axis=0, concat_axis=0, tiled=True)]
    pallas_call x1, Pallas kernels: 9.68 us -> 7.99 us  [call_own(): pl.pallas_call(functools.partial(own_kernel, shape), out_shape=jax.ShapeD...]
    all_to_all x1, starting transfers between devices: 17.2 us -> 16.2 us  [shards(): lax.all_to_all(feats, 'tm', split_axis=0, concat_axis=0, axis_index_group...]
  transfers between devices with their start and end apart: 2 -> 4, of which waited for: 1 -> 1; matrix products, arithmetic and copies ran while one was open for 6% -> 7% of each run, Pallas kernels for 11% -> 10%
where the time goes in v3:
time: 81 us; the launch traced here: 80.6 us
  Pallas kernels  24.2 us (30%)
  starting transfers between devices  23.7 us (29%)
  blocking collectives  23.4 us (29%)
  local copies, waits for them, and re-layouts  6.89 us (9%)
  waiting for transfers between devices  2.18 us (3%)
    all_to_all x1, blocking collectives, shards(): lax.all_to_all(messages, 'rows', split_axis=0, concat_axis=0, tiled=True)  23.4 us
    all_to_all x1, starting transfers between devices, shards(): lax.all_to_all(feats, 'tm', split_axis=0, concat_axis=0, axis_index_group...  16.2 us
    pallas_call x1, Pallas kernels, call_join(): pl.pallas_call(functools.partial(join_kernel, shape), out_shape=jax.Shape...  15.2 us
    pallas_call x1, Pallas kernels, call_own(): pl.pallas_call(functools.partial(own_kernel, shape), out_shape=jax.ShapeD...  7.99 us
    ppermute x1, starting transfers between devices, shards(): other = lax.ppermute(got, 'tm', [(i, i ^ 1) for i in range(window)])  3.86 us
    transpose x2, local copies, waits for them, and re-layouts, taps(): turned = jnp.transpose(weight, (1, 3, 0, 2))  3 us
    ppermute x1, starting transfers between devices, shards(): lax.ppermute(col_table, 'rows', up)  2.3 us
    all_to_all x1, waiting for transfers between devices, shards(): lax.all_to_all(feats, 'tm', split_axis=0, concat_axis=0, axis_index_group...  2.17 us
  transfers between devices with their start and end apart: 4, of which 1 were waited for; matrix products, arithmetic and copies ran while one was open for 7% of the time, Pallas kernels for 10%

profile of v3, /device:TPU:1, one launch (start us, length us, event | category | flops | bytes accessed | tf_op | source)
XLA Modules:
  0.0 80.6 jit_solution(1253309380553008174)
XLA Ops:
  0.0 0.0 copy-start.2
  0.0 0.0 copy-start.1
  0.0 1.4 %broadcast_in_dim.11 = bf16[16,16,256]{2,1,0:T(8,128)(2,1)} broadcast(bf16[16,256]{1,0:T(8,128)(2,1)} %bitcast.14), dimensions={1,2} | broadcast | bytes 139264 | tf_op jit(solution)/shard_map/broadcast_in_dim | solution.py:264
  1.4 16.2 %all-to-all-start = ((bf16[16,16,256]{2,1,0:T(8,128)(2,1)}), bf16[16,16,256]{2,1,0:T(8,128)(2,1)S(1)}, u32[]{:S(2)}, u32[]{:S(2)}) async-start(bf16[16,16,256]{2,1,0:T(8,128)(2,1)} %broadcast_in_dim.11), calls=%async_computation | async-start | bytes 262144 | tf_op jit(solution)/shard_map/all_to_all | solution.py:266
  17.6 2.3 %collective-permute-start = (s32[8,128]{1,0:T(8,128)}, s32[8,128]{1,0:T(8,128)S(1)}, u32[]{:S(2)}, u32[]{:S(2)}) collective-permute-start(s32[8,128]{1,0:T(8,128)} %mid.1), channel_id=1, source_target_pairs={{0,1},{1,2},{2,3},{3,4},{4,5},{5,6},{6,7},{7,8},{8,9},{9,10},{10,1... | collective-permute-start | bytes 12296 | tf_op jit(solution)/shard_map/ppermute | solution.py:271
  19.9 1.3 %collective-permute-start.1 = (s32[8,128]{1,0:T(8,128)}, s32[8,128]{1,0:T(8,128)S(1)}, u32[]{:S(2)}, u32[]{:S(2)}) collective-permute-start(s32[8,128]{1,0:T(8,128)} %mid.1), channel_id=1, source_target_pairs={{1,0},{2,1},{3,2},{4,3},{5,4},{6,5},{7,6},{8,7},{9,8},{10,9},{11,1... | collective-permute-start | bytes 12296 | tf_op jit(solution)/shard_map/ppermute | solution.py:273
  21.3 0.8 copy.17
  22.0 0.1 reshape.12
  22.1 0.1 pad_add_fusion.scal
  22.2 0.9 %copy.14 = bf16[256,80]{1,0:T(8,128)(2,1)S(1)} copy(bf16[256,80]{0,1:T(8,128)(2,1)} %param.10) | data formatting | bytes 81920 | tf_op args[2]
  23.1 1.1 %copy.15 = bf16[3,80,3,80]{3,2,1,0:T(4,128)(2,1)S(1)} copy(bf16[3,80,3,80]{1,3,0,2:T(8,128)(2,1)} %bitcast.13) | data formatting | bytes 230400 | tf_op jit(solution)/shard_map/transpose | solution.py:191
  24.2 0.2 reshape.13.w_bev
  24.4 1.9 %copy.16 = bf16[3,160,3,160]{3,2,1,0:T(4,128)(2,1)S(1)} copy(bf16[3,160,3,160]{1,3,0,2:T(8,128)(2,1)} %bitcast.12) | data formatting | bytes 921600 | tf_op jit(solution)/shard_map/transpose | solution.py:191
  26.3 0.6 reshape.14.w_out
  26.9 0.0 collective-permute-done.low
  26.9 0.0 collective-permute-done.1.high
  26.9 2.2 %all-to-all-done.feats = bf16[16,16,256]{2,1,0:T(8,128)(2,1)S(1)} async-done(((bf16[16,16,256]{2,1,0:T(8,128)(2,1)}), bf16[16,16,256]{2,1,0:T(8,128)(2,1)S(1)}, u32[]{:S(2)}, u32[]{:S(2)}) %all-to-all-start) | async-done | bytes 131104 | tf_op jit(solution)/shard_map/all_to_all | solution.py:266
  29.1 0.0 copy-done.1
  29.1 0.0 copy-start
  29.1 1.1 %pack.1 = bf16[16,144,128]{2,1,0:T(8,128)(2,1)S(1)} custom-call(s32[37]{0:T(128)S(1)} %pad_add_fusion.scal, bf16[16,16,256]{2,1,0:T(8,128)(2,1)S(1)} %all-to-all-done.feats, bf16[256,128]{1,0:T(8,128)(2,1)S(1)} %copy-done.1, bf16[256,128]{1,0:T(8,128)(2,1)S(1)} %pad.5.w_ctx), custom_call_target="tpu_custom_call" | custom-call | tf_op jit(solution)/shard_map/pack/pallas_call | solution.py:211
  30.1 23.4 %all_to_all.10.got = bf16[16,144,128]{2,1,0:T(8,128)(2,1)S(1)} all-to-all(bf16[16,144,128]{2,1,0:T(8,128)(2,1)S(1)} %pack.1), channel_id=1, replica_groups=mesh['tm'=32,'rows'=16] {'rows'}, dimensions={0} | all-to-all | bytes 1179648 | tf_op jit(solution)/shard_map/all_to_all | solution.py:288
  53.5 3.9 %collective-permute-start.2 = (bf16[16,144,128]{2,1,0:T(8,128)(2,1)S(1)}, bf16[16,144,128]{2,1,0:T(8,128)(2,1)S(1)}, u32[]{:S(2)}, u32[]{:S(2)}) collective-permute-start(bf16[16,144,128]{2,1,0:T(8,128)(2,1)S(1)} %all_to_all.10.got), channel_id=1, source_target_pairs={{0,16},{16,0},{32,48},{48,32},{64,80},{80,64},{96,112},{112,96},{1... | collective-permute-start | bytes 1769480 | tf_op jit(solution)/shard_map/ppermute | solution.py:289
  57.4 0.0 copy-done.2
  57.4 8.0 %own.1 = bf16[12,720,128]{2,1,0:T(8,128)(2,1)S(1)} custom-call(s32[37]{0:T(128)S(1)} %pad_add_fusion.scal, bf16[16,144,128]{2,1,0:T(8,128)(2,1)S(1)} %all_to_all.10.got, s32[8,128]{1,0:T(8,128)S(1)} %collective-permute-done.low, s32[8,128]{1,0:T(8,128)S(1)} %copy-done.2, s32[8,128]{1,0:T(8,128)S(1)} %collective-permute-done.1.high, ...), custom_call_target="tpu_custom_call" | custom-call | tf_op jit(solution)/shard_map/own/pallas_call | solution.py:224
  65.4 0.0 collective-permute-done.2.other
  65.4 0.0 copy-done
  65.4 15.2 %join.1 = bf16[8,160,128]{2,1,0:T(8,128)(2,1)} custom-call(s32[37]{0:T(128)S(1)} %pad_add_fusion.scal, bf16[16,144,128]{2,1,0:T(8,128)(2,1)S(1)} %collective-permute-done.2.other, s32[8,128]{1,0:T(8,128)S(1)} %collective-permute-done.low, s32[8,128]{1,0:T(8,128)S(1)} %copy-done.2, s32[8,128]{1,0:T(8,128)S(1)} %collective-permute-done.1.high, ...), custom_call_target="tpu_custom_call" | custom-call | tf_op jit(solution)/shard_map/join/pallas_call | solution.py:237
  (2 shorter events, 0.0 us)
Async XLA Ops:
  0.0 57.4 %copy-start.2 = (s32[8,128]{1,0:T(8,128)S(1)}, s32[8,128]{1,0:T(8,128)}, u32[]{:S(2)}) copy-start(s32[8,128]{1,0:T(8,128)} %mid.1) | copy-start | bytes 12292
  0.0 29.1 %copy-start.1 = (bf16[256,128]{1,0:T(8,128)(2,1)S(1)}, bf16[256,128]{1,0:T(8,128)(2,1)}, u32[]{:S(2)}) copy-start(bf16[256,128]{1,0:T(8,128)(2,1)} %w_depth.1) | copy-start | bytes 196612
  1.4 27.7 %all-to-all-start = ((bf16[16,16,256]{2,1,0:T(8,128)(2,1)}), bf16[16,16,256]{2,1,0:T(8,128)(2,1)S(1)}, u32[]{:S(2)}, u32[]{:S(2)}) async-start(bf16[16,16,256]{2,1,0:T(8,128)(2,1)} %broadcast_in_dim.11), calls=%async_computation | async-start | bytes 262144 | tf_op jit(solution)/shard_map/all_to_all | solution.py:266
  17.6 9.2 %collective-permute-start = (s32[8,128]{1,0:T(8,128)}, s32[8,128]{1,0:T(8,128)S(1)}, u32[]{:S(2)}, u32[]{:S(2)}) collective-permute-start(s32[8,128]{1,0:T(8,128)} %mid.1), channel_id=1, source_target_pairs={{0,1},{1,2},{2,3},{3,4},{4,5},{5,6},{6,7},{7,8},{8,9},{9,10},{10,1... | collective-permute-start | bytes 12296 | tf_op jit(solution)/shard_map/ppermute | solution.py:271
  19.9 6.9 %collective-permute-start.1 = (s32[8,128]{1,0:T(8,128)}, s32[8,128]{1,0:T(8,128)S(1)}, u32[]{:S(2)}, u32[]{:S(2)}) collective-permute-start(s32[8,128]{1,0:T(8,128)} %mid.1), channel_id=1, source_target_pairs={{1,0},{2,1},{3,2},{4,3},{5,4},{6,5},{7,6},{8,7},{9,8},{10,9},{11,1... | collective-permute-start | bytes 12296 | tf_op jit(solution)/shard_map/ppermute | solution.py:273
  29.1 36.4 %copy-start = (bf16[3,3,1360,160]{2,3,1,0:T(8,128)(2,1)S(1)}, bf16[3,3,1360,160]{2,3,1,0:T(8,128)(2,1)}, u32[]{:S(2)}) copy-start(bf16[3,3,1360,160]{2,3,1,0:T(8,128)(2,1)} %param.14) | copy-start | bytes 11750404
  53.5 11.9 %collective-permute-start.2 = (bf16[16,144,128]{2,1,0:T(8,128)(2,1)S(1)}, bf16[16,144,128]{2,1,0:T(8,128)(2,1)S(1)}, u32[]{:S(2)}, u32[]{:S(2)}) collective-permute-start(bf16[16,144,128]{2,1,0:T(8,128)(2,1)S(1)} %all_to_all.10.got), channel_id=1, source_target_pairs={{0,16},{16,0},{32,48},{48,32},{64,80},{80,64},{96,112},{112,96},{1... | collective-permute-start | bytes 1769480 | tf_op jit(solution)/shard_map/ppermute | solution.py:289

commit v4 on v3

--- a/solution.py
+++ b/solution.py
@@ -5,6 +5,7 @@
 from jax import lax
 from jax.experimental import pallas as pl
 from jax.experimental.pallas import tpu as pltpu
+from jax.sharding import Mesh
 from jax.sharding import PartitionSpec as P
 
 BF = jnp.bfloat16
@@ -30,37 +31,38 @@
 
 
 def pack_kernel(shape, scal, feats, w_depth, w_ctx, out, stack):
-    blocks, share, columns, chans, rows, total = shape
+    ranks, share, columns, chans, rows, total, cols, wide = shape
     span = rows + 2 * EXTRA
+    far = scal[3]
+    alone = feats.shape[1]
     for slot in range(share):
         source = scal[1] + slot
-        piece = feats[jnp.maximum(source, 0)]
-        stack[slot * columns : (slot + 1) * columns, :] = jnp.where(
-            source >= 0, piece, jnp.zeros_like(piece)
-        )
+        for part in range(columns // alone):
+            piece = feats[jnp.maximum(source, 0) * (columns // alone) + part]
+            at = slot * columns + part * alone
+            stack[at : at + alone, :] = jnp.where(source >= 0, piece, jnp.zeros_like(piece))
     stacked = stack[...]
     depth = jax.nn.sigmoid(jnp.dot(stacked, w_depth[...], preferred_element_type=F32))
     main = depth.astype(BF).astype(F32)
     rest = depth - main
     ctx = jnp.dot(stacked, w_ctx[...], preferred_element_type=F32)
     lane = lax.broadcasted_iota(jnp.int32, ctx.shape, 1)
-    cols = depth.shape[1]
-    for block in range(blocks):
-        first = rows * block - EXTRA
+    for rank in range(ranks):
+        first = rows * (rank // 2 * 4 + rank % 2 + 2 * far) - EXTRA
         message = jnp.where(lane < chans, ctx, 0.0)
         for part, values in enumerate((main, rest)):
             start = chans + part * span
-            turned = pltpu.roll(values, (start - first) % cols, 1)
-            low = max(start, start - first)
-            high = min(start + span, total - first + start)
+            turned = pltpu.roll(values, lax.rem(start - first + total, total), 1)
+            low = jnp.maximum(start, start - first)
+            high = jnp.minimum(start + span, total - first + start)
             message = jnp.where((lane >= low) & (lane < high), turned, message)
-        out[block] = message.astype(BF)
+        out[rank] = message.astype(BF)
 
 
 def lift_and_convolve(shape, scal, got, tables, w_bev, store, ctx, dep, tab, lifted, skip, last, frames):
-    blocks, share, columns, chans, rows, total, cols, wide = shape
+    ranks, share, columns, chans, rows, total, cols, wide = shape
     here = scal[0]
-    count = blocks * columns
+    count = ranks * columns
     span = rows + 2 * EXTRA
 
     for i in range(frames):
@@ -68,14 +70,16 @@
         if not isinstance(at, int):
             at = pl.multiple_of(at, 16)
         piece = got[:, pl.ds(at, columns), :].reshape(count, cols)
-        turned = piece.astype(F32).T
+        turned = piece.T.astype(F32)
         ctx[i * chans : (i + 1) * chans, :] = turned[:chans].astype(BF)
         dep[:, i, :] = turned[chans : chans + span]
         dep[:, 16 + i, :] = turned[chans + span : chans + 2 * span]
     for side in range(3):
         tab[side * rows : (side + 1) * rows, :] = tables[side][...]
 
-    number = lax.broadcasted_iota(jnp.int32, (count, cols), 0)
+    alone = columns // 2
+    place = lax.broadcasted_iota(jnp.int32, (count, cols), 0)
+    number = (place & ~(3 * alone)) | ((place & alone) << 1) | ((place & (2 * alone)) >> 1)
 
     def lift(pair, carry):
         hots = []
@@ -105,17 +109,17 @@
     lane = lax.broadcasted_iota(jnp.int32, (chans, cols), 1)
     need = rows + 4
 
-    def bev(i, carry):
+    def bev(i):
         k = last - 2 * i
-        dy = scal[3 + 2 * k]
-        dx = scal[4 + 2 * k]
+        dy = scal[4 + 2 * k]
+        dx = scal[5 + 2 * k]
         base = dy + REACH
-        at = pl.multiple_of(i * chans, 16)
+        at = i * chans
         inside = (lane + dx >= 0) & (lane + dx < cols)
         turn = jnp.where(dx > 0, cols - dx, -dx)
         for pair in range(need // BEV):
             sides = [
-                lifted[pl.ds(base + BEV * pair + half, 3), pl.ds(at, chans), :].reshape(3 * chans, cols)
+                lifted[pl.ds(base + BEV * pair + half, 3), at : at + chans, :].reshape(3 * chans, cols)
                 for half in range(BEV)
             ]
             acc = jnp.dot(w_bev[...], jnp.concatenate(sides, axis=1), preferred_element_type=F32)
@@ -125,16 +129,16 @@
                 value = pltpu.roll(value, turn, 1)
                 keep = inside & (row >= 0) & (row < total)
                 store(BEV * pair + half, i, jnp.where(keep, value, 0.0).astype(BF))
-        return carry
-
-    lax.fori_loop(0, frames, bev, 0)
+
+    for i in range(frames):
+        bev(i)
 
 
 def own_kernel(shape, scal, got, low, mid, high, w_bev, out, ctx, dep, tab, lifted):
     share, chans = shape[1], shape[3]
 
     def store(j, i, value):
-        out[j, pl.ds(pl.multiple_of(i * chans, 16), chans), :] = value
+        out[j, i * chans : (i + 1) * chans, :] = value
 
     lift_and_convolve(
         shape, scal, got, (low, mid, high), w_bev, store, ctx, dep, tab, lifted, 0, 2 * share - 2, share
@@ -144,12 +148,12 @@
 def join_kernel(
     shape, scal, other, low, mid, high, own, w_bev, w_join, w_out, out, ctx, dep, tab, lifted, moved, hidden
 ):
-    blocks, share, columns, chans, rows, total, cols, wide = shape
+    ranks, share, columns, chans, rows, total, cols, wide = shape
     here = scal[0]
     last = 2 * share - 3
 
     def store(j, i, value):
-        moved[j, pl.ds(pl.multiple_of((last - 2 * i) * chans, 16), chans), :] = value
+        moved[j, (last - 2 * i) * chans : (last - 2 * i + 1) * chans, :] = value
 
     lift_and_convolve(
         shape, scal, other, (low, mid, high), w_bev, store, ctx, dep, tab, lifted, scal[2], last, share - 1
@@ -207,10 +211,10 @@
 
 
 def call_pack(shape, scal, feats, w_depth, w_ctx):
-    blocks, share, columns, chans, rows, total, cols, wide = shape
+    ranks, share, columns, chans, rows, total, cols, wide = shape
     return pl.pallas_call(
-        functools.partial(pack_kernel, shape[:6]),
-        out_shape=jax.ShapeDtypeStruct((blocks, share * columns, cols), BF),
+        functools.partial(pack_kernel, shape),
+        out_shape=jax.ShapeDtypeStruct((ranks, share * columns, cols), BF),
         in_specs=[SMEM, VMEM, VMEM, VMEM],
         out_specs=VMEM,
         scratch_shapes=[pltpu.VMEM((share * columns, feats.shape[2]), BF)],
@@ -220,26 +224,26 @@
 
 
 def call_own(shape, scal, got, tables, w_bev):
-    blocks, share, columns, chans, rows, total, cols, wide = shape
+    ranks, share, columns, chans, rows, total, cols, wide = shape
     return pl.pallas_call(
         functools.partial(own_kernel, shape),
         out_shape=jax.ShapeDtypeStruct((rows + 4, share * chans, cols), BF),
         in_specs=[SMEM] + [VMEM] * 5,
         out_specs=VMEM,
-        scratch_shapes=scratch(share, chans, blocks * columns, rows, cols),
+        scratch_shapes=scratch(share, chans, ranks * columns, rows, cols),
         compiler_params=pltpu.CompilerParams(vmem_limit_bytes=24 * 1024 * 1024),
         name="own",
     )(scal, got, *tables, w_bev)
 
 
 def call_join(shape, scal, other, tables, own, w_bev, w_join, w_out):
-    blocks, share, columns, chans, rows, total, cols, wide = shape
+    ranks, share, columns, chans, rows, total, cols, wide = shape
     return pl.pallas_call(
         functools.partial(join_kernel, shape),
         out_shape=jax.ShapeDtypeStruct((rows, wide, cols), BF),
         in_specs=[SMEM] + [VMEM] * 8,
         out_specs=VMEM,
-        scratch_shapes=scratch(share - 1, chans, blocks * columns, rows, cols)
+        scratch_shapes=scratch(share - 1, chans, ranks * columns, rows, cols)
         + [
             pltpu.VMEM((rows + 4, (2 * share - 1) * chans, cols), BF),
             pltpu.VMEM((rows + 2, wide, cols), BF),
@@ -254,39 +258,42 @@
     frames = offsets.shape[1] + 1
     chans = w_ctx.shape[1]
     wide = w_out.shape[3]
-    columns, depth_k = col_feat.shape[1:]
-    blocks = lax.axis_size("rows")
-    window = lax.axis_size("tm")
+    alone, depth_k = col_feat.shape[1:]
+    ranks = lax.axis_size("x") * lax.axis_size("near")
+    chips = lax.axis_size("chip")
     total = w_depth.shape[1]
     share = (frames + 1) // 2
-    shape = (blocks, share, columns, chans, rows, total, cols, wide)
-
-    feats = jnp.broadcast_to(col_feat, (window // 2, columns, depth_k))
-    groups = [list(range(core, window, 2)) for core in range(2)]
-    feats = lax.all_to_all(
-        feats, "tm", split_axis=0, concat_axis=0, axis_index_groups=groups, tiled=True
-    )
-    up = [(i, i + 1) for i in range(blocks - 1)]
+    columns = 2 * alone
+    shape = (ranks, share, columns, chans, rows, total, cols, wide)
+    line = ("x", "far", "near")
+
+    feats = jnp.broadcast_to(col_feat, (chips * 2, alone, depth_k))
+    feats = lax.all_to_all(feats, ("chip", "far"), split_axis=0, concat_axis=0, tiled=True)
+    up = [(i, i + 1) for i in range(2 * ranks - 1)]
     tables = (
-        lax.ppermute(col_table, "rows", up),
+        lax.ppermute(col_table, line, up),
         col_table,
-        lax.ppermute(col_table, "rows", [(t, s) for s, t in up]),
+        lax.ppermute(col_table, line, [(t, s) for s, t in up]),
     )
     w_ctx = jnp.pad(w_ctx, ((0, 0), (0, cols - chans)))
     feats, tables, w_ctx, w_bev, w_out = lax.optimization_barrier(
         (feats, tables, w_ctx, taps(w_bev), taps(w_out))
     )
 
-    frame = lax.axis_index("tm").astype(jnp.int32)
     head = jnp.stack(
-        [lax.axis_index("rows").astype(jnp.int32), (frame >> 1) - (share - 1), frame & 1]
+        [
+            lax.axis_index(line).astype(jnp.int32),
+            lax.axis_index("chip").astype(jnp.int32) - (share - 1),
+            lax.axis_index("core").astype(jnp.int32),
+            lax.axis_index("far").astype(jnp.int32),
+        ]
     )
     moves = jnp.concatenate([jnp.zeros((1, 2), jnp.int32), offsets[0]], axis=0)
     scal = jnp.concatenate([head, moves.reshape(-1)])
 
     messages = call_pack(shape, scal, feats, w_depth, w_ctx)
-    got = lax.all_to_all(messages, "rows", split_axis=0, concat_axis=0, tiled=True)
-    other = lax.ppermute(got, "tm", [(i, i ^ 1) for i in range(window)])
+    got = lax.all_to_all(messages, ("x", "near"), split_axis=0, concat_axis=0, tiled=True)
+    other = lax.ppermute(got, "core", [(0, 1), (1, 0)])
 
     w_join = jnp.transpose(w_join, (0, 1, 3, 2)).reshape(3, 3 * wide, frames * chans)
     own = call_own(shape, scal, got, tables, w_bev)
@@ -295,15 +302,20 @@
 
 
 def solution(mesh):
+    split = Mesh(
+        mesh.devices.reshape(mesh.shape["tm"] // 2, 2, mesh.shape["rows"] // 4, 2, 2),
+        ("chip", "core", "x", "far", "near"),
+    )
+    tm, rows = ("chip", "core"), ("x", "far", "near")
     in_specs = (
-        P("tm", "rows", None),
-        P(),
-        P(),
-        P("rows", None),
-        P(),
-        P("tm", None, None),
-        P(),
-        P(),
-    )
-    out_specs = P("tm", "rows", None, None)
-    return jax.shard_map(shards, mesh=mesh, in_specs=in_specs, out_specs=out_specs, check_vma=False)
+        P(tm, rows, None),
+        P(),
+        P(),
+        P(rows, None),
+        P(),
+        P(tm, None, None),
+        P(),
+        P(),
+    )
+    out_specs = P(tm, rows, None, None)
+    return jax.shard_map(shards, mesh=split, in_specs=in_specs, out_specs=out_specs, check_vma=False)

time: 81 us -> 70.6 us (0.87)
  blocking collectives: 23.4 us -> 12 us
  Pallas kernels: 24.2 us -> 20.3 us
  starting transfers between devices: 23.7 us -> 26.3 us
  waiting for transfers between devices: 2.18 us -> 4.43 us
    all_to_all x1, blocking collectives: 23.4 us -> 12 us  [shards(): lax.all_to_all(messages, ('x', 'near'), split_axis=0, concat_axis=0, tile...]
    ppermute x3, starting transfers between devices: 7.46 us -> 9.78 us  [the longest x1 6.18 us: shards(): other = lax.ppermute(got, 'core', [(0, 1), (1, 0)])]
    all_to_all x1, waiting for transfers between devices: 2.17 us -> 4.43 us  [shards(): lax.all_to_all(feats, ('chip', 'far'), split_axis=0, concat_axis=0, tiled...]
    pallas_call x1, Pallas kernels: 7.99 us -> 5.92 us  [call_own(): pl.pallas_call(functools.partial(own_kernel, shape), out_shape=jax.ShapeD...]
    pallas_call x1, Pallas kernels: 15.2 us -> 13.3 us  [call_join(): pl.pallas_call(functools.partial(join_kernel, shape), out_shape=jax.Shape...]
  transfers between devices with their start and end apart: 4 -> 4, of which waited for: 1 -> 1; matrix products, arithmetic and copies ran while one was open for 7% -> 8% of each run, Pallas kernels for 10% -> 8%
where the time goes in v4:
time: 70.6 us; the launch traced here: 70.2 us
  starting transfers between devices  26.3 us (37%)
  Pallas kernels  20.3 us (29%)
  blocking collectives  12 us (17%)
  local copies, waits for them, and re-layouts  7.03 us (10%)
  waiting for transfers between devices  4.43 us (6%)
    all_to_all x1, starting transfers between devices, shards(): lax.all_to_all(feats, ('chip', 'far'), split_axis=0, concat_axis=0, tiled...  16.5 us
    pallas_call x1, Pallas kernels, call_join(): pl.pallas_call(functools.partial(join_kernel, shape), out_shape=jax.Shape...  13.3 us
    all_to_all x1, blocking collectives, shards(): lax.all_to_all(messages, ('x', 'near'), split_axis=0, concat_axis=0, tile...  12 us
    ppermute x1, starting transfers between devices, shards(): other = lax.ppermute(got, 'core', [(0, 1), (1, 0)])  6.18 us
    pallas_call x1, Pallas kernels, call_own(): pl.pallas_call(functools.partial(own_kernel, shape), out_shape=jax.ShapeD...  5.92 us
    all_to_all x1, waiting for transfers between devices, shards(): lax.all_to_all(feats, ('chip', 'far'), split_axis=0, concat_axis=0, tiled...  4.43 us
    transpose x2, local copies, waits for them, and re-layouts, taps(): turned = jnp.transpose(weight, (1, 3, 0, 2))  3 us
    ppermute x1, starting transfers between devices, shards(): lax.ppermute(col_table, line, up)  2.3 us
  transfers between devices with their start and end apart: 4, of which 1 were waited for; matrix products, arithmetic and copies ran while one was open for 8% of the time, Pallas kernels for 8%

profile of v4, /device:TPU:1, one launch (start us, length us, event | category | flops | bytes accessed | tf_op | source)
XLA Modules:
  0.0 70.2 jit_solution(13098696093407969857)
XLA Ops:
  0.0 0.0 copy-start.2
  0.0 0.0 copy-start.1
  0.0 1.4 %broadcast_in_dim.11 = bf16[32,16,256]{2,1,0:T(8,128)(2,1)} broadcast(bf16[16,256]{1,0:T(8,128)(2,1)} %bitcast.15), dimensions={1,2} | broadcast | bytes 270336 | tf_op jit(solution)/shard_map/broadcast_in_dim | solution.py:270
  1.5 16.5 %all-to-all-start = ((bf16[32,16,256]{2,1,0:T(8,128)(2,1)}), bf16[32,16,256]{2,1,0:T(8,128)(2,1)S(1)}, u32[]{:S(2)}, u32[]{:S(2)}) async-start(bf16[32,16,256]{2,1,0:T(8,128)(2,1)} %broadcast_in_dim.11), calls=%async_computation | async-start | bytes 524288 | tf_op jit(solution)/shard_map/all_to_all | solution.py:271
  18.0 2.3 %collective-permute-start = (s32[8,128]{1,0:T(8,128)}, s32[8,128]{1,0:T(8,128)S(1)}, u32[]{:S(2)}, u32[]{:S(2)}) collective-permute-start(s32[8,128]{1,0:T(8,128)} %mid.1), channel_id=1, source_target_pairs={{0,1},{1,2},{2,3},{3,4},{4,5},{5,6},{6,7},{7,8},{8,9},{9,10},{10,1... | collective-permute-start | bytes 12296 | tf_op jit(solution)/shard_map/ppermute | solution.py:274
  20.3 1.3 %collective-permute-start.1 = (s32[8,128]{1,0:T(8,128)}, s32[8,128]{1,0:T(8,128)S(1)}, u32[]{:S(2)}, u32[]{:S(2)}) collective-permute-start(s32[8,128]{1,0:T(8,128)} %mid.1), channel_id=1, source_target_pairs={{1,0},{2,1},{3,2},{4,3},{5,4},{6,5},{7,6},{8,7},{9,8},{10,9},{11,1... | collective-permute-start | bytes 12296 | tf_op jit(solution)/shard_map/ppermute | solution.py:276
  21.6 0.8 %copy.17 = s32[16,2]{1,0:T(8,128)S(1)} copy(s32[16,2]{0,1:T(2,128)} %bitcast.16) | data formatting | bytes 256
  22.4 0.1 reshape.12
  22.5 0.9 %copy.14 = bf16[256,80]{1,0:T(8,128)(2,1)S(1)} copy(bf16[256,80]{0,1:T(8,128)(2,1)} %param.10) | data formatting | bytes 81920 | tf_op args[2]
  23.4 1.1 %copy.15 = bf16[3,80,3,80]{3,2,1,0:T(4,128)(2,1)S(1)} copy(bf16[3,80,3,80]{1,3,0,2:T(8,128)(2,1)} %bitcast.14) | data formatting | bytes 230400 | tf_op jit(solution)/shard_map/transpose | solution.py:195
  24.5 0.2 reshape.13.w_bev
  24.6 1.9 %copy.16 = bf16[3,160,3,160]{3,2,1,0:T(4,128)(2,1)S(1)} copy(bf16[3,160,3,160]{1,3,0,2:T(8,128)(2,1)} %bitcast.13) | data formatting | bytes 921600 | tf_op jit(solution)/shard_map/transpose | solution.py:195
  26.5 0.6 reshape.14.w_out
  27.1 0.1 concatenate.7.scal
  27.2 0.0 collective-permute-done.low
  27.2 0.0 collective-permute-done.1.high
  27.2 4.4 %all-to-all-done.feats = bf16[32,16,256]{2,1,0:T(8,128)(2,1)S(1)} async-done(((bf16[32,16,256]{2,1,0:T(8,128)(2,1)}), bf16[32,16,256]{2,1,0:T(8,128)(2,1)S(1)}, u32[]{:S(2)}, u32[]{:S(2)}) %all-to-all-start) | async-done | bytes 262176 | tf_op jit(solution)/shard_map/all_to_all | solution.py:271
  31.7 0.0 copy-done.1
  31.7 0.0 copy-start
  31.7 1.1 %pack.1 = bf16[8,288,128]{2,1,0:T(8,128)(2,1)S(1)} custom-call(s32[38]{0:T(128)S(1)} %concatenate.7.scal, bf16[32,16,256]{2,1,0:T(8,128)(2,1)S(1)} %all-to-all-done.feats, bf16[256,128]{1,0:T(8,128)(2,1)S(1)} %copy-done.1, bf16[256,128]{1,0:T(8,128)(2,1)S(1)} %pad.5.w_ctx), custom_call_target="tpu_custom_call" | custom-call | tf_op jit(solution)/shard_map/pack/pallas_call | solution.py:215
  32.8 12.0 %all_to_all.10.got = bf16[8,288,128]{2,1,0:T(8,128)(2,1)S(1)} all-to-all(bf16[8,288,128]{2,1,0:T(8,128)(2,1)S(1)} %pack.1), channel_id=1, replica_groups=mesh['chip'=16,'core'=2,'x'=4,'far'=2,'near'=2] {'x','near'}, dimensions={0} | all-to-all | bytes 1179648 | tf_op jit(solution)/shard_map/all_to_all | solution.py:295
  44.7 6.2 %collective-permute-start.2 = (bf16[8,288,128]{2,1,0:T(8,128)(2,1)S(1)}, bf16[8,288,128]{2,1,0:T(8,128)(2,1)S(1)}, u32[]{:S(2)}, u32[]{:S(2)}) collective-permute-start(bf16[8,288,128]{2,1,0:T(8,128)(2,1)S(1)} %all_to_all.10.got), channel_id=1, source_target_pairs={{0,16},{16,0},{1,17},{17,1},{2,18},{18,2},{3,19},{19,3},{4,20},{20... | collective-permute-start | bytes 1769480 | tf_op jit(solution)/shard_map/ppermute | solution.py:296
  50.9 0.0 copy-done.2
  50.9 5.9 %own.1 = bf16[12,720,128]{2,1,0:T(8,128)(2,1)S(1)} custom-call(s32[38]{0:T(128)S(1)} %concatenate.7.scal, bf16[8,288,128]{2,1,0:T(8,128)(2,1)S(1)} %all_to_all.10.got, s32[8,128]{1,0:T(8,128)S(1)} %collective-permute-done.low, s32[8,128]{1,0:T(8,128)S(1)} %copy-done.2, s32[8,128]{1,0:T(8,128)S(1)} %collective-permute-done.1.high, ...), custom_call_target="tpu_custom_call" | custom-call | tf_op jit(solution)/shard_map/own/pallas_call | solution.py:228
  56.9 0.0 collective-permute-done.2.other
  56.9 0.0 copy-done
  56.9 13.3 %join.1 = bf16[8,160,128]{2,1,0:T(8,128)(2,1)} custom-call(s32[38]{0:T(128)S(1)} %concatenate.7.scal, bf16[8,288,128]{2,1,0:T(8,128)(2,1)S(1)} %collective-permute-done.2.other, s32[8,128]{1,0:T(8,128)S(1)} %collective-permute-done.low, s32[8,128]{1,0:T(8,128)S(1)} %copy-done.2, s32[8,128]{1,0:T(8,128)S(1)} %collective-permute-done.1.high, ...), custom_call_target="tpu_custom_call" | custom-call | tf_op jit(solution)/shard_map/join/pallas_call | solution.py:241
  (2 shorter events, 0.0 us)
Async XLA Ops:
  0.0 50.9 %copy-start.2 = (s32[8,128]{1,0:T(8,128)S(1)}, s32[8,128]{1,0:T(8,128)}, u32[]{:S(2)}) copy-start(s32[8,128]{1,0:T(8,128)} %mid.1) | copy-start | bytes 12292
  0.0 31.7 %copy-start.1 = (bf16[256,128]{1,0:T(8,128)(2,1)S(1)}, bf16[256,128]{1,0:T(8,128)(2,1)}, u32[]{:S(2)}) copy-start(bf16[256,128]{1,0:T(8,128)(2,1)} %w_depth.1) | copy-start | bytes 196612
  1.5 30.2 %all-to-all-start = ((bf16[32,16,256]{2,1,0:T(8,128)(2,1)}), bf16[32,16,256]{2,1,0:T(8,128)(2,1)S(1)}, u32[]{:S(2)}, u32[]{:S(2)}) async-start(bf16[32,16,256]{2,1,0:T(8,128)(2,1)} %broadcast_in_dim.11), calls=%async_computation | async-start | bytes 524288 | tf_op jit(solution)/shard_map/all_to_all | solution.py:271
  18.0 9.3 %collective-permute-start = (s32[8,128]{1,0:T(8,128)}, s32[8,128]{1,0:T(8,128)S(1)}, u32[]{:S(2)}, u32[]{:S(2)}) collective-permute-start(s32[8,128]{1,0:T(8,128)} %mid.1), channel_id=1, source_target_pairs={{0,1},{1,2},{2,3},{3,4},{4,5},{5,6},{6,7},{7,8},{8,9},{9,10},{10,1... | collective-permute-start | bytes 12296 | tf_op jit(solution)/shard_map/ppermute | solution.py:274
  20.3 7.0 %collective-permute-start.1 = (s32[8,128]{1,0:T(8,128)}, s32[8,128]{1,0:T(8,128)S(1)}, u32[]{:S(2)}, u32[]{:S(2)}) collective-permute-start(s32[8,128]{1,0:T(8,128)} %mid.1), channel_id=1, source_target_pairs={{1,0},{2,1},{3,2},{4,3},{5,4},{6,5},{7,6},{8,7},{9,8},{10,9},{11,1... | collective-permute-start | bytes 12296 | tf_op jit(solution)/shard_map/ppermute | solution.py:276
  31.7 25.2 %copy-start = (bf16[3,3,1360,160]{2,3,1,0:T(8,128)(2,1)S(1)}, bf16[3,3,1360,160]{2,3,1,0:T(8,128)(2,1)}, u32[]{:S(2)}) copy-start(bf16[3,3,1360,160]{2,3,1,0:T(8,128)(2,1)} %param.14) | copy-start | bytes 11750404
  44.7 12.1 %collective-permute-start.2 = (bf16[8,288,128]{2,1,0:T(8,128)(2,1)S(1)}, bf16[8,288,128]{2,1,0:T(8,128)(2,1)S(1)}, u32[]{:S(2)}, u32[]{:S(2)}) collective-permute-start(bf16[8,288,128]{2,1,0:T(8,128)(2,1)S(1)} %all_to_all.10.got), channel_id=1, source_target_pairs={{0,16},{16,0},{1,17},{17,1},{2,18},{18,2},{3,19},{19,3},{4,20},{20... | collective-permute-start | bytes 1769480 | tf_op jit(solution)/shard_map/ppermute | solution.py:296

commit v5 on v4

--- a/solution.py
+++ b/solution.py
@@ -20,7 +20,7 @@
 
 
 def silu(v):
-    return v / (1.0 + jnp.exp(-v))
+    return (0.5 * v) * (1.0 + jnp.tanh(0.5 * v))
 
 
 def spread(acc, lane, chans):
@@ -146,11 +146,13 @@
 
 
 def join_kernel(
-    shape, scal, other, low, mid, high, own, w_bev, w_join, w_out, out, ctx, dep, tab, lifted, moved, hidden
+    shape, scal, other, low, mid, high, own, w_bev, far_join, w_out, out, ctx, dep, tab, lifted, moved, hidden, w_join, sem
 ):
     ranks, share, columns, chans, rows, total, cols, wide = shape
     here = scal[0]
     last = 2 * share - 3
+    fetch = pltpu.make_async_copy(far_join, w_join, sem)
+    fetch.start()
 
     def store(j, i, value):
         moved[j, (last - 2 * i) * chans : (last - 2 * i + 1) * chans, :] = value
@@ -163,6 +165,7 @@
         for j in range(rows + 4):
             moved[j, at : at + chans, :] = own[j, i * chans : (i + 1) * chans, :]
 
+    fetch.wait()
     lane_wide = lax.broadcasted_iota(jnp.int32, (wide, cols), 1)
 
     def join(pair, carry):
@@ -241,14 +244,16 @@
     return pl.pallas_call(
         functools.partial(join_kernel, shape),
         out_shape=jax.ShapeDtypeStruct((rows, wide, cols), BF),
-        in_specs=[SMEM] + [VMEM] * 8,
+        in_specs=[SMEM] + [VMEM] * 6 + [pl.BlockSpec(memory_space=pltpu.HBM), VMEM],
         out_specs=VMEM,
         scratch_shapes=scratch(share - 1, chans, ranks * columns, rows, cols)
         + [
             pltpu.VMEM((rows + 4, (2 * share - 1) * chans, cols), BF),
             pltpu.VMEM((rows + 2, wide, cols), BF),
+            pltpu.VMEM(w_join.shape, BF),
+            pltpu.SemaphoreType.DMA,
         ],
-        compiler_params=pltpu.CompilerParams(vmem_limit_bytes=36 * 1024 * 1024),
+        compiler_params=pltpu.CompilerParams(vmem_limit_bytes=50 * 1024 * 1024),
         name="join",
     )(scal, other, *tables, own, w_bev, w_join, w_out)
 
@@ -269,16 +274,8 @@
 
     feats = jnp.broadcast_to(col_feat, (chips * 2, alone, depth_k))
     feats = lax.all_to_all(feats, ("chip", "far"), split_axis=0, concat_axis=0, tiled=True)
-    up = [(i, i + 1) for i in range(2 * ranks - 1)]
-    tables = (
-        lax.ppermute(col_table, line, up),
-        col_table,
-        lax.ppermute(col_table, line, [(t, s) for s, t in up]),
-    )
     w_ctx = jnp.pad(w_ctx, ((0, 0), (0, cols - chans)))
-    feats, tables, w_ctx, w_bev, w_out = lax.optimization_barrier(
-        (feats, tables, w_ctx, taps(w_bev), taps(w_out))
-    )
+    feats, w_ctx, w_bev, w_out = lax.optimization_barrier((feats, w_ctx, taps(w_bev), taps(w_out)))
 
     head = jnp.stack(
         [
@@ -292,7 +289,15 @@
     scal = jnp.concatenate([head, moves.reshape(-1)])
 
     messages = call_pack(shape, scal, feats, w_depth, w_ctx)
+    messages, col_table = lax.optimization_barrier((messages, col_table))
     got = lax.all_to_all(messages, ("x", "near"), split_axis=0, concat_axis=0, tiled=True)
+    up = [(i, i + 1) for i in range(2 * ranks - 1)]
+    tables = (
+        lax.ppermute(col_table, line, up),
+        col_table,
+        lax.ppermute(col_table, line, [(t, s) for s, t in up]),
+    )
+    got, tables = lax.optimization_barrier((got, tables))
     other = lax.ppermute(got, "core", [(0, 1), (1, 0)])
 
     w_join = jnp.transpose(w_join, (0, 1, 3, 2)).reshape(3, 3 * wide, frames * chans)

time: 70.6 us -> 76.5 us (1.084)
  the two profiles are of different devices: /device:TPU:1 before, /device:TPU:7 now
where the time goes in v5:
time: 76.5 us; the launch traced here: 76 us
  starting transfers between devices  32.4 us (42%)
  Pallas kernels  23 us (30%)
  waiting for transfers between devices  13.2 us (17%)
  local copies, waits for them, and re-layouts  7.03 us (9%)
    all_to_all x1, starting transfers between devices, shards(): lax.all_to_all(feats, ('chip', 'far'), split_axis=0, concat_axis=0, tiled...  15.7 us
    pallas_call x1, Pallas kernels, call_join(): pl.pallas_call(functools.partial(join_kernel, shape), out_shape=jax.Shape...  15.3 us
    all_to_all x1, waiting for transfers between devices, shards(): lax.all_to_all(feats, ('chip', 'far'), split_axis=0, concat_axis=0, tiled...  8.07 us
    ppermute x1, starting transfers between devices, shards(): other = lax.ppermute(got, 'core', [(0, 1), (1, 0)])  5.81 us
    pallas_call x1, Pallas kernels, call_own(): pl.pallas_call(functools.partial(own_kernel, shape), out_shape=jax.ShapeD...  5.8 us
    ppermute x1, waiting for transfers between devices, shards(): lax.ppermute(col_table, line, up)  5.11 us
    ppermute x1, starting transfers between devices, shards(): lax.ppermute(col_table, line, [(t, s) for s, t in up])  4.78 us
    all_to_all x1, starting transfers between devices, shards(): lax.all_to_all(messages, ('x', 'near'), split_axis=0, concat_axis=0, tile...  4.22 us
  transfers between devices with their start and end apart: 5, of which 2 were waited for; matrix products, arithmetic and copies ran while one was open for 7% of the time, Pallas kernels for 8%

profile of v5, /device:TPU:7, one launch (start us, length us, event | category | flops | bytes accessed | tf_op | source)
XLA Modules:
  0.0 76.0 jit_solution(11112246314519883317)
XLA Ops:
  0.0 0.0 copy-start
  0.0 0.0 copy-start.1
  0.0 1.4 %broadcast_in_dim.11 = bf16[32,16,256]{2,1,0:T(8,128)(2,1)} broadcast(bf16[16,256]{1,0:T(8,128)(2,1)} %bitcast.15), dimensions={1,2} | broadcast | bytes 270336 | tf_op jit(solution)/shard_map/broadcast_in_dim | solution.py:275
  1.5 15.7 %all-to-all-start = ((bf16[32,16,256]{2,1,0:T(8,128)(2,1)}), bf16[32,16,256]{2,1,0:T(8,128)(2,1)S(1)}, u32[]{:S(2)}, u32[]{:S(2)}) async-start(bf16[32,16,256]{2,1,0:T(8,128)(2,1)} %broadcast_in_dim.11), calls=%async_computation | async-start | bytes 524288 | tf_op jit(solution)/shard_map/all_to_all | solution.py:276
  17.2 0.8 copy.17
  17.9 0.1 reshape.12
  18.0 0.9 %copy.14 = bf16[256,80]{1,0:T(8,128)(2,1)S(1)} copy(bf16[256,80]{0,1:T(8,128)(2,1)} %param.10) | data formatting | bytes 81920 | tf_op args[2]
  18.9 1.1 %copy.15 = bf16[3,80,3,80]{3,2,1,0:T(4,128)(2,1)S(1)} copy(bf16[3,80,3,80]{1,3,0,2:T(8,128)(2,1)} %bitcast.14) | data formatting | bytes 230400 | tf_op jit(solution)/shard_map/transpose | solution.py:198
  20.0 0.2 reshape.13.w_bev
  20.2 1.9 %copy.16 = bf16[3,160,3,160]{3,2,1,0:T(4,128)(2,1)S(1)} copy(bf16[3,160,3,160]{1,3,0,2:T(8,128)(2,1)} %bitcast.13) | data formatting | bytes 921600 | tf_op jit(solution)/shard_map/transpose | solution.py:198
  22.1 0.6 reshape.14.w_out
  22.7 0.1 concatenate.7.scal
  22.8 8.1 %all-to-all-done.feats = bf16[32,16,256]{2,1,0:T(8,128)(2,1)S(1)} async-done(((bf16[32,16,256]{2,1,0:T(8,128)(2,1)}), bf16[32,16,256]{2,1,0:T(8,128)(2,1)S(1)}, u32[]{:S(2)}, u32[]{:S(2)}) %all-to-all-start) | async-done | bytes 262176 | tf_op jit(solution)/shard_map/all_to_all | solution.py:276
  30.9 0.0 copy-done
  30.9 1.9 %pack.1 = bf16[8,288,128]{2,1,0:T(8,128)(2,1)} custom-call(s32[38]{0:T(128)S(1)} %concatenate.7.scal, bf16[32,16,256]{2,1,0:T(8,128)(2,1)S(1)} %all-to-all-done.feats, bf16[256,128]{1,0:T(8,128)(2,1)S(1)} %copy-done, bf16[256,128]{1,0:T(8,128)(2,1)S(1)} %pad.5.w_ctx), custom_call_target="tpu_custom_call" | custom-call | tf_op jit(solution)/shard_map/pack/pallas_call | solution.py:218
  32.8 4.2 %all-to-all-start.1 = ((bf16[8,288,128]{2,1,0:T(8,128)(2,1)}), bf16[8,288,128]{2,1,0:T(8,128)(2,1)S(1)}, u32[]{:S(2)}, u32[]{:S(2)}) async-start(bf16[8,288,128]{2,1,0:T(8,128)(2,1)} %pack.1), calls=%async_computation.1 | async-start | bytes 1179648 | tf_op jit(solution)/shard_map/all_to_all | solution.py:293
  37.0 0.0 copy-done.1
  37.0 4.8 %collective-permute-start.1 = (s32[8,128]{1,0:T(8,128)S(1)}, s32[8,128]{1,0:T(8,128)S(1)}, u32[]{:S(2)}, u32[]{:S(2)}) collective-permute-start(s32[8,128]{1,0:T(8,128)S(1)} %copy-done.1), channel_id=1, source_target_pairs={{1,0},{2,1},{3,2},{4,3},{5,4},{6,5},{7,6},{8,7},{9,8},{10,9},{11,1... | collective-permute-start | bytes 12296 | tf_op jit(solution)/shard_map/ppermute | solution.py:298
  41.8 1.9 %collective-permute-start = (s32[8,128]{1,0:T(8,128)S(1)}, s32[8,128]{1,0:T(8,128)S(1)}, u32[]{:S(2)}, u32[]{:S(2)}) collective-permute-start(s32[8,128]{1,0:T(8,128)S(1)} %copy-done.1), channel_id=1, source_target_pairs={{0,1},{1,2},{2,3},{3,4},{4,5},{5,6},{6,7},{7,8},{8,9},{9,10},{10,1... | collective-permute-start | bytes 12296 | tf_op jit(solution)/shard_map/ppermute | solution.py:296
  43.7 0.0 collective-permute-done.1.high
  43.7 5.1 %collective-permute-done.low = s32[8,128]{1,0:T(8,128)S(1)} collective-permute-done((s32[8,128]{1,0:T(8,128)S(1)}, s32[8,128]{1,0:T(8,128)S(1)}, u32[]{:S(2)}, u32[]{:S(2)}) %collective-permute-start) | collective-permute-done | bytes 4128 | tf_op jit(solution)/shard_map/ppermute | solution.py:296
  48.8 0.0 all-to-all-done.1.got
  48.8 5.8 %collective-permute-start.2 = (bf16[8,288,128]{2,1,0:T(8,128)(2,1)S(1)}, bf16[8,288,128]{2,1,0:T(8,128)(2,1)S(1)}, u32[]{:S(2)}, u32[]{:S(2)}) collective-permute-start(bf16[8,288,128]{2,1,0:T(8,128)(2,1)S(1)} %all-to-all-done.1.got), channel_id=1, source_target_pairs={{0,16},{16,0},{1,17},{17,1},{2,18},{18,2},{3,19},{19,3},{4,20},{20... | collective-permute-start | bytes 1769480 | tf_op jit(solution)/shard_map/ppermute | solution.py:301
  54.7 5.8 %own.1 = bf16[12,720,128]{2,1,0:T(8,128)(2,1)S(1)} custom-call(s32[38]{0:T(128)S(1)} %concatenate.7.scal, bf16[8,288,128]{2,1,0:T(8,128)(2,1)S(1)} %all-to-all-done.1.got, s32[8,128]{1,0:T(8,128)S(1)} %collective-permute-done.low, s32[8,128]{1,0:T(8,128)S(1)} %copy-done.1, s32[8,128]{1,0:T(8,128)S(1)} %collective-permute-done.1.high, ...), custom_call_target="tpu_custom_call" | custom-call | tf_op jit(solution)/shard_map/own/pallas_call | solution.py:231
  60.5 0.0 collective-permute-done.2.other
  60.5 15.3 %join.1 = bf16[8,160,128]{2,1,0:T(8,128)(2,1)} custom-call(s32[38]{0:T(128)S(1)} %concatenate.7.scal, bf16[8,288,128]{2,1,0:T(8,128)(2,1)S(1)} %collective-permute-done.2.other, s32[8,128]{1,0:T(8,128)S(1)} %collective-permute-done.low, s32[8,128]{1,0:T(8,128)S(1)} %copy-done.1, s32[8,128]{1,0:T(8,128)S(1)} %collective-permute-done.1.high, ...), custom_call_target="tpu_custom_call" | custom-call | tf_op jit(solution)/shard_map/join/pallas_call | solution.py:244
  (2 shorter events, 0.0 us)
Async XLA Ops:
  0.0 30.9 %copy-start = (bf16[256,128]{1,0:T(8,128)(2,1)S(1)}, bf16[256,128]{1,0:T(8,128)(2,1)}, u32[]{:S(2)}) copy-start(bf16[256,128]{1,0:T(8,128)(2,1)} %w_depth.1) | copy-start | bytes 196612
  0.0 37.0 %copy-start.1 = (s32[8,128]{1,0:T(8,128)S(1)}, s32[8,128]{1,0:T(8,128)}, u32[]{:S(2)}) copy-start(s32[8,128]{1,0:T(8,128)} %mid.1) | copy-start | bytes 12292
  1.5 29.4 %all-to-all-start = ((bf16[32,16,256]{2,1,0:T(8,128)(2,1)}), bf16[32,16,256]{2,1,0:T(8,128)(2,1)S(1)}, u32[]{:S(2)}, u32[]{:S(2)}) async-start(bf16[32,16,256]{2,1,0:T(8,128)(2,1)} %broadcast_in_dim.11), calls=%async_computation | async-start | bytes 524288 | tf_op jit(solution)/shard_map/all_to_all | solution.py:276
  32.8 16.1 %all-to-all-start.1 = ((bf16[8,288,128]{2,1,0:T(8,128)(2,1)}), bf16[8,288,128]{2,1,0:T(8,128)(2,1)S(1)}, u32[]{:S(2)}, u32[]{:S(2)}) async-start(bf16[8,288,128]{2,1,0:T(8,128)(2,1)} %pack.1), calls=%async_computation.1 | async-start | bytes 1179648 | tf_op jit(solution)/shard_map/all_to_all | solution.py:293
  37.0 6.7 %collective-permute-start.1 = (s32[8,128]{1,0:T(8,128)S(1)}, s32[8,128]{1,0:T(8,128)S(1)}, u32[]{:S(2)}, u32[]{:S(2)}) collective-permute-start(s32[8,128]{1,0:T(8,128)S(1)} %copy-done.1), channel_id=1, source_target_pairs={{1,0},{2,1},{3,2},{4,3},{5,4},{6,5},{7,6},{8,7},{9,8},{10,9},{11,1... | collective-permute-start | bytes 12296 | tf_op jit(solution)/shard_map/ppermute | solution.py:298
  41.8 7.0 %collective-permute-start = (s32[8,128]{1,0:T(8,128)S(1)}, s32[8,128]{1,0:T(8,128)S(1)}, u32[]{:S(2)}, u32[]{:S(2)}) collective-permute-start(s32[8,128]{1,0:T(8,128)S(1)} %copy-done.1), channel_id=1, source_target_pairs={{0,1},{1,2},{2,3},{3,4},{4,5},{5,6},{6,7},{7,8},{8,9},{9,10},{10,1... | collective-permute-start | bytes 12296 | tf_op jit(solution)/shard_map/ppermute | solution.py:296
  48.8 11.6 %collective-permute-start.2 = (bf16[8,288,128]{2,1,0:T(8,128)(2,1)S(1)}, bf16[8,288,128]{2,1,0:T(8,128)(2,1)S(1)}, u32[]{:S(2)}, u32[]{:S(2)}) collective-permute-start(bf16[8,288,128]{2,1,0:T(8,128)(2,1)S(1)} %all-to-all-done.1.got), channel_id=1, source_target_pairs={{0,16},{16,0},{1,17},{17,1},{2,18},{18,2},{3,19},{19,3},{4,20},{20... | collective-permute-start | bytes 1769480 | tf_op jit(solution)/shard_map/ppermute | solution.py:301

commit v6 on v4

--- a/solution.py
+++ b/solution.py
@@ -15,12 +15,12 @@
 GROUP = 3
 LIFT = 22
 BEV = 2
-JOIN = 10
+JOIN = 2
 CLOSE = 8
 
 
 def silu(v):
-    return v / (1.0 + jnp.exp(-v))
+    return (0.5 * v) * (1.0 + jnp.tanh(0.5 * v))
 
 
 def spread(acc, lane, chans):
@@ -155,17 +155,17 @@
     def store(j, i, value):
         moved[j, (last - 2 * i) * chans : (last - 2 * i + 1) * chans, :] = value
 
-    lift_and_convolve(
-        shape, scal, other, (low, mid, high), w_bev, store, ctx, dep, tab, lifted, scal[2], last, share - 1
-    )
     for i in range(share):
         at = (2 * share - 2 - 2 * i) * chans
         for j in range(rows + 4):
             moved[j, at : at + chans, :] = own[j, i * chans : (i + 1) * chans, :]
+    lift_and_convolve(
+        shape, scal, other, (low, mid, high), w_bev, store, ctx, dep, tab, lifted, scal[2], last, share - 1
+    )
 
     lane_wide = lax.broadcasted_iota(jnp.int32, (wide, cols), 1)
 
-    def join(pair, carry):
+    def join(pair):
         acc = None
         for a in range(3):
             both = jnp.concatenate([moved[JOIN * pair + h + a] for h in range(JOIN)], axis=1)
@@ -176,19 +176,19 @@
             value = silu(spread(acc[:, half * cols : (half + 1) * cols], lane_wide, wide))
             keep = (row >= 0) & (row < total)
             hidden[JOIN * pair + half] = jnp.where(keep, value, 0.0).astype(BF)
-        return carry
-
-    lax.fori_loop(0, (rows + 2) // JOIN, join, 0)
-
-    def close(pair, carry):
+
+    for pair in range((rows + 2) // JOIN):
+        join(pair)
+
+    def close(pair):
         sides = [hidden[pl.ds(CLOSE * pair + half, 3), :, :].reshape(3 * wide, cols) for half in range(CLOSE)]
         acc = jnp.dot(w_out[...], jnp.concatenate(sides, axis=1), preferred_element_type=F32)
         for half in range(CLOSE):
             value = spread(acc[:, half * cols : (half + 1) * cols], lane_wide, wide)
             out[CLOSE * pair + half] = value.astype(BF)
-        return carry
-
-    lax.fori_loop(0, rows // CLOSE, close, 0)
+
+    for pair in range(rows // CLOSE):
+        close(pair)
 
 
 def taps(weight):
@@ -269,15 +269,18 @@
 
     feats = jnp.broadcast_to(col_feat, (chips * 2, alone, depth_k))
     feats = lax.all_to_all(feats, ("chip", "far"), split_axis=0, concat_axis=0, tiled=True)
+    w_ctx = jnp.pad(w_ctx, ((0, 0), (0, cols - chans)))
+    col_table, w_ctx, w_bev, w_out = lax.optimization_barrier(
+        (col_table, w_ctx, taps(w_bev), taps(w_out))
+    )
     up = [(i, i + 1) for i in range(2 * ranks - 1)]
     tables = (
         lax.ppermute(col_table, line, up),
         col_table,
         lax.ppermute(col_table, line, [(t, s) for s, t in up]),
     )
-    w_ctx = jnp.pad(w_ctx, ((0, 0), (0, cols - chans)))
     feats, tables, w_ctx, w_bev, w_out = lax.optimization_barrier(
-        (feats, tables, w_ctx, taps(w_bev), taps(w_out))
+        (feats, tables, w_ctx, w_bev, w_out)
     )
 
     head = jnp.stack(

time: 70.6 us -> 72.2 us (1.023)
  blocking collectives: 12 us -> 14.1 us
  starting transfers between devices: 26.3 us -> 28 us
  waiting for transfers between devices: 4.43 us -> 3.43 us
    all_to_all x1, blocking collectives: 12 us -> 14.1 us  [shards(): lax.all_to_all(messages, ('x', 'near'), split_axis=0, concat_axis=0, tile...]
    ppermute x1, starting transfers between devices: 2.3 us -> 3.99 us  [shards(): lax.ppermute(col_table, line, up)]
    all_to_all x1, waiting for transfers between devices: 4.43 us -> 3 us  [shards(): lax.all_to_all(feats, ('chip', 'far'), split_axis=0, concat_axis=0, tiled...]
    unnamed x8 -> x10, local copies, waits for them, and re-layouts: 1.66 us -> 0.99 us
  transfers between devices with their start and end apart: 4 -> 4, of which waited for: 1 -> 2; matrix products, arithmetic and copies ran while one was open for 8% -> 7% of each run, Pallas kernels for 8% -> 8%
where the time goes in v6:
time: 72.2 us; the launch traced here: 71.8 us
  starting transfers between devices  28 us (39%)
  Pallas kernels  19.8 us (27%)
  blocking collectives  14.1 us (20%)
  local copies, waits for them, and re-layouts  6.37 us (9%)
  waiting for transfers between devices  3.43 us (5%)
    all_to_all x1, starting transfers between devices, shards(): lax.all_to_all(feats, ('chip', 'far'), split_axis=0, concat_axis=0, tiled...  16.5 us
    all_to_all x1, blocking collectives, shards(): lax.all_to_all(messages, ('x', 'near'), split_axis=0, concat_axis=0, tile...  14.1 us
    pallas_call x1, Pallas kernels, call_join(): pl.pallas_call(functools.partial(join_kernel, shape), out_shape=jax.Shape...  12.9 us
    ppermute x1, starting transfers between devices, shards(): other = lax.ppermute(got, 'core', [(0, 1), (1, 0)])  6.16 us
    pallas_call x1, Pallas kernels, call_own(): pl.pallas_call(functools.partial(own_kernel, shape), out_shape=jax.ShapeD...  5.8 us
    ppermute x1, starting transfers between devices, shards(): lax.ppermute(col_table, line, up)  3.99 us
    transpose x2, local copies, waits for them, and re-layouts, taps(): turned = jnp.transpose(weight, (1, 3, 0, 2))  3.01 us
    all_to_all x1, waiting for transfers between devices, shards(): lax.all_to_all(feats, ('chip', 'far'), split_axis=0, concat_axis=0, tiled...  3 us
  transfers between devices with their start and end apart: 4, of which 2 were waited for; matrix products, arithmetic and copies ran while one was open for 7% of the time, Pallas kernels for 8%

profile of v6, /device:TPU:1, one launch (start us, length us, event | category | flops | bytes accessed | tf_op | source)
XLA Modules:
  0.0 71.8 jit_solution(4636717555636617581)
XLA Ops:
  0.0 0.0 copy-start.2
  0.0 0.0 copy-start.3
  0.0 0.0 copy-start.1
  0.0 1.5 %broadcast_in_dim.11 = bf16[32,16,256]{2,1,0:T(8,128)(2,1)} broadcast(bf16[16,256]{1,0:T(8,128)(2,1)} %bitcast.15), dimensions={1,2} | broadcast | bytes 270336 | tf_op jit(solution)/shard_map/broadcast_in_dim | solution.py:270
  1.5 16.5 %all-to-all-start = ((bf16[32,16,256]{2,1,0:T(8,128)(2,1)}), bf16[32,16,256]{2,1,0:T(8,128)(2,1)S(1)}, u32[]{:S(2)}, u32[]{:S(2)}) async-start(bf16[32,16,256]{2,1,0:T(8,128)(2,1)} %broadcast_in_dim.11), calls=%async_computation | async-start | bytes 524288 | tf_op jit(solution)/shard_map/all_to_all | solution.py:271
  18.0 0.9 %copy.14 = bf16[256,80]{1,0:T(8,128)(2,1)S(1)} copy(bf16[256,80]{0,1:T(8,128)(2,1)} %param.10) | data formatting | bytes 81920 | tf_op args[2]
  18.9 1.1 %copy.15 = bf16[3,80,3,80]{3,2,1,0:T(4,128)(2,1)S(1)} copy(bf16[3,80,3,80]{1,3,0,2:T(8,128)(2,1)} %bitcast.14) | data formatting | bytes 230400 | tf_op jit(solution)/shard_map/transpose | solution.py:195
  20.0 0.2 reshape.13.w_bev
  20.2 1.9 %copy.16 = bf16[3,160,3,160]{3,2,1,0:T(4,128)(2,1)S(1)} copy(bf16[3,160,3,160]{1,3,0,2:T(8,128)(2,1)} %bitcast.13) | data formatting | bytes 921600 | tf_op jit(solution)/shard_map/transpose | solution.py:195
  22.1 0.6 reshape.14.w_out
  22.7 0.0 copy-done.2
  22.7 1.3 %collective-permute-start.1 = (s32[8,128]{1,0:T(8,128)S(1)}, s32[8,128]{1,0:T(8,128)S(1)}, u32[]{:S(2)}, u32[]{:S(2)}) collective-permute-start(s32[8,128]{1,0:T(8,128)S(1)} %copy-done.2), channel_id=1, source_target_pairs={{1,0},{2,1},{3,2},{4,3},{5,4},{6,5},{7,6},{8,7},{9,8},{10,9},{11,1... | collective-permute-start | bytes 12296 | tf_op jit(solution)/shard_map/ppermute | solution.py:280
  24.0 4.0 %collective-permute-start = (s32[8,128]{1,0:T(8,128)S(1)}, s32[8,128]{1,0:T(8,128)S(1)}, u32[]{:S(2)}, u32[]{:S(2)}) collective-permute-start(s32[8,128]{1,0:T(8,128)S(1)} %copy-done.2), channel_id=1, source_target_pairs={{0,1},{1,2},{2,3},{3,4},{4,5},{5,6},{6,7},{7,8},{8,9},{9,10},{10,1... | collective-permute-start | bytes 12296 | tf_op jit(solution)/shard_map/ppermute | solution.py:278
  28.0 0.0 copy-done.3
  28.0 0.1 copy.17
  28.1 0.1 reshape.12
  28.2 0.1 concatenate.7.scal
  28.3 0.0 collective-permute-done.1.high
  28.3 0.4 collective-permute-done.low
  28.7 3.0 %all-to-all-done.feats = bf16[32,16,256]{2,1,0:T(8,128)(2,1)S(1)} async-done(((bf16[32,16,256]{2,1,0:T(8,128)(2,1)}), bf16[32,16,256]{2,1,0:T(8,128)(2,1)S(1)}, u32[]{:S(2)}, u32[]{:S(2)}) %all-to-all-start) | async-done | bytes 262176 | tf_op jit(solution)/shard_map/all_to_all | solution.py:271
  31.7 0.0 copy-done.1
  31.7 0.0 copy-start
  31.7 1.1 %pack.1 = bf16[8,288,128]{2,1,0:T(8,128)(2,1)S(1)} custom-call(s32[38]{0:T(128)S(1)} %concatenate.7.scal, bf16[32,16,256]{2,1,0:T(8,128)(2,1)S(1)} %all-to-all-done.feats, bf16[256,128]{1,0:T(8,128)(2,1)S(1)} %copy-done.1, bf16[256,128]{1,0:T(8,128)(2,1)S(1)} %pad.5.w_ctx), custom_call_target="tpu_custom_call" | custom-call | tf_op jit(solution)/shard_map/pack/pallas_call | solution.py:215
  32.8 14.1 %all_to_all.10.got = bf16[8,288,128]{2,1,0:T(8,128)(2,1)S(1)} all-to-all(bf16[8,288,128]{2,1,0:T(8,128)(2,1)S(1)} %pack.1), channel_id=1, replica_groups=mesh['chip'=16,'core'=2,'x'=4,'far'=2,'near'=2] {'x','near'}, dimensions={0} | all-to-all | bytes 1179648 | tf_op jit(solution)/shard_map/all_to_all | solution.py:298
  47.0 6.2 %collective-permute-start.2 = (bf16[8,288,128]{2,1,0:T(8,128)(2,1)S(1)}, bf16[8,288,128]{2,1,0:T(8,128)(2,1)S(1)}, u32[]{:S(2)}, u32[]{:S(2)}) collective-permute-start(bf16[8,288,128]{2,1,0:T(8,128)(2,1)S(1)} %all_to_all.10.got), channel_id=1, source_target_pairs={{0,16},{16,0},{1,17},{17,1},{2,18},{18,2},{3,19},{19,3},{4,20},{20... | collective-permute-start | bytes 1769480 | tf_op jit(solution)/shard_map/ppermute | solution.py:299
  53.1 5.8 %own.1 = bf16[12,720,128]{2,1,0:T(8,128)(2,1)S(1)} custom-call(s32[38]{0:T(128)S(1)} %concatenate.7.scal, bf16[8,288,128]{2,1,0:T(8,128)(2,1)S(1)} %all_to_all.10.got, s32[8,128]{1,0:T(8,128)S(1)} %collective-permute-done.low, s32[8,128]{1,0:T(8,128)S(1)} %copy-done.2, s32[8,128]{1,0:T(8,128)S(1)} %collective-permute-done.1.high, ...), custom_call_target="tpu_custom_call" | custom-call | tf_op jit(solution)/shard_map/own/pallas_call | solution.py:228
  58.9 0.0 collective-permute-done.2.other
  58.9 0.0 copy-done
  59.0 12.9 %join.1 = bf16[8,160,128]{2,1,0:T(8,128)(2,1)} custom-call(s32[38]{0:T(128)S(1)} %concatenate.7.scal, bf16[8,288,128]{2,1,0:T(8,128)(2,1)S(1)} %collective-permute-done.2.other, s32[8,128]{1,0:T(8,128)S(1)} %collective-permute-done.low, s32[8,128]{1,0:T(8,128)S(1)} %copy-done.2, s32[8,128]{1,0:T(8,128)S(1)} %collective-permute-done.1.high, ...), custom_call_target="tpu_custom_call" | custom-call | tf_op jit(solution)/shard_map/join/pallas_call | solution.py:241
  (2 shorter events, 0.0 us)
Async XLA Ops:
  0.0 22.7 %copy-start.2 = (s32[8,128]{1,0:T(8,128)S(1)}, s32[8,128]{1,0:T(8,128)}, u32[]{:S(2)}) copy-start(s32[8,128]{1,0:T(8,128)} %mid.1) | copy-start | bytes 12292
  0.0 28.0 %copy-start.3 = (s32[1,16,2]{1,2,0:T(2,128)S(1)}, s32[1,16,2]{1,2,0:T(2,128)}, u32[]{:S(2)}) copy-start(s32[1,16,2]{1,2,0:T(2,128)} %param.13) | copy-start | bytes 388
  0.0 31.7 %copy-start.1 = (bf16[256,128]{1,0:T(8,128)(2,1)S(1)}, bf16[256,128]{1,0:T(8,128)(2,1)}, u32[]{:S(2)}) copy-start(bf16[256,128]{1,0:T(8,128)(2,1)} %w_depth.1) | copy-start | bytes 196612
  1.5 30.2 %all-to-all-start = ((bf16[32,16,256]{2,1,0:T(8,128)(2,1)}), bf16[32,16,256]{2,1,0:T(8,128)(2,1)S(1)}, u32[]{:S(2)}, u32[]{:S(2)}) async-start(bf16[32,16,256]{2,1,0:T(8,128)(2,1)} %broadcast_in_dim.11), calls=%async_computation | async-start | bytes 524288 | tf_op jit(solution)/shard_map/all_to_all | solution.py:271
  22.7 5.6 %collective-permute-start.1 = (s32[8,128]{1,0:T(8,128)S(1)}, s32[8,128]{1,0:T(8,128)S(1)}, u32[]{:S(2)}, u32[]{:S(2)}) collective-permute-start(s32[8,128]{1,0:T(8,128)S(1)} %copy-done.2), channel_id=1, source_target_pairs={{1,0},{2,1},{3,2},{4,3},{5,4},{6,5},{7,6},{8,7},{9,8},{10,9},{11,1... | collective-permute-start | bytes 12296 | tf_op jit(solution)/shard_map/ppermute | solution.py:280
  24.0 4.7 %collective-permute-start = (s32[8,128]{1,0:T(8,128)S(1)}, s32[8,128]{1,0:T(8,128)S(1)}, u32[]{:S(2)}, u32[]{:S(2)}) collective-permute-start(s32[8,128]{1,0:T(8,128)S(1)} %copy-done.2), channel_id=1, source_target_pairs={{0,1},{1,2},{2,3},{3,4},{4,5},{5,6},{6,7},{7,8},{8,9},{9,10},{10,1... | collective-permute-start | bytes 12296 | tf_op jit(solution)/shard_map/ppermute | solution.py:278
  31.7 27.2 %copy-start = (bf16[3,3,1360,160]{2,3,1,0:T(8,128)(2,1)S(1)}, bf16[3,3,1360,160]{2,3,1,0:T(8,128)(2,1)}, u32[]{:S(2)}) copy-start(bf16[3,3,1360,160]{2,3,1,0:T(8,128)(2,1)} %param.14) | copy-start | bytes 11750404
  47.0 12.0 %collective-permute-start.2 = (bf16[8,288,128]{2,1,0:T(8,128)(2,1)S(1)}, bf16[8,288,128]{2,1,0:T(8,128)(2,1)S(1)}, u32[]{:S(2)}, u32[]{:S(2)}) collective-permute-start(bf16[8,288,128]{2,1,0:T(8,128)(2,1)S(1)} %all_to_all.10.got), channel_id=1, source_target_pairs={{0,16},{16,0},{1,17},{17,1},{2,18},{18,2},{3,19},{19,3},{4,20},{20... | collective-permute-start | bytes 1769480 | tf_op jit(solution)/shard_map/ppermute | solution.py:299

commit v7 on v6

--- a/solution.py
+++ b/solution.py
@@ -30,7 +30,7 @@
     return acc[chans : 2 * chans] + low + high
 
 
-def pack_kernel(shape, scal, feats, w_depth, w_ctx, out, stack):
+def pack_kernel(shape, scal, feats, w_depth, w_ctx, table, pair_table, out, stack):
     ranks, share, columns, chans, rows, total, cols, wide = shape
     span = rows + 2 * EXTRA
     far = scal[3]
@@ -47,6 +47,10 @@
     rest = depth - main
     ctx = jnp.dot(stacked, w_ctx[...], preferred_element_type=F32)
     lane = lax.broadcasted_iota(jnp.int32, ctx.shape, 1)
+    mine, theirs = table[...].astype(F32), pair_table[...].astype(F32)
+    tabs = jnp.concatenate(
+        [jnp.where(far == 0, mine, theirs), jnp.where(far == 0, theirs, mine)], axis=0
+    ).astype(BF)
     for rank in range(ranks):
         first = rows * (rank // 2 * 4 + rank % 2 + 2 * far) - EXTRA
         message = jnp.where(lane < chans, ctx, 0.0)
@@ -56,10 +60,11 @@
             low = jnp.maximum(start, start - first)
             high = jnp.minimum(start + span, total - first + start)
             message = jnp.where((lane >= low) & (lane < high), turned, message)
-        out[rank] = message.astype(BF)
-
-
-def lift_and_convolve(shape, scal, got, tables, w_bev, store, ctx, dep, tab, lifted, skip, last, frames):
+        out[rank, : share * columns, :] = message.astype(BF)
+        out[rank, share * columns :, :] = tabs
+
+
+def lift_and_convolve(shape, scal, got, w_bev, store, ctx, dep, tab, lifted, skip, last, frames):
     ranks, share, columns, chans, rows, total, cols, wide = shape
     here = scal[0]
     count = ranks * columns
@@ -75,7 +80,10 @@
         dep[:, i, :] = turned[chans : chans + span]
         dep[:, 16 + i, :] = turned[chans + span : chans + 2 * span]
     for side in range(3):
-        tab[side * rows : (side + 1) * rows, :] = tables[side][...]
+        block = jnp.clip(here + (side - 1), 0, 2 * ranks - 1)
+        both = got[(block >> 2) * 2 + (block & 1), share * columns :, :].astype(F32)
+        half = jnp.where((block & 2) == 0, both[:rows], both[rows:])
+        tab[side * rows : (side + 1) * rows, :] = half.astype(jnp.int32)
 
     alone = columns // 2
     place = lax.broadcasted_iota(jnp.int32, (count, cols), 0)
@@ -134,19 +142,19 @@
         bev(i)
 
 
-def own_kernel(shape, scal, got, low, mid, high, w_bev, out, ctx, dep, tab, lifted):
+def own_kernel(shape, scal, got, w_bev, out, ctx, dep, tab, lifted):
     share, chans = shape[1], shape[3]
 
     def store(j, i, value):
         out[j, i * chans : (i + 1) * chans, :] = value
 
     lift_and_convolve(
-        shape, scal, got, (low, mid, high), w_bev, store, ctx, dep, tab, lifted, 0, 2 * share - 2, share
+        shape, scal, got, w_bev, store, ctx, dep, tab, lifted, 0, 2 * share - 2, share
     )
 
 
 def join_kernel(
-    shape, scal, other, low, mid, high, own, w_bev, w_join, w_out, out, ctx, dep, tab, lifted, moved, hidden
+    shape, scal, other, own, w_bev, w_join, w_out, out, ctx, dep, tab, lifted, moved, hidden
 ):
     ranks, share, columns, chans, rows, total, cols, wide = shape
     here = scal[0]
@@ -160,7 +168,7 @@
         for j in range(rows + 4):
             moved[j, at : at + chans, :] = own[j, i * chans : (i + 1) * chans, :]
     lift_and_convolve(
-        shape, scal, other, (low, mid, high), w_bev, store, ctx, dep, tab, lifted, scal[2], last, share - 1
+        shape, scal, other, w_bev, store, ctx, dep, tab, lifted, scal[2], last, share - 1
     )
 
     lane_wide = lax.broadcasted_iota(jnp.int32, (wide, cols), 1)
@@ -210,38 +218,38 @@
     ]
 
 
-def call_pack(shape, scal, feats, w_depth, w_ctx):
+def call_pack(shape, scal, feats, w_depth, w_ctx, table, pair_table):
     ranks, share, columns, chans, rows, total, cols, wide = shape
     return pl.pallas_call(
         functools.partial(pack_kernel, shape),
-        out_shape=jax.ShapeDtypeStruct((ranks, share * columns, cols), BF),
-        in_specs=[SMEM, VMEM, VMEM, VMEM],
+        out_shape=jax.ShapeDtypeStruct((ranks, share * columns + 2 * rows, cols), BF),
+        in_specs=[SMEM] + [VMEM] * 5,
         out_specs=VMEM,
         scratch_shapes=[pltpu.VMEM((share * columns, feats.shape[2]), BF)],
         compiler_params=pltpu.CompilerParams(vmem_limit_bytes=32 * 1024 * 1024),
         name="pack",
-    )(scal, feats, w_depth, w_ctx)
-
-
-def call_own(shape, scal, got, tables, w_bev):
+    )(scal, feats, w_depth, w_ctx, table, pair_table)
+
+
+def call_own(shape, scal, got, w_bev):
     ranks, share, columns, chans, rows, total, cols, wide = shape
     return pl.pallas_call(
         functools.partial(own_kernel, shape),
         out_shape=jax.ShapeDtypeStruct((rows + 4, share * chans, cols), BF),
-        in_specs=[SMEM] + [VMEM] * 5,
+        in_specs=[SMEM] + [VMEM] * 2,
         out_specs=VMEM,
         scratch_shapes=scratch(share, chans, ranks * columns, rows, cols),
         compiler_params=pltpu.CompilerParams(vmem_limit_bytes=24 * 1024 * 1024),
         name="own",
-    )(scal, got, *tables, w_bev)
-
-
-def call_join(shape, scal, other, tables, own, w_bev, w_join, w_out):
+    )(scal, got, w_bev)
+
+
+def call_join(shape, scal, other, own, w_bev, w_join, w_out):
     ranks, share, columns, chans, rows, total, cols, wide = shape
     return pl.pallas_call(
         functools.partial(join_kernel, shape),
         out_shape=jax.ShapeDtypeStruct((rows, wide, cols), BF),
-        in_specs=[SMEM] + [VMEM] * 8,
+        in_specs=[SMEM] + [VMEM] * 5,
         out_specs=VMEM,
         scratch_shapes=scratch(share - 1, chans, ranks * columns, rows, cols)
         + [
@@ -250,7 +258,7 @@
         ],
         compiler_params=pltpu.CompilerParams(vmem_limit_bytes=36 * 1024 * 1024),
         name="join",
-    )(scal, other, *tables, own, w_bev, w_join, w_out)
+    )(scal, other, own, w_bev, w_join, w_out)
 
 
 def shards(col_feat, w_depth, w_ctx, col_table, w_bev, offsets, w_join, w_out):
@@ -265,27 +273,18 @@
     share = (frames + 1) // 2
     columns = 2 * alone
     shape = (ranks, share, columns, chans, rows, total, cols, wide)
-    line = ("x", "far", "near")
 
     feats = jnp.broadcast_to(col_feat, (chips * 2, alone, depth_k))
     feats = lax.all_to_all(feats, ("chip", "far"), split_axis=0, concat_axis=0, tiled=True)
+    pair_table = lax.ppermute(col_table, "far", [(0, 1), (1, 0)])
     w_ctx = jnp.pad(w_ctx, ((0, 0), (0, cols - chans)))
-    col_table, w_ctx, w_bev, w_out = lax.optimization_barrier(
-        (col_table, w_ctx, taps(w_bev), taps(w_out))
-    )
-    up = [(i, i + 1) for i in range(2 * ranks - 1)]
-    tables = (
-        lax.ppermute(col_table, line, up),
-        col_table,
-        lax.ppermute(col_table, line, [(t, s) for s, t in up]),
-    )
-    feats, tables, w_ctx, w_bev, w_out = lax.optimization_barrier(
-        (feats, tables, w_ctx, w_bev, w_out)
+    feats, pair_table, w_ctx, w_bev, w_out = lax.optimization_barrier(
+        (feats, pair_table, w_ctx, taps(w_bev), taps(w_out))
     )
 
     head = jnp.stack(
         [
-            lax.axis_index(line).astype(jnp.int32),
+            lax.axis_index(("x", "far", "near")).astype(jnp.int32),
             lax.axis_index("chip").astype(jnp.int32) - (share - 1),
             lax.axis_index("core").astype(jnp.int32),
             lax.axis_index("far").astype(jnp.int32),
@@ -294,13 +293,13 @@
     moves = jnp.concatenate([jnp.zeros((1, 2), jnp.int32), offsets[0]], axis=0)
     scal = jnp.concatenate([head, moves.reshape(-1)])
 
-    messages = call_pack(shape, scal, feats, w_depth, w_ctx)
+    messages = call_pack(shape, scal, feats, w_depth, w_ctx, col_table, pair_table)
     got = lax.all_to_all(messages, ("x", "near"), split_axis=0, concat_axis=0, tiled=True)
     other = lax.ppermute(got, "core", [(0, 1), (1, 0)])
 
     w_join = jnp.transpose(w_join, (0, 1, 3, 2)).reshape(3, 3 * wide, frames * chans)
-    own = call_own(shape, scal, got, tables, w_bev)
-    joined = call_join(shape, scal, other, tables, own, w_bev, w_join, w_out)
+    own = call_own(shape, scal, got, w_bev)
+    joined = call_join(shape, scal, other, own, w_bev, w_join, w_out)
     return joined[None]
 
 

time: 72.2 us -> 70.3 us (0.974)
  blocking collectives: 14.1 us -> 12.2 us
  starting transfers between devices: 28 us -> 26.8 us
    all_to_all x1, blocking collectives: 14.1 us -> 12.2 us  [shards(): lax.all_to_all(messages, ('x', 'near'), split_axis=0, concat_axis=0, tile...]
    ppermute x2 -> x1, starting transfers between devices: 5.28 us -> 4.04 us  [shards(): pair_table = lax.ppermute(col_table, 'far', [(0, 1), (1, 0)])]
    all_to_all x1, waiting for transfers between devices: 3 us -> 3.95 us  [shards(): lax.all_to_all(feats, ('chip', 'far'), split_axis=0, concat_axis=0, tiled...]
    unnamed x10 -> x8, local copies, waits for them, and re-layouts: 0.99 us -> 1.66 us
  transfers between devices with their start and end apart: 4 -> 3, of which waited for: 2 -> 1; matrix products, arithmetic and copies ran while one was open for 7% -> 8% of each run, Pallas kernels for 8% -> 8%
where the time goes in v7:
time: 70.3 us; the launch traced here: 69.9 us
  starting transfers between devices  26.8 us (38%)
  Pallas kernels  19.8 us (28%)
  blocking collectives  12.2 us (17%)
  local copies, waits for them, and re-layouts  7.03 us (10%)
  waiting for transfers between devices  3.96 us (6%)
    all_to_all x1, starting transfers between devices, shards(): lax.all_to_all(feats, ('chip', 'far'), split_axis=0, concat_axis=0, tiled...  16.5 us
    pallas_call x1, Pallas kernels, call_join(): pl.pallas_call(functools.partial(join_kernel, shape), out_shape=jax.Shape...  12.9 us
    all_to_all x1, blocking collectives, shards(): lax.all_to_all(messages, ('x', 'near'), split_axis=0, concat_axis=0, tile...  12.2 us
    ppermute x1, starting transfers between devices, shards(): other = lax.ppermute(got, 'core', [(0, 1), (1, 0)])  6.27 us
    pallas_call x1, Pallas kernels, call_own(): pl.pallas_call(functools.partial(own_kernel, shape), out_shape=jax.ShapeD...  5.81 us
    ppermute x1, starting transfers between devices, shards(): pair_table = lax.ppermute(col_table, 'far', [(0, 1), (1, 0)])  4.04 us
    all_to_all x1, waiting for transfers between devices, shards(): lax.all_to_all(feats, ('chip', 'far'), split_axis=0, concat_axis=0, tiled...  3.95 us
    transpose x2, local copies, waits for them, and re-layouts, taps(): turned = jnp.transpose(weight, (1, 3, 0, 2))  3 us
  transfers between devices with their start and end apart: 3, of which 1 were waited for; matrix products, arithmetic and copies ran while one was open for 8% of the time, Pallas kernels for 8%

profile of v7, /device:TPU:1, one launch (start us, length us, event | category | flops | bytes accessed | tf_op | source)
XLA Modules:
  0.0 69.9 jit_solution(6041761875434844859)
XLA Ops:
  0.0 0.0 copy-start.2
  0.0 0.0 copy-start.1
  0.0 1.4 %broadcast_in_dim.11 = bf16[32,16,256]{2,1,0:T(8,128)(2,1)} broadcast(bf16[16,256]{1,0:T(8,128)(2,1)} %bitcast.15), dimensions={1,2} | broadcast | bytes 270336 | tf_op jit(solution)/shard_map/broadcast_in_dim | solution.py:277
  1.5 16.5 %all-to-all-start = ((bf16[32,16,256]{2,1,0:T(8,128)(2,1)}), bf16[32,16,256]{2,1,0:T(8,128)(2,1)S(1)}, u32[]{:S(2)}, u32[]{:S(2)}) async-start(bf16[32,16,256]{2,1,0:T(8,128)(2,1)} %broadcast_in_dim.11), calls=%async_computation | async-start | bytes 524288 | tf_op jit(solution)/shard_map/all_to_all | solution.py:278
  18.0 4.0 %collective-permute-start = (s32[8,128]{1,0:T(8,128)}, s32[8,128]{1,0:T(8,128)S(1)}, u32[]{:S(2)}, u32[]{:S(2)}) collective-permute-start(s32[8,128]{1,0:T(8,128)} %table.1), channel_id=1, source_target_pairs={{0,2},{2,0},{1,3},{3,1},{4,6},{6,4},{5,7},{7,5},{8,10},{10,8},{9,1... | collective-permute-start | bytes 12296 | tf_op jit(solution)/shard_map/ppermute | solution.py:279
  22.0 0.8 %copy.17 = s32[16,2]{1,0:T(8,128)S(1)} copy(s32[16,2]{0,1:T(2,128)} %bitcast.16) | data formatting | bytes 256
  22.8 0.1 reshape.12
  22.9 0.9 %copy.14 = bf16[256,80]{1,0:T(8,128)(2,1)S(1)} copy(bf16[256,80]{0,1:T(8,128)(2,1)} %param.10) | data formatting | bytes 81920 | tf_op args[2]
  23.8 1.1 %copy.15 = bf16[3,80,3,80]{3,2,1,0:T(4,128)(2,1)S(1)} copy(bf16[3,80,3,80]{1,3,0,2:T(8,128)(2,1)} %bitcast.14) | data formatting | bytes 230400 | tf_op jit(solution)/shard_map/transpose | solution.py:203
  24.9 0.2 reshape.13.w_bev
  25.1 1.9 %copy.16 = bf16[3,160,3,160]{3,2,1,0:T(4,128)(2,1)S(1)} copy(bf16[3,160,3,160]{1,3,0,2:T(8,128)(2,1)} %bitcast.13) | data formatting | bytes 921600 | tf_op jit(solution)/shard_map/transpose | solution.py:203
  27.0 0.6 reshape.14.w_out
  27.6 0.1 concatenate.7.scal
  27.7 0.0 collective-permute-done.pair_table
  27.7 4.0 %all-to-all-done.feats = bf16[32,16,256]{2,1,0:T(8,128)(2,1)S(1)} async-done(((bf16[32,16,256]{2,1,0:T(8,128)(2,1)}), bf16[32,16,256]{2,1,0:T(8,128)(2,1)S(1)}, u32[]{:S(2)}, u32[]{:S(2)}) %all-to-all-start) | async-done | bytes 262176 | tf_op jit(solution)/shard_map/all_to_all | solution.py:278
  31.6 0.0 copy-done.2
  31.6 0.0 copy-done.1
  31.6 0.0 copy-start
  31.6 1.1 %pack.1 = bf16[8,304,128]{2,1,0:T(8,128)(2,1)S(1)} custom-call(s32[38]{0:T(128)S(1)} %concatenate.7.scal, bf16[32,16,256]{2,1,0:T(8,128)(2,1)S(1)} %all-to-all-done.feats, bf16[256,128]{1,0:T(8,128)(2,1)S(1)} %copy-done.1, bf16[256,128]{1,0:T(8,128)(2,1)S(1)} %pad.5.w_ctx, s32[8,128]{1,0:T(8,128)S(1)} %copy-done.2, s32[8,128]{1,0:T(8,128)S(1)} %collective-permute-done.pair_table), custom_call_target="tpu_custom_call" | custom-call | tf_op jit(solution)/shard_map/pack/pallas_call | solution.py:223
  32.7 12.2 %all_to_all.10.got = bf16[8,304,128]{2,1,0:T(8,128)(2,1)S(1)} all-to-all(bf16[8,304,128]{2,1,0:T(8,128)(2,1)S(1)} %pack.1), channel_id=1, replica_groups=mesh['chip'=16,'core'=2,'x'=4,'far'=2,'near'=2] {'x','near'}, dimensions={0} | all-to-all | bytes 1245184 | tf_op jit(solution)/shard_map/all_to_all | solution.py:297
  44.9 6.3 %collective-permute-start.1 = (bf16[8,304,128]{2,1,0:T(8,128)(2,1)S(1)}, bf16[8,304,128]{2,1,0:T(8,128)(2,1)S(1)}, u32[]{:S(2)}, u32[]{:S(2)}) collective-permute-start(bf16[8,304,128]{2,1,0:T(8,128)(2,1)S(1)} %all_to_all.10.got), channel_id=1, source_target_pairs={{0,16},{16,0},{1,17},{17,1},{2,18},{18,2},{3,19},{19,3},{4,20},{20... | collective-permute-start | bytes 1867784 | tf_op jit(solution)/shard_map/ppermute | solution.py:298
  51.2 5.8 %own.1 = bf16[12,720,128]{2,1,0:T(8,128)(2,1)S(1)} custom-call(s32[38]{0:T(128)S(1)} %concatenate.7.scal, bf16[8,304,128]{2,1,0:T(8,128)(2,1)S(1)} %all_to_all.10.got, bf16[240,240]{1,0:T(8,128)(2,1)S(1)} %reshape.13.w_bev), custom_call_target="tpu_custom_call" | custom-call | tf_op jit(solution)/shard_map/own/pallas_call | solution.py:236
  57.0 0.0 collective-permute-done.1.other
  57.0 0.0 copy-done
  57.0 12.9 %join.1 = bf16[8,160,128]{2,1,0:T(8,128)(2,1)} custom-call(s32[38]{0:T(128)S(1)} %concatenate.7.scal, bf16[8,304,128]{2,1,0:T(8,128)(2,1)S(1)} %collective-permute-done.1.other, bf16[12,720,128]{2,1,0:T(8,128)(2,1)S(1)} %own.1, bf16[240,240]{1,0:T(8,128)(2,1)S(1)} %reshape.13.w_bev, bf16[3,480,1360]{2,1,0:T(8,128)(2,1)S(1)} %bitcast.12, ...), custom_call_target="tpu_custom_call" | custom-call | tf_op jit(solution)/shard_map/join/pallas_call | solution.py:249
  (2 shorter events, 0.0 us)
Async XLA Ops:
  0.0 31.6 %copy-start.2 = (s32[8,128]{1,0:T(8,128)S(1)}, s32[8,128]{1,0:T(8,128)}, u32[]{:S(2)}) copy-start(s32[8,128]{1,0:T(8,128)} %table.1) | copy-start | bytes 12292
  0.0 31.6 %copy-start.1 = (bf16[256,128]{1,0:T(8,128)(2,1)S(1)}, bf16[256,128]{1,0:T(8,128)(2,1)}, u32[]{:S(2)}) copy-start(bf16[256,128]{1,0:T(8,128)(2,1)} %w_depth.1) | copy-start | bytes 196612
  1.5 30.2 %all-to-all-start = ((bf16[32,16,256]{2,1,0:T(8,128)(2,1)}), bf16[32,16,256]{2,1,0:T(8,128)(2,1)S(1)}, u32[]{:S(2)}, u32[]{:S(2)}) async-start(bf16[32,16,256]{2,1,0:T(8,128)(2,1)} %broadcast_in_dim.11), calls=%async_computation | async-start | bytes 524288 | tf_op jit(solution)/shard_map/all_to_all | solution.py:278
  18.0 9.7 %collective-permute-start = (s32[8,128]{1,0:T(8,128)}, s32[8,128]{1,0:T(8,128)S(1)}, u32[]{:S(2)}, u32[]{:S(2)}) collective-permute-start(s32[8,128]{1,0:T(8,128)} %table.1), channel_id=1, source_target_pairs={{0,2},{2,0},{1,3},{3,1},{4,6},{6,4},{5,7},{7,5},{8,10},{10,8},{9,1... | collective-permute-start | bytes 12296 | tf_op jit(solution)/shard_map/ppermute | solution.py:279
  31.6 25.4 %copy-start = (bf16[3,3,1360,160]{2,3,1,0:T(8,128)(2,1)S(1)}, bf16[3,3,1360,160]{2,3,1,0:T(8,128)(2,1)}, u32[]{:S(2)}) copy-start(bf16[3,3,1360,160]{2,3,1,0:T(8,128)(2,1)} %param.14) | copy-start | bytes 11750404
  44.9 12.1 %collective-permute-start.1 = (bf16[8,304,128]{2,1,0:T(8,128)(2,1)S(1)}, bf16[8,304,128]{2,1,0:T(8,128)(2,1)S(1)}, u32[]{:S(2)}, u32[]{:S(2)}) collective-permute-start(bf16[8,304,128]{2,1,0:T(8,128)(2,1)S(1)} %all_to_all.10.got), channel_id=1, source_target_pairs={{0,16},{16,0},{1,17},{17,1},{2,18},{18,2},{3,19},{19,3},{4,20},{20... | collective-permute-start | bytes 1867784 | tf_op jit(solution)/shard_map/ppermute | solution.py:298

commit v8 on v7

--- a/solution.py
+++ b/solution.py
@@ -45,7 +45,10 @@
     depth = jax.nn.sigmoid(jnp.dot(stacked, w_depth[...], preferred_element_type=F32))
     main = depth.astype(BF).astype(F32)
     rest = depth - main
-    ctx = jnp.dot(stacked, w_ctx[...], preferred_element_type=F32)
+    turned_ctx = jnp.concatenate(
+        [w_ctx[...], jnp.zeros((cols - chans, w_ctx.shape[1]), BF)], axis=0
+    )
+    ctx = lax.dot_general(stacked, turned_ctx, (((1,), (1,)), ((), ())), preferred_element_type=F32)
     lane = lax.broadcasted_iota(jnp.int32, ctx.shape, 1)
     mine, theirs = table[...].astype(F32), pair_table[...].astype(F32)
     tabs = jnp.concatenate(
@@ -64,7 +67,7 @@
         out[rank, share * columns :, :] = tabs
 
 
-def lift_and_convolve(shape, scal, got, w_bev, store, ctx, dep, tab, lifted, skip, last, frames):
+def lift_and_convolve(shape, scal, moves, got, w_bev, store, ctx, dep, tab, lifted, skip, last, frames):
     ranks, share, columns, chans, rows, total, cols, wide = shape
     here = scal[0]
     count = ranks * columns
@@ -119,8 +122,10 @@
 
     def bev(i):
         k = last - 2 * i
-        dy = scal[4 + 2 * k]
-        dx = scal[5 + 2 * k]
+        if k == 0:
+            dy, dx = jnp.int32(0), jnp.int32(0)
+        else:
+            dy, dx = moves[0, k - 1], moves[1, k - 1]
         base = dy + REACH
         at = i * chans
         inside = (lane + dx >= 0) & (lane + dx < cols)
@@ -142,21 +147,32 @@
         bev(i)
 
 
-def own_kernel(shape, scal, got, w_bev, out, ctx, dep, tab, lifted):
+def turn_taps(weight, out):
+    size = weight.shape[3]
+    for b in range(3):
+        column = jnp.concatenate([weight[a, b] for a in range(3)], axis=0)
+        out[b * size : (b + 1) * size, :] = column.astype(F32).T.astype(BF)
+
+
+def own_kernel(shape, scal, moves, got, weight, out, ctx, dep, tab, lifted, w_bev):
     share, chans = shape[1], shape[3]
+    turn_taps(weight, w_bev)
 
     def store(j, i, value):
         out[j, i * chans : (i + 1) * chans, :] = value
 
     lift_and_convolve(
-        shape, scal, got, w_bev, store, ctx, dep, tab, lifted, 0, 2 * share - 2, share
+        shape, scal, moves, got, w_bev, store, ctx, dep, tab, lifted, 0, 2 * share - 2, share
     )
 
 
 def join_kernel(
-    shape, scal, other, own, w_bev, w_join, w_out, out, ctx, dep, tab, lifted, moved, hidden
+    shape, scal, moves, other, own, weight, w_join, weight_out, out,
+    ctx, dep, tab, lifted, moved, hidden, w_bev, w_out,
 ):
     ranks, share, columns, chans, rows, total, cols, wide = shape
+    turn_taps(weight, w_bev)
+    turn_taps(weight_out, w_out)
     here = scal[0]
     last = 2 * share - 3
 
@@ -168,7 +184,7 @@
         for j in range(rows + 4):
             moved[j, at : at + chans, :] = own[j, i * chans : (i + 1) * chans, :]
     lift_and_convolve(
-        shape, scal, other, w_bev, store, ctx, dep, tab, lifted, scal[2], last, share - 1
+        shape, scal, moves, other, w_bev, store, ctx, dep, tab, lifted, scal[2], last, share - 1
     )
 
     lane_wide = lax.broadcasted_iota(jnp.int32, (wide, cols), 1)
@@ -199,11 +215,6 @@
         close(pair)
 
 
-def taps(weight):
-    turned = jnp.transpose(weight, (1, 3, 0, 2))
-    return turned.reshape(weight.shape[1] * weight.shape[3], weight.shape[0] * weight.shape[2])
-
-
 VMEM = pl.BlockSpec(memory_space=pltpu.VMEM)
 SMEM = pl.BlockSpec(memory_space=pltpu.SMEM)
 
@@ -231,34 +242,37 @@
     )(scal, feats, w_depth, w_ctx, table, pair_table)
 
 
-def call_own(shape, scal, got, w_bev):
+def call_own(shape, scal, moves, got, w_bev):
     ranks, share, columns, chans, rows, total, cols, wide = shape
     return pl.pallas_call(
         functools.partial(own_kernel, shape),
         out_shape=jax.ShapeDtypeStruct((rows + 4, share * chans, cols), BF),
-        in_specs=[SMEM] + [VMEM] * 2,
+        in_specs=[SMEM] * 2 + [VMEM] * 2,
         out_specs=VMEM,
-        scratch_shapes=scratch(share, chans, ranks * columns, rows, cols),
+        scratch_shapes=scratch(share, chans, ranks * columns, rows, cols)
+        + [pltpu.VMEM((3 * chans, 3 * chans), BF)],
         compiler_params=pltpu.CompilerParams(vmem_limit_bytes=24 * 1024 * 1024),
         name="own",
-    )(scal, got, w_bev)
-
-
-def call_join(shape, scal, other, own, w_bev, w_join, w_out):
+    )(scal, moves, got, w_bev)
+
+
+def call_join(shape, scal, moves, other, own, w_bev, w_join, w_out):
     ranks, share, columns, chans, rows, total, cols, wide = shape
     return pl.pallas_call(
         functools.partial(join_kernel, shape),
         out_shape=jax.ShapeDtypeStruct((rows, wide, cols), BF),
-        in_specs=[SMEM] + [VMEM] * 5,
+        in_specs=[SMEM] * 2 + [VMEM] * 5,
         out_specs=VMEM,
         scratch_shapes=scratch(share - 1, chans, ranks * columns, rows, cols)
         + [
             pltpu.VMEM((rows + 4, (2 * share - 1) * chans, cols), BF),
             pltpu.VMEM((rows + 2, wide, cols), BF),
+            pltpu.VMEM((3 * chans, 3 * chans), BF),
+            pltpu.VMEM((3 * wide, 3 * wide), BF),
         ],
         compiler_params=pltpu.CompilerParams(vmem_limit_bytes=36 * 1024 * 1024),
         name="join",
-    )(scal, other, own, w_bev, w_join, w_out)
+    )(scal, moves, other, own, w_bev, w_join, w_out)
 
 
 def shards(col_feat, w_depth, w_ctx, col_table, w_bev, offsets, w_join, w_out):
@@ -277,12 +291,7 @@
     feats = jnp.broadcast_to(col_feat, (chips * 2, alone, depth_k))
     feats = lax.all_to_all(feats, ("chip", "far"), split_axis=0, concat_axis=0, tiled=True)
     pair_table = lax.ppermute(col_table, "far", [(0, 1), (1, 0)])
-    w_ctx = jnp.pad(w_ctx, ((0, 0), (0, cols - chans)))
-    feats, pair_table, w_ctx, w_bev, w_out = lax.optimization_barrier(
-        (feats, pair_table, w_ctx, taps(w_bev), taps(w_out))
-    )
-
-    head = jnp.stack(
+    scal = jnp.stack(
         [
             lax.axis_index(("x", "far", "near")).astype(jnp.int32),
             lax.axis_index("chip").astype(jnp.int32) - (share - 1),
@@ -290,16 +299,15 @@
             lax.axis_index("far").astype(jnp.int32),
         ]
     )
-    moves = jnp.concatenate([jnp.zeros((1, 2), jnp.int32), offsets[0]], axis=0)
-    scal = jnp.concatenate([head, moves.reshape(-1)])
-
-    messages = call_pack(shape, scal, feats, w_depth, w_ctx, col_table, pair_table)
+    moves = offsets[0].T
+
+    messages = call_pack(shape, scal, feats, w_depth, w_ctx.T, col_table, pair_table)
     got = lax.all_to_all(messages, ("x", "near"), split_axis=0, concat_axis=0, tiled=True)
     other = lax.ppermute(got, "core", [(0, 1), (1, 0)])
 
     w_join = jnp.transpose(w_join, (0, 1, 3, 2)).reshape(3, 3 * wide, frames * chans)
-    own = call_own(shape, scal, got, w_bev)
-    joined = call_join(shape, scal, other, own, w_bev, w_join, w_out)
+    own = call_own(shape, scal, moves, got, w_bev)
+    joined = call_join(shape, scal, moves, other, own, w_bev, w_join, w_out)
     return joined[None]
 
 

time: 70.3 us -> 75.3 us (1.071)
  waiting for transfers between devices: 3.96 us -> 9.51 us
    ppermute x1, waiting for transfers between devices: 0.01 us -> 4.03 us  [shards(): pair_table = lax.ppermute(col_table, 'far', [(0, 1), (1, 0)])]
    unnamed x8 -> x18, local copies, waits for them, and re-layouts: 1.66 us -> 5.23 us
    transpose x2 -> x0, local copies, waits for them, and re-layouts: 3 us -> none  [taps(): turned = jnp.transpose(weight, (1, 3, 0, 2))]
    all_to_all x1, waiting for transfers between devices: 3.95 us -> 5.47 us  [shards(): lax.all_to_all(feats, ('chip', 'far'), split_axis=0, concat_axis=0, tiled...]
    reshape x3 -> x0, local copies, waits for them, and re-layouts: 0.8 us -> none  [the longest x2 0.72 us: taps(): turned.reshape(weight.shape[1] * weight.shape[3], weight.shape[0] * weigh...]
  transfers between devices with their start and end apart: 3 -> 3, of which waited for: 1 -> 2; matrix products, arithmetic and copies ran while one was open for 8% -> 0% of each run, Pallas kernels for 8% -> 8%
where the time goes in v8:
time: 75.3 us; the launch traced here: 74.9 us
  starting transfers between devices  26.6 us (35%)
  Pallas kernels  19.8 us (26%)
  blocking collectives  12 us (16%)
  waiting for transfers between devices  9.51 us (13%)
  local copies, waits for them, and re-layouts  6.71 us (9%)
    all_to_all x1, starting transfers between devices, shards(): lax.all_to_all(feats, ('chip', 'far'), split_axis=0, concat_axis=0, tiled...  16.5 us
    pallas_call x1, Pallas kernels, call_join(): pl.pallas_call(functools.partial(join_kernel, shape), out_shape=jax.Shape...  13 us
    all_to_all x1, blocking collectives, shards(): lax.all_to_all(messages, ('x', 'near'), split_axis=0, concat_axis=0, tile...  12 us
    ppermute x1, starting transfers between devices, shards(): other = lax.ppermute(got, 'core', [(0, 1), (1, 0)])  6.09 us
    pallas_call x1, Pallas kernels, call_own(): pl.pallas_call(functools.partial(own_kernel, shape), out_shape=jax.ShapeD...  5.75 us
    all_to_all x1, waiting for transfers between devices, shards(): lax.all_to_all(feats, ('chip', 'far'), split_axis=0, concat_axis=0, tiled...  5.47 us
    unnamed x18, local copies, waits for them, and re-layouts  5.23 us
    ppermute x1, starting transfers between devices, shards(): pair_table = lax.ppermute(col_table, 'far', [(0, 1), (1, 0)])  4.04 us
  transfers between devices with their start and end apart: 3, of which 2 were waited for; matrix products, arithmetic and copies ran while one was open for 0% of the time, Pallas kernels for 8%

profile of v8, /device:TPU:1, one launch (start us, length us, event | category | flops | bytes accessed | tf_op | source)
XLA Modules:
  0.0 74.9 jit_solution(4142967701128651954)
XLA Ops:
  0.0 0.0 copy-start.8
  0.0 0.0 copy-start.1
  0.0 1.5 %broadcast_in_dim.11 = bf16[32,16,256]{2,1,0:T(8,128)(2,1)} broadcast(bf16[16,256]{1,0:T(8,128)(2,1)} %bitcast.17), dimensions={1,2} | broadcast | bytes 270336 | tf_op jit(solution)/shard_map/broadcast_in_dim | solution.py:291
  1.5 16.5 %all-to-all-start = ((bf16[32,16,256]{2,1,0:T(8,128)(2,1)}), bf16[32,16,256]{2,1,0:T(8,128)(2,1)S(1)}, u32[]{:S(2)}, u32[]{:S(2)}) async-start(bf16[32,16,256]{2,1,0:T(8,128)(2,1)} %broadcast_in_dim.11), calls=%async_computation | async-start | bytes 524288 | tf_op jit(solution)/shard_map/all_to_all | solution.py:292
  18.0 4.0 %collective-permute-start = (s32[8,128]{1,0:T(8,128)}, s32[8,128]{1,0:T(8,128)S(1)}, u32[]{:S(2)}, u32[]{:S(2)}) collective-permute-start(s32[8,128]{1,0:T(8,128)} %table.1), channel_id=1, source_target_pairs={{0,2},{2,0},{1,3},{3,1},{4,6},{6,4},{5,7},{7,5},{8,10},{10,8},{9,1... | collective-permute-start | bytes 12296 | tf_op jit(solution)/shard_map/ppermute | solution.py:293
  22.1 0.1 pad_add_fusion.scal
  22.2 4.0 %collective-permute-done.pair_table = s32[8,128]{1,0:T(8,128)S(1)} collective-permute-done((s32[8,128]{1,0:T(8,128)}, s32[8,128]{1,0:T(8,128)S(1)}, u32[]{:S(2)}, u32[]{:S(2)}) %collective-permute-start) | collective-permute-done | bytes 4128 | tf_op jit(solution)/shard_map/ppermute | solution.py:293
  26.2 5.5 %all-to-all-done.feats = bf16[32,16,256]{2,1,0:T(8,128)(2,1)S(1)} async-done(((bf16[32,16,256]{2,1,0:T(8,128)(2,1)}), bf16[32,16,256]{2,1,0:T(8,128)(2,1)S(1)}, u32[]{:S(2)}, u32[]{:S(2)}) %all-to-all-start) | async-done | bytes 262176 | tf_op jit(solution)/shard_map/all_to_all | solution.py:292
  31.7 0.0 copy-start
  31.7 0.0 copy-start.4
  31.7 1.0 %copy-done.4 = bf16[256,128]{1,0:T(8,128)(2,1)S(1)} copy-done((bf16[256,128]{1,0:T(8,128)(2,1)S(1)}, bf16[256,128]{1,0:T(8,128)(2,1)}, u32[]{:S(2)}) %copy-start.4) | copy-done | bytes 65560
  32.7 0.0 copy-start.5
  32.7 1.0 %copy-done.5 = bf16[256,80]{0,1:T(8,128)(2,1)S(1)} copy-done((bf16[256,80]{0,1:T(8,128)(2,1)S(1)}, bf16[256,80]{0,1:T(8,128)(2,1)}, u32[]{:S(2)}) %copy-start.5) | copy-done | bytes 40984
  33.7 0.0 copy-start.6
  33.7 0.7 copy-done.6
  34.4 1.1 %pack.1 = bf16[8,304,128]{2,1,0:T(8,128)(2,1)S(1)} custom-call(s32[4]{0:T(128)S(1)} %pad_add_fusion.scal, bf16[32,16,256]{2,1,0:T(8,128)(2,1)S(1)} %all-to-all-done.feats, bf16[256,128]{1,0:T(8,128)(2,1)S(1)} %copy-done.4, bf16[80,256]{1,0:T(8,128)(2,1)S(1)} %bitcast.14, s32[8,128]{1,0:T(8,128)S(1)} %copy-done.6, s32[8,128]{1,0:T(8,128)S(1)} %collective-permute-done.pair_table), custom_call_target="tpu_custom_call" | custom-call | tf_op jit(solution)/shard_map/pack/pallas_call | solution.py:234
  35.5 12.0 %all_to_all.10.got = bf16[8,304,128]{2,1,0:T(8,128)(2,1)S(1)} all-to-all(bf16[8,304,128]{2,1,0:T(8,128)(2,1)S(1)} %pack.1), channel_id=1, replica_groups=mesh['chip'=16,'core'=2,'x'=4,'far'=2,'near'=2] {'x','near'}, dimensions={0} | all-to-all | bytes 1245184 | tf_op jit(solution)/shard_map/all_to_all | solution.py:305
  47.5 6.1 %collective-permute-start.1 = (bf16[8,304,128]{2,1,0:T(8,128)(2,1)S(1)}, bf16[8,304,128]{2,1,0:T(8,128)(2,1)S(1)}, u32[]{:S(2)}, u32[]{:S(2)}) collective-permute-start(bf16[8,304,128]{2,1,0:T(8,128)(2,1)S(1)} %all_to_all.10.got), channel_id=1, source_target_pairs={{0,16},{16,0},{1,17},{17,1},{2,18},{18,2},{3,19},{19,3},{4,20},{20... | collective-permute-start | bytes 1867784 | tf_op jit(solution)/shard_map/ppermute | solution.py:306
  53.6 0.0 copy-start.2
  53.6 0.9 %copy-done.2 = bf16[3,3,80,80]{3,2,1,0:T(8,128)(2,1)S(1)} copy-done((bf16[3,3,80,80]{3,2,1,0:T(8,128)(2,1)S(1)}, bf16[3,3,80,80]{3,2,1,0:T(8,128)(2,1)}, u32[]{:S(2)}) %copy-start.2) | copy-done | bytes 115224
  54.5 0.0 copy-start.7
  54.5 0.7 copy-done.7
  55.2 5.7 %own.1 = bf16[12,720,128]{2,1,0:T(8,128)(2,1)S(1)} custom-call(s32[4]{0:T(128)S(1)} %pad_add_fusion.scal, s32[2,16]{1,0:T(2,128)S(1)} %bitcast.15, bf16[8,304,128]{2,1,0:T(8,128)(2,1)S(1)} %all_to_all.10.got, bf16[3,3,80,80]{3,2,1,0:T(8,128)(2,1)S(1)} %copy-done.2), custom_call_target="tpu_custom_call" | custom-call | tf_op jit(solution)/shard_map/own/pallas_call | solution.py:247
  60.9 0.0 collective-permute-done.1.other
  61.0 0.0 copy-done.8
  61.0 0.0 copy-done.1
  61.0 0.0 copy-done
  61.0 0.0 copy-start.3
  61.0 0.9 %copy-done.3 = bf16[3,3,80,80]{3,2,1,0:T(8,128)(2,1)S(1)} copy-done((bf16[3,3,80,80]{3,2,1,0:T(8,128)(2,1)S(1)}, bf16[3,3,80,80]{3,2,1,0:T(8,128)(2,1)}, u32[]{:S(2)}) %copy-start.3) | copy-done | bytes 115224
  61.9 13.0 %join.1 = bf16[8,160,128]{2,1,0:T(8,128)(2,1)} custom-call(s32[4]{0:T(128)S(1)} %pad_add_fusion.scal, s32[2,16]{1,0:T(2,128)S(1)} %bitcast.16, bf16[8,304,128]{2,1,0:T(8,128)(2,1)S(1)} %collective-permute-done.1.other, bf16[12,720,128]{2,1,0:T(8,128)(2,1)S(1)} %own.1, bf16[3,3,80,80]{3,2,1,0:T(8,128)(2,1)S(1)} %copy-done.3, ...), custom_call_target="tpu_custom_call" | custom-call | tf_op jit(solution)/shard_map/join/pallas_call | solution.py:261
Async XLA Ops:
  0.0 61.0 %copy-start.8 = (s32[1,16,2]{1,2,0:T(2,128)S(1)}, s32[1,16,2]{1,2,0:T(2,128)}, u32[]{:S(2)}) copy-start(s32[1,16,2]{1,2,0:T(2,128)} %param.13) | copy-start | bytes 388
  0.0 61.0 %copy-start.1 = (bf16[3,3,160,160]{3,2,1,0:T(8,128)(2,1)S(1)}, bf16[3,3,160,160]{3,2,1,0:T(8,128)(2,1)}, u32[]{:S(2)}) copy-start(bf16[3,3,160,160]{3,2,1,0:T(8,128)(2,1)} %weight_out.1) | copy-start | bytes 1382404
  1.5 30.2 %all-to-all-start = ((bf16[32,16,256]{2,1,0:T(8,128)(2,1)}), bf16[32,16,256]{2,1,0:T(8,128)(2,1)S(1)}, u32[]{:S(2)}, u32[]{:S(2)}) async-start(bf16[32,16,256]{2,1,0:T(8,128)(2,1)} %broadcast_in_dim.11), calls=%async_computation | async-start | bytes 524288 | tf_op jit(solution)/shard_map/all_to_all | solution.py:292
  18.0 8.2 %collective-permute-start = (s32[8,128]{1,0:T(8,128)}, s32[8,128]{1,0:T(8,128)S(1)}, u32[]{:S(2)}, u32[]{:S(2)}) collective-permute-start(s32[8,128]{1,0:T(8,128)} %table.1), channel_id=1, source_target_pairs={{0,2},{2,0},{1,3},{3,1},{4,6},{6,4},{5,7},{7,5},{8,10},{10,8},{9,1... | collective-permute-start | bytes 12296 | tf_op jit(solution)/shard_map/ppermute | solution.py:293
  31.7 29.3 %copy-start = (bf16[3,3,1360,160]{2,3,1,0:T(8,128)(2,1)S(1)}, bf16[3,3,1360,160]{2,3,1,0:T(8,128)(2,1)}, u32[]{:S(2)}) copy-start(bf16[3,3,1360,160]{2,3,1,0:T(8,128)(2,1)} %param.14) | copy-start | bytes 11750404
  31.7 1.0 %copy-start.4 = (bf16[256,128]{1,0:T(8,128)(2,1)S(1)}, bf16[256,128]{1,0:T(8,128)(2,1)}, u32[]{:S(2)}) copy-start(bf16[256,128]{1,0:T(8,128)(2,1)} %w_depth.1) | copy-start | bytes 196612
  32.7 1.0 %copy-start.5 = (bf16[256,80]{0,1:T(8,128)(2,1)S(1)}, bf16[256,80]{0,1:T(8,128)(2,1)}, u32[]{:S(2)}) copy-start(bf16[256,80]{0,1:T(8,128)(2,1)} %param.10) | copy-start | bytes 122884
  33.7 0.7 copy-start.6
  47.5 13.5 %collective-permute-start.1 = (bf16[8,304,128]{2,1,0:T(8,128)(2,1)S(1)}, bf16[8,304,128]{2,1,0:T(8,128)(2,1)S(1)}, u32[]{:S(2)}, u32[]{:S(2)}) collective-permute-start(bf16[8,304,128]{2,1,0:T(8,128)(2,1)S(1)} %all_to_all.10.got), channel_id=1, source_target_pairs={{0,16},{16,0},{1,17},{17,1},{2,18},{18,2},{3,19},{19,3},{4,20},{20... | collective-permute-start | bytes 1867784 | tf_op jit(solution)/shard_map/ppermute | solution.py:306
  53.6 0.9 %copy-start.2 = (bf16[3,3,80,80]{3,2,1,0:T(8,128)(2,1)S(1)}, bf16[3,3,80,80]{3,2,1,0:T(8,128)(2,1)}, u32[]{:S(2)}) copy-start(bf16[3,3,80,80]{3,2,1,0:T(8,128)(2,1)} %weight.3) | copy-start | bytes 345604
  54.5 0.7 copy-start.7
  61.0 0.9 %copy-start.3 = (bf16[3,3,80,80]{3,2,1,0:T(8,128)(2,1)S(1)}, bf16[3,3,80,80]{3,2,1,0:T(8,128)(2,1)}, u32[]{:S(2)}) copy-start(bf16[3,3,80,80]{3,2,1,0:T(8,128)(2,1)} %weight.3) | copy-start | bytes 345604
